TPU v7x, 32 devices: a whole 2x2x4 slice. The times are simulated.
32 devices in a mesh: dp: 8 (over z, x), tensor: 4 (over y, core).
Axes of the slice: x: 2, y: 2, z: 4, core: 2. Of those that a mesh axis runs over, the one named last changes fastest.
Arguments:
- tokens: bfloat16 [32768, 768], P('dp'), may hold values from -6 to 6
- lengths: int32 [64], P('dp'), may hold values from 40 to 512
- cotangent: bfloat16 [16384, 768], P('dp'), may hold values from -6 to 6
- query_weight: float32 [768, 768], P('dp', 'tensor'), may hold values from -0.21875 to 0.21875
- key_weight: float32 [768, 768], P('dp', 'tensor'), may hold values from -0.21875 to 0.21875
- value_weight: float32 [768, 768], P('dp', 'tensor'), may hold values from -0.21875 to 0.21875
- value_bias: float32 [768], P('tensor'), may hold values from -0.6 to 0.6
- output_weight: float32 [768, 768], P('tensor', 'dp'), may hold values from -1.75 to 1.75
- b_out: float32 [768], replicated, may hold values from -1.5 to 1.5
- rel_table: float32 [12, 1024], P('tensor'), may hold values from -4 to 4
- norm_gain: float32 [768], replicated, may hold values from 0.1 to 1.9
- norm_shift: float32 [768], replicated, may hold values from -1.5 to 1.5
- up_weight: float32 [768, 3072], P('dp', 'tensor'), may hold values from -0.21875 to 0.21875
- hidden_bias: float32 [3072], P('tensor'), may hold values from -1.5 to 1.5
- down_weight: float32 [3072, 768], P('tensor', 'dp'), may hold values from -0.109375 to 0.109375
- b_down: float32 [768], replicated, may hold values from -1.5 to 1.5
- final_gain: float32 [768], replicated, may hold values from 0.1 to 1.9
- final_shift: float32 [768], replicated, may hold values from -1.5 to 1.5
Outputs:
- output: bfloat16 [16384, 768], P('dp')
- tokens_grad: bfloat16 [32768, 768], P('dp')
- query_grad: float32 [768, 768], P('dp', 'tensor')
- key_grad: float32 [768, 768], P('dp', 'tensor')
- value_grad: float32 [768, 768], P('dp', 'tensor')
- vbias_grad: float32 [768], P('tensor')
- outw_grad: float32 [768, 768], P('tensor', 'dp')
- obias_grad: float32 [768], replicated
- table_grad: float32 [12, 1024], P('tensor')
- ngain_grad: float32 [768], replicated
- nshift_grad: float32 [768], replicated
- upw_grad: float32 [768, 3072], P('dp', 'tensor')
- ubias_grad: float32 [3072], P('tensor')
- downw_grad: float32 [3072, 768], P('tensor', 'dp')
- dbias_grad: float32 [768], replicated
- fgain_grad: float32 [768], replicated
- fshift_grad: float32 [768], replicated
All inputs are finite; a program needn't handle non-finite values.
Results may differ from a plain program's by a relative error of at most 0.02.
Values may be sent and summed in bfloat16 or wider, within the bound.
A program may use at most 256 MiB of HBM per device.

v0:
```python
import jax
import jax.numpy as jnp
from jax import lax
from jax.sharding import PartitionSpec as P

epsilon = 1e-06


def shifted_table(pos_table, length):
    half_len = length // 2
    head_rows = pos_table.shape[0]
    row_step = 2 * length - 2
    repeated = jnp.tile(pos_table, (1, half_len))
    window = repeated[:, length : length + half_len * row_step]
    return window.reshape(head_rows, half_len, row_step)[:, :, :length]


def smooth_gate(values):
    return jax.nn.gelu(values, approximate=False)


def norm_forward(values, gain_vec, shift_vec):
    row_mean = jnp.mean(values, axis=-1, keepdims=True)
    centred = values - row_mean
    row_var = jnp.mean(centred * centred, axis=-1, keepdims=True)
    inv_std = lax.rsqrt(row_var + epsilon)
    unit_rows = centred * inv_std
    return (unit_rows * gain_vec + shift_vec, (unit_rows, inv_std))


def norm_backward(upstream, saved_stats, gain_vec):
    unit_rows, inv_std = saved_stats
    gain_grad = jnp.sum(upstream * unit_rows, axis=(0, 1))
    shift_grad = jnp.sum(upstream, axis=(0, 1))
    scaled = upstream * gain_vec
    input_grad = inv_std * (
        scaled
        - jnp.mean(scaled, axis=-1, keepdims=True)
        - unit_rows * jnp.mean(scaled * unit_rows, axis=-1, keepdims=True)
    )
    return (input_grad, gain_grad, shift_grad)


def shards(
    tokens,
    lengths,
    cotangent,
    query_weight,
    key_weight,
    value_weight,
    value_bias,
    output_weight,
    b_out,
    rel_table,
    norm_gain,
    norm_shift,
    up_weight,
    hidden_bias,
    down_weight,
    b_down,
    final_gain,
    final_shift,
):
    seq_count = lengths.shape[0]
    length = tokens.shape[0] // seq_count
    half_len = length // 2
    model_width = tokens.shape[1]
    head_count = rel_table.shape[0]
    head_dim = query_weight.shape[1] // head_count
    score_scale = head_dim ** (-0.5)
    masters = (
        query_weight.astype(jnp.bfloat16),
        key_weight.astype(jnp.bfloat16),
        value_weight.astype(jnp.bfloat16),
        output_weight.astype(jnp.bfloat16),
        up_weight.astype(jnp.bfloat16),
        down_weight.astype(jnp.bfloat16),
    )
    (
        query_weight_gathered,
        key_weight_gathered,
        value_weight_gathered,
        output_weight_gathered,
        up_weight_gathered,
        down_weight_gathered,
    ) = (
        lax.all_gather(masters[0], "dp", axis=0, tiled=True),
        lax.all_gather(masters[1], "dp", axis=0, tiled=True),
        lax.all_gather(masters[2], "dp", axis=0, tiled=True),
        lax.all_gather(masters[3], "dp", axis=1, tiled=True),
        lax.all_gather(masters[4], "dp", axis=0, tiled=True),
        lax.all_gather(masters[5], "dp", axis=1, tiled=True),
    )
    sequence_tokens = tokens.reshape(seq_count, length, model_width)
    key_valid = lax.broadcasted_iota(jnp.int32, (seq_count, length), 1) < lengths[:, None]
    query_valid = (
        2 * lax.broadcasted_iota(jnp.int32, (seq_count, half_len), 1) < lengths[:, None]
    ).astype(jnp.float32)
    pooled = jnp.mean(
        sequence_tokens.astype(jnp.float32).reshape(seq_count, half_len, 2, model_width), axis=2
    )
    pooled_reduced = pooled.astype(jnp.bfloat16)
    query_rows = (
        jnp.einsum(
            "sku,uz->skz", pooled_reduced, query_weight_gathered, preferred_element_type=jnp.float32
        )
        * score_scale
    ).astype(jnp.bfloat16)
    key_rows_reduced = jnp.einsum(
        "yil,lj->yij", sequence_tokens, key_weight_gathered, preferred_element_type=jnp.float32
    ).astype(jnp.bfloat16)
    value_rows_reduced = (
        jnp.einsum(
            "yil,lj->yij",
            sequence_tokens,
            value_weight_gathered,
            preferred_element_type=jnp.float32,
        )
        + value_bias
    ).astype(jnp.bfloat16)
    query_heads = query_rows.reshape(seq_count, half_len, head_count, head_dim)
    key_heads = key_rows_reduced.reshape(seq_count, length, head_count, head_dim)
    value_heads = value_rows_reduced.reshape(seq_count, length, head_count, head_dim)
    rel_bias, bias_pull = jax.vjp(lambda pos_table: shifted_table(pos_table, length), rel_table)

    def scores_of():
        raw_scores = (
            jnp.einsum(
                "bqhe,bkhe->bhqk", query_heads, key_heads, preferred_element_type=jnp.float32
            )
            + rel_bias[None]
        )
        return jnp.where(key_valid[:, None, None, :], raw_scores, -1e30)

    scores = scores_of()
    row_max = jnp.max(scores, axis=-1, keepdims=True)
    exponent = jnp.exp(scores - row_max)
    row_total = jnp.sum(exponent, axis=-1, keepdims=True)
    attn_probs = exponent / row_total
    log_total = row_max + jnp.log(row_total)
    context_rows = (
        jnp.einsum(
            "bhqk,bkhe->bqhe",
            attn_probs.astype(jnp.bfloat16),
            value_heads,
            preferred_element_type=jnp.float32,
        )
        .reshape(seq_count, half_len, head_count * head_dim)
        .astype(jnp.bfloat16)
    )
    attn_part = jnp.einsum(
        "atx,xo->ato", context_rows, output_weight_gathered, preferred_element_type=jnp.float32
    ).astype(jnp.bfloat16)
    attention_mixed = lax.psum(attn_part, "tensor").astype(jnp.float32)
    hidden_in = pooled + attention_mixed + b_out
    normed, first_stats = norm_forward(hidden_in, norm_gain, norm_shift)
    normalized_reduced = normed.astype(jnp.bfloat16)
    preactivation = (
        jnp.einsum(
            "pjg,gy->pjy",
            normalized_reduced,
            up_weight_gathered,
            preferred_element_type=jnp.float32,
        )
        + hidden_bias
    )
    activation_output, gate_pull = jax.vjp(smooth_gate, preactivation)
    activation_reduced = activation_output.astype(jnp.bfloat16)
    ffn_part = jnp.einsum(
        "jtu,ul->jtl", activation_reduced, down_weight_gathered, preferred_element_type=jnp.float32
    ).astype(jnp.bfloat16)
    feedforward_result = lax.psum(ffn_part, "tensor").astype(jnp.float32)
    summed = normed + feedforward_result + b_down
    result, second_stats = norm_forward(summed, final_gain, final_shift)
    output = (
        (result * query_valid[..., None])
        .astype(jnp.bfloat16)
        .reshape(seq_count * half_len, model_width)
    )
    grad_result = (
        cotangent.reshape(seq_count, half_len, model_width).astype(jnp.float32)
        * query_valid[..., None]
    )
    grad_summed, final_gain_grad, final_shift_grad = norm_backward(
        grad_result, second_stats, final_gain
    )
    feedforward_gradient_reduced = grad_summed.astype(jnp.bfloat16)
    down_bias_grad = jnp.sum(grad_summed, axis=(0, 1))
    down_weight_gradient = jnp.einsum(
        "lkn,lka->na",
        activation_reduced,
        feedforward_gradient_reduced,
        preferred_element_type=jnp.float32,
    )
    act_grad = jnp.einsum(
        "xin,hn->xih",
        feedforward_gradient_reduced,
        down_weight_gathered,
        preferred_element_type=jnp.float32,
    )
    preactivation_gradient = gate_pull(act_grad)[0].astype(jnp.bfloat16)
    up_bias_grad = jnp.sum(preactivation_gradient.astype(jnp.float32), axis=(0, 1))
    up_weight_gradient = jnp.einsum(
        "hsx,hsy->xy",
        normalized_reduced,
        preactivation_gradient,
        preferred_element_type=jnp.float32,
    )
    normed_part = jnp.einsum(
        "znt,it->zni",
        preactivation_gradient,
        up_weight_gathered,
        preferred_element_type=jnp.float32,
    ).astype(jnp.bfloat16)
    normed_grad = grad_summed + lax.psum(normed_part, "tensor").astype(jnp.float32)
    hidden_grad, norm_gain_grad, norm_shift_grad = norm_backward(
        normed_grad, first_stats, norm_gain
    )
    attention_gradient_reduced = hidden_grad.astype(jnp.bfloat16)
    out_bias_grad = jnp.sum(hidden_grad, axis=(0, 1))
    output_gradient = jnp.einsum(
        "sjc,sjr->cr", context_rows, attention_gradient_reduced, preferred_element_type=jnp.float32
    )
    context_grad = (
        jnp.einsum(
            "mlw,kw->mlk",
            attention_gradient_reduced,
            output_weight_gathered,
            preferred_element_type=jnp.float32,
        )
        .astype(jnp.bfloat16)
        .reshape(seq_count, half_len, head_count, head_dim)
    )
    probs_again = jnp.exp(scores_of() - log_total)
    prob_grad = jnp.einsum(
        "bqhe,bkhe->bhqk", context_grad, value_heads, preferred_element_type=jnp.float32
    )
    row_dot = jnp.sum(probs_again * prob_grad, axis=-1, keepdims=True)
    score_grad = (probs_again * (prob_grad - row_dot)).astype(jnp.bfloat16)
    table_grad = bias_pull(jnp.sum(score_grad.astype(jnp.float32), axis=0))[0]
    value_cotangent = (
        jnp.einsum(
            "bhqk,bqhe->bkhe",
            probs_again.astype(jnp.bfloat16),
            context_grad,
            preferred_element_type=jnp.float32,
        )
        .astype(jnp.bfloat16)
        .reshape(seq_count, length, head_count * head_dim)
    )
    query_cotangent = (
        jnp.einsum("bhqk,bkhe->bqhe", score_grad, key_heads, preferred_element_type=jnp.float32)
        .astype(jnp.bfloat16)
        .reshape(seq_count, half_len, head_count * head_dim)
    )
    key_cotangent = (
        jnp.einsum("bhqk,bqhe->bkhe", score_grad, query_heads, preferred_element_type=jnp.float32)
        .astype(jnp.bfloat16)
        .reshape(seq_count, length, head_count * head_dim)
    )
    query_w_grad = (
        jnp.einsum(
            "frp,frs->ps", pooled_reduced, query_cotangent, preferred_element_type=jnp.float32
        )
        * score_scale
    )
    key_weight_gradient = jnp.einsum(
        "glm,glu->mu", sequence_tokens, key_cotangent, preferred_element_type=jnp.float32
    )
    value_w_grad = jnp.einsum(
        "glm,glu->mu", sequence_tokens, value_cotangent, preferred_element_type=jnp.float32
    )
    value_bias_grad = jnp.sum(value_cotangent.astype(jnp.float32), axis=(0, 1))
    pooled_part = (
        jnp.einsum(
            "sho,no->shn",
            query_cotangent,
            query_weight_gathered,
            preferred_element_type=jnp.float32,
        )
        * score_scale
    )
    token_part = jnp.einsum(
        "pmh,ih->pmi", key_cotangent, key_weight_gathered, preferred_element_type=jnp.float32
    ) + jnp.einsum(
        "pmh,ih->pmi", value_cotangent, value_weight_gathered, preferred_element_type=jnp.float32
    )
    token_part = (
        (token_part.reshape(seq_count, half_len, 2, model_width) + 0.5 * pooled_part[:, :, None, :])
        .reshape(seq_count, length, model_width)
        .astype(jnp.bfloat16)
    )
    token_sum = lax.psum(token_part, "tensor").astype(jnp.float32)
    tokens_grad = (
        (token_sum.reshape(seq_count, half_len, 2, model_width) + 0.5 * hidden_grad[:, :, None, :])
        .reshape(seq_count * length, model_width)
        .astype(jnp.bfloat16)
    )
    query_sum, key_sum, value_sum, outw_sum, up_sum, down_sum = (
        lax.psum_scatter(query_w_grad, "dp", scatter_dimension=0, tiled=True),
        lax.psum_scatter(key_weight_gradient, "dp", scatter_dimension=0, tiled=True),
        lax.psum_scatter(value_w_grad, "dp", scatter_dimension=0, tiled=True),
        lax.psum_scatter(output_gradient, "dp", scatter_dimension=1, tiled=True),
        lax.psum_scatter(up_weight_gradient, "dp", scatter_dimension=0, tiled=True),
        lax.psum_scatter(down_weight_gradient, "dp", scatter_dimension=1, tiled=True),
    )
    (
        vbias_sum,
        obias_sum,
        table_sum,
        ngain_sum,
        nshift_sum,
        ubias_sum,
        dbias_sum,
        fgain_sum,
        fshift_sum,
    ) = lax.psum(
        (
            value_bias_grad,
            out_bias_grad,
            table_grad,
            norm_gain_grad,
            norm_shift_grad,
            up_bias_grad,
            down_bias_grad,
            final_gain_grad,
            final_shift_grad,
        ),
        "dp",
    )
    return (
        output,
        tokens_grad,
        query_sum,
        key_sum,
        value_sum,
        vbias_sum,
        outw_sum,
        obias_sum,
        table_sum,
        ngain_sum,
        nshift_sum,
        up_sum,
        ubias_sum,
        down_sum,
        dbias_sum,
        fgain_sum,
        fshift_sum,
    )


def solution(mesh):
    in_specs = (
        P("dp", None),
        P("dp"),
        P("dp", None),
        P("dp", "tensor"),
        P("dp", "tensor"),
        P("dp", "tensor"),
        P("tensor"),
        P("tensor", "dp"),
        P(),
        P("tensor", None),
        P(),
        P(),
        P("dp", "tensor"),
        P("tensor"),
        P("tensor", "dp"),
        P(),
        P(),
        P(),
    )
    out_specs = (
        P("dp", None),
        P("dp", None),
        P("dp", "tensor"),
        P("dp", "tensor"),
        P("dp", "tensor"),
        P("tensor"),
        P("tensor", "dp"),
        P(),
        P("tensor", None),
        P(),
        P(),
        P("dp", "tensor"),
        P("tensor"),
        P("tensor", "dp"),
        P(),
        P(),
        P(),
    )
    return jax.shard_map(shards, mesh=mesh, in_specs=in_specs, out_specs=out_specs, check_vma=False)
```

profile of v0, /device:TPU:0, one launch (start us, length us, event | category | flops | bytes accessed | tf_op | source)
XLA Modules:
  0.0 961.2 jit_solution(14077429777384731691)
XLA Ops:
  13.1 34.9 %all_gather.21 = bf16[192,768]{0,1:T(8,128)(2,1)} all-gather(bf16[192,96]{0,1:T(8,128)(2,1)S(1)} %copy.60), channel_id=1, replica_groups=mesh['dp'=8,'tensor'=4] {'dp'}, dimensions={1}, use_global_device_ids=true | all-gather | bytes 331776 | tf_op jit(solution)/shard_map/all_gather | solution.py:90
  48.0 33.0 %all_gather.18 = bf16[768,192]{1,0:T(8,128)(2,1)} all-gather(bf16[96,192]{1,0:T(8,128)(2,1)S(1)} %convert_element_type.151), channel_id=1, replica_groups=mesh['dp'=8,'tensor'=4] {'dp'}, dimensions={0}, use_global_device_ids=true | all-gather | bytes 331776 | tf_op jit(solution)/shard_map/all_gather | solution.py:89
  81.0 33.1 %all_gather.20 = bf16[768,192]{1,0:T(8,128)(2,1)} all-gather(bf16[96,192]{1,0:T(8,128)(2,1)S(1)} %convert_element_type.156), channel_id=1, replica_groups=mesh['dp'=8,'tensor'=4] {'dp'}, dimensions={0}, use_global_device_ids=true | all-gather | bytes 331776 | tf_op jit(solution)/shard_map/all_gather | solution.py:88
  114.1 31.0 %all_gather.19 = bf16[768,192]{1,0:T(8,128)(2,1)S(1)} all-gather(bf16[96,192]{1,0:T(8,128)(2,1)S(1)} %convert_element_type.154), channel_id=1, replica_groups=mesh['dp'=8,'tensor'=4] {'dp'}, dimensions={0}, use_global_device_ids=true | all-gather | bytes 331776 | tf_op jit(solution)/shard_map/all_gather | solution.py:87
  150.1 5.9 reshape.217
  156.0 14.7 %reshape.227 = f32[8,256,2,768]{3,2,1,0:T(2,128)} reshape(bf16[4096,768]{1,0:T(8,128)(2,1)} %param.18) | data formatting | bytes 18874368 | tf_op jit(solution)/shard_map/convert_element_type | solution.py:100
  170.8 5.1 convolution_convert_fusion.4
  175.8 5.6 add_convert_fusion.3
  181.4 19.9 %reduce_sum.191 = f32[8,256,768]{2,1,0:T(8,128)} reduce(f32[8,256,2,768]{3,2,1,0:T(2,128)} %reshape.227, f32[]{:T(128)} %constant.38.clone.1), dimensions={2}, to_apply=%region_0.0 | reduce | flops 1572864 | bytes 18874372 | tf_op jit(solution)/shard_map/reduce_sum | solution.py:99
  201.3 4.1 multiply_convert_fusion.4
  212.8 4.3 fusion.27
  222.3 68.3 %all-reduce.8.cloned.1.call-done = bf16[8,256,768]{2,1,0:T(8,128)(2,1)} async-done(((bf16[8,256,768]{2,1,0:T(8,128)(2,1)}), bf16[8,256,768]{2,1,0:T(8,128)(2,1)}) %all-reduce.8.cloned.1.call-update) | async-done | bytes 3145744 | tf_op jit(solution)/shard_map/psum | solution.py:154
  290.6 5.0 fusion.54
  299.3 7.5 fusion.23
  309.3 15.5 %multiply_convert_fusion.2 = (bf16[8,256,768]{2,1,0:T(8,128)(2,1)}, f32[8,256,768]{2,1,0:T(8,128)}) fusion(f32[8,256,768]{2,1,0:T(8,128)S(1)} %get-tuple-element.102, f32[768]{0:T(1024)S(1)} %copy-done.42, u8[256,768]{1,0:T(8,128)(4,1)S(1)} %get-tuple-element.75, u8[256,768]{1,0:T(8,128)(4,1)S(1)} %get-tuple-element.74), kind=kLoop, calls=%fused_computation.33 | loop fusion | flops 111673344 | bytes 16124928 | tf_op jit(solution)/shard_map/convert_element_type | solution.py:168
  324.9 6.7 convolution_convert_fusion.2
  339.4 60.8 %all-reduce.10.cloned.1.call-done = bf16[8,256,768]{2,1,0:T(8,128)(2,1)} async-done(((bf16[8,256,768]{2,1,0:T(8,128)(2,1)}), bf16[8,256,768]{2,1,0:T(8,128)(2,1)}) %all-reduce.10.cloned.1.call-update) | async-done | bytes 3145744 | tf_op jit(solution)/shard_map/psum | solution.py:172
  400.2 4.9 fusion.52
  406.1 3.5 multiply_reduce_fusion.1
  409.6 4.0 subtract_multiply_fusion.1
  413.6 8.7 convert_reduce_fusion.1
  422.3 6.2 convolution_convert_fusion.1
  428.7 68.6 %all-reduce.12.cloned.1.call-done = bf16[8,256,768]{2,1,0:T(8,128)(2,1)} async-done(((bf16[8,256,768]{2,1,0:T(8,128)(2,1)}), bf16[8,256,768]{2,1,0:T(8,128)(2,1)}) %all-reduce.12.cloned.1.call-update) | async-done | bytes 3145744 | tf_op jit(solution)/shard_map/psum | solution.py:215
  497.3 8.2 multiply_reduce_fusion.2
  505.5 6.8 fusion.51
  517.2 4.0 fusion.24
  521.2 7.6 convert_reduce_fusion.2
  528.8 9.4 multiply_reduce_fusion
  538.3 8.0 convert_reduce_fusion
  550.6 6.9 add.181
  557.6 15.8 %add.182 = f32[8,512,768]{2,1,0:T(8,128)} reshape(f32[8,256,2,768]{3,2,1,0:T(2,128)} %add.181) | data formatting | bytes 25165824 | tf_op jit(solution)/shard_map/add | solution.py:289
  573.4 6.4 fusion.39
  579.8 12.1 %add_convert_fusion.1 = bf16[8,512,768]{2,1,0:T(8,128)(2,1)} fusion(f32[8,512,768]{2,1,0:T(8,128)} %add.182, f32[8,512,768]{2,1,0:T(8,128)} %fusion.39, bf16[8,512,192]{1,2,0:T(8,128)(2,1)S(1)} %bitcast.143, bf16[768,192]{1,0:T(8,128)(2,1)S(1)} %copy-done.21), kind=kOutput, calls=%fused_computation.2 | convolution fusion | flops 1217396736 | bytes 33325056 | tf_op jit(solution)/shard_map/pmh,ih->pmi/dot_general | solution.py:285
  592.0 4.7 convolution_bitcast_fusion.3
  597.9 5.1 fusion.28
  603.1 4.2 convolution_bitcast_fusion.4
  608.6 8.0 convolution_bitcast_fusion
  616.8 8.5 convolution_bitcast_fusion.1
  628.8 6.5 add.184
  635.3 15.9 %add.185 = f32[4096,768]{1,0:T(8,128)} reshape(f32[8,256,2,768]{3,2,1,0:T(2,128)} %add.184) | data formatting | bytes 25165824 | tf_op jit(solution)/shard_map/add | solution.py:295
  653.1 5.8 reshape.225
  664.0 38.4 %all-reduce.2 = (f32[192]{0:T(256)}, f32[768]{0:T(1024)}, f32[3,1024]{1,0:T(4,128)}, f32[768]{0:T(1024)}, f32[768]{0:T(1024)}, /*index=5*/f32[768]{0:T(1024)}, f32[768]{0:T(1024)}, f32[768]{0:T(1024)}, f32[768]{0:T(1024)}) all-reduce(f32[192]{0:T(256)S(1)} %reduce_sum.203, ...), channel_id=1, replica_groups=mesh['dp'=8,'tensor'=4] {'dp'}, use_global_device_ids=true, to_apply=%region_20.21 | all-reduce | flops 8640 | bytes 69120 | tf_op jit(solution)/shard_map/psum | solution.py:317
  704.0 7.9 all-reduce.14.cloned.1.call-done
  711.9 10.5 %add_convert_fusion = bf16[4096,768]{1,0:T(8,128)(2,1)} fusion(f32[4096,768]{1,0:T(8,128)} %add.185, bf16[4096,768]{1,0:T(8,128)(2,1)} %all-reduce.14.cloned.1.call-done), kind=kLoop, calls=%fused_computation.1 | loop fusion | flops 9437184 | bytes 25165824 | tf_op jit(solution)/shard_map/convert_element_type | solution.py:297
  722.4 21.3 %reduce-scatter.13.cloned.1.call-done = f32[96,192]{1,0:T(8,128)} async-done(((f32[768,192]{1,0:T(8,128)}), f32[96,192]{1,0:T(8,128)}) %reduce-scatter.13.cloned.1.call-update) | async-done | bytes 73744 | tf_op jit(solution)/shard_map/reduce_scatter | solution.py:300
  743.7 65.9 %reduce-scatter.19.cloned.1.call-done = f32[96,192]{1,0:T(8,128)} async-done(((f32[768,192]{1,0:T(8,128)}), f32[96,192]{1,0:T(8,128)}) %reduce-scatter.19.cloned.1.call-update) | async-done | bytes 73744
  809.6 72.0 %reduce-scatter.17.cloned.1.call-done = f32[768,96]{0,1:T(8,128)} async-done(((f32[768,768]{0,1:T(8,128)}), f32[768,96]{0,1:T(8,128)}) %reduce-scatter.17.cloned.1.call-update) | async-done | bytes 294928 | tf_op jit(solution)/shard_map/reduce_scatter | solution.py:305
  881.6 72.2 %reduce-scatter.15.cloned.1.call-done = f32[96,768]{1,0:T(8,128)} async-done(((f32[768,768]{1,0:T(8,128)}), f32[96,768]{1,0:T(8,128)}) %reduce-scatter.15.cloned.1.call-update) | async-done | bytes 294928 | tf_op jit(solution)/shard_map/reduce_scatter | solution.py:304
  (194 shorter events, 61.7 us)
Async XLA Ops:
  8.0 137.0 %copy-start = (f32[3,1024]{1,0:T(4,128)S(1)}, f32[3,1024]{1,0:T(4,128)}, u32[]{:S(2)}) copy-start(f32[3,1024]{1,0:T(4,128)} %param.27) | copy-start | bytes 36868
  8.0 282.6 %all-reduce.8.cloned.1.call-start = ((), (), s32[]{:S(2)}) async-start(), calls=%async_computation.6 | async-start | bytes 6291456 | tf_op jit(solution)/shard_map/psum | solution.py:154
  156.0 14.7 %copy-start.12 = (f32[3,256,1022]{2,1,0:T(8,128)}, f32[3,256,1022]{2,1,0:T(8,128)S(1)}, u32[]{:S(2)}) copy-start(f32[3,256,1022]{2,1,0:T(8,128)S(1)} %reshape.217) | copy-start | bytes 9418756
  170.7 5.1 copy-start.20
  170.7 5.1 copy-start.51
  175.8 29.6 %copy-start.7 = (bf16[8,512,192]{1,2,0:T(8,128)(2,1)}, bf16[8,512,192]{1,2,0:T(8,128)(2,1)S(1)}, u32[]{:S(2)}) copy-start(bf16[8,512,192]{1,2,0:T(8,128)(2,1)S(1)} %convolution_convert_fusion.4) | copy-start | bytes 4718596
  181.4 29.7 %copy-start.22 = (bf16[8,512,192]{1,2,0:T(8,128)(2,1)}, bf16[8,512,192]{1,2,0:T(8,128)(2,1)S(1)}, u32[]{:S(2)}) copy-start(bf16[8,512,192]{1,2,0:T(8,128)(2,1)S(1)} %add_convert_fusion.3) | copy-start | bytes 4718596
  211.1 6.1 copy-start.28
  212.8 5.2 copy-start.15
  217.2 73.5 %copy-start.48 = (f32[768]{0:T(1024)S(1)}, f32[768]{0:T(1024)}, u32[]{:S(2)}) copy-start(f32[768]{0:T(1024)} %param.26) | copy-start | bytes 9220
  220.8 78.5 %all-gather.3.cloned.1.call-start = ((), (), s32[]{:S(2)}) async-start(), calls=%async_computation.7 | async-start | bytes 1327104 | tf_op jit(solution)/shard_map/all_gather | solution.py:91
  221.5 103.3 %all-gather.5.cloned.1.call-start = ((), (), s32[]{:S(2)}) async-start(), calls=%async_computation.8 | async-start | bytes 1327104 | tf_op jit(solution)/shard_map/all_gather | solution.py:92
  222.3 177.9 %all-reduce.10.cloned.1.call-start = ((), (), s32[]{:S(2)}) async-start(), calls=%async_computation.9 | async-start | bytes 6291456 | tf_op jit(solution)/shard_map/psum | solution.py:172
  324.9 8.1 copy-start.6
  331.6 165.7 %all-reduce.12.cloned.1.call-start = ((), (), s32[]{:S(2)}) async-start(), calls=%async_computation.10 | async-start | bytes 6291456 | tf_op jit(solution)/shard_map/psum | solution.py:215
  406.0 7.5 slice-start.4
  406.0 7.5 slice-start.6
  413.6 8.7 copy-start.5
  413.6 8.7 copy-start.50
  422.3 6.3 copy-start.25
  422.3 6.3 copy-start.29
  422.3 75.0 %copy-start.32 = (f32[768]{0:T(1024)S(1)}, f32[768]{0:T(1024)}, u32[]{:S(2)}) copy-start(f32[768]{0:T(1024)} %param.28) | copy-start | bytes 9220
  428.6 273.8 %reduce-scatter.23.cloned.1.call-start = ((), (), s32[]{:S(2)}) async-start(), calls=%async_computation.17 | async-start | bytes 884736
  497.3 8.2 copy-start.9
  505.5 9.5 copy-start.19
  521.2 7.6 copy-start.23
  521.2 17.0 %slice-start = ((s8[12582912]{0:T(1024)(128)(4,1)}), s8[4194304]{0:T(1024)(128)(4,1)S(1)}, s32[]{:S(2)}) async-start(s8[12582912]{0:T(1024)(128)(4,1)} %bitcast.122), calls=%async_computation.18 | async-start | bytes 8388608
  521.2 17.0 %slice-start.1 = ((s8[12582912]{0:T(1024)(128)(4,1)}), s8[4194304]{0:T(1024)(128)(4,1)S(1)}, s32[]{:S(2)}) async-start(s8[12582912]{0:T(1024)(128)(4,1)} %bitcast.122), calls=%async_computation.19 | async-start | bytes 8388608
  528.8 9.5 slice-start.2
  538.3 8.0 copy-start.8
  549.5 162.4 %all-reduce.14.cloned.1.call-start = ((), (), s32[]{:S(2)}) async-start(), calls=%async_computation.11 | async-start | bytes 12582912 | tf_op jit(solution)/shard_map/psum | solution.py:293
  557.6 15.8 %copy-start.17 = (bf16[768,192]{1,0:T(8,128)(2,1)S(1)}, bf16[768,192]{1,0:T(8,128)(2,1)}, u32[]{:S(2)}) copy-start(bf16[768,192]{1,0:T(8,128)(2,1)} %all_gather.20) | copy-start | bytes 884740
  573.4 6.4 copy-start.13
  573.4 6.4 copy-start.21
  591.9 130.5 %reduce-scatter.21.cloned.1.call-start = ((), (), s32[]{:S(2)}) async-start(), calls=%async_computation.16 | async-start | bytes 884736
  597.9 145.9 %reduce-scatter.13.cloned.1.call-start = ((), (), s32[]{:S(2)}) async-start(), calls=%async_computation.12 | async-start | bytes 884736 | tf_op jit(solution)/shard_map/reduce_scatter | solution.py:300
  603.1 206.5 %reduce-scatter.19.cloned.1.call-start = ((), (), s32[]{:S(2)}) async-start(), calls=%async_computation.15 | async-start | bytes 884736
  608.5 8.3 copy-start.45
  608.5 273.1 %reduce-scatter.17.cloned.1.call-start = ((), (), s32[]{:S(2)}) async-start(), calls=%async_computation.14 | async-start | bytes 2654208 | tf_op jit(solution)/shard_map/reduce_scatter | solution.py:305
  616.6 337.3 %reduce-scatter.15.cloned.1.call-start = ((), (), s32[]{:S(2)}) async-start(), calls=%async_computation.13 | async-start | bytes 2654208 | tf_op jit(solution)/shard_map/reduce_scatter | solution.py:304
  658.8 5.1 copy-start.35
  658.8 5.1 copy-start.36
  658.8 5.1 copy-start.37
  658.8 5.1 copy-start.38
  658.8 5.1 copy-start.39
  658.9 5.1 copy-start.40
  658.9 5.1 copy-start.46
  711.9 242.0 %copy-start.1 = (f32[3,1024]{1,0:T(4,128)S(1)}, f32[3,1024]{1,0:T(4,128)}, u32[]{:S(2)}) copy-start(f32[3,1024]{1,0:T(4,128)} %param.27) | copy-start | bytes 36868
  (24 other events, 76.3 us)
Sparse Core Ops, SparseCore 0:
  220.9 69.7 all-reduce.7
  331.7 68.4 all-reduce.9
  428.7 68.5 all-reduce.11
  592.1 119.7 all-reduce.13
Sparse Core Ops, SparseCore 1:
  224.0 42.6 all-gather.2
  269.3 39.9 all-gather.4
  549.6 62.6 reduce-scatter.22
  616.6 61.7 reduce-scatter.20
  682.2 61.5 reduce-scatter.12
  748.0 61.5 reduce-scatter.18
  813.5 68.0 reduce-scatter.16
  885.6 68.2 reduce-scatter.14
where the time goes:
time: 966 us; the launch traced here: 961 us
  waiting for transfers between devices  437 us (45%)
  blocking collectives  170 us (18%)
  matrix products  130 us (13%)
  other arithmetic  107 us (11%)
  local copies, waits for them, and re-layouts  100 us (10%)
  between operations  16.3 us (2%)
    reduce_scatter x1, waiting for transfers between devices, shards(): lax.psum_scatter(up_weight_gradient, 'dp', scatter_dimension=0, tiled=True)  72.2 us
    reduce_scatter x1, waiting for transfers between devices, shards(): lax.psum_scatter(down_weight_gradient, 'dp', scatter_dimension=1, tiled=T...  72 us
    psum x1, waiting for transfers between devices, shards(): lax.psum(normed_part, 'tensor').astype(jnp.float32)  68.6 us
    psum x1, waiting for transfers between devices, shards(): attention_mixed = lax.psum(attn_part, 'tensor').astype(jnp.float32)  68.3 us
    unnamed x15, waiting for transfers between devices  66.1 us
    psum x1, waiting for transfers between devices, shards(): feedforward_result = lax.psum(ffn_part, 'tensor').astype(jnp.float32)  60.8 us
    psum x1, blocking collectives, shards(): lax.psum((value_bias_grad, out_bias_grad, table_grad, norm_gain_grad, nor...  38.4 us
    all_gather x1, blocking collectives, shards(): lax.all_gather(masters[3], 'dp', axis=1, tiled=True)  34.9 us
  transfers between devices with their start and end apart: 12, of which 8 were waited for; matrix products, arithmetic and copies ran while one was open for 17% of the time, Pallas kernels for 0%

commit v1 on v0

v1 whole, which is shorter than its diff:
```python
import functools

import jax
import jax.numpy as jnp
from jax import lax
from jax.experimental import pallas as pl
from jax.experimental.pallas import tpu as pltpu
from jax.sharding import PartitionSpec as P

MESH = pl.DeviceIdType.MESH
F32 = jnp.float32
BF16 = jnp.bfloat16
EPS = 1e-06
VMEM_LIMIT = 58 * 2**20


def dot_nn(a, b):
    return lax.dot_general(a, b, (((1,), (0,)), ((), ())), preferred_element_type=F32)


def dot_nt(a, b):
    return lax.dot_general(a, b, (((1,), (1,)), ((), ())), preferred_element_type=F32)


def dot_tn(a, b):
    return lax.dot_general(a, b, (((0,), (0,)), ((), ())), preferred_element_type=F32)


def gather_kernel(
    n_hi, a_in, u_in, d_in, s_in, a_out, u_out, d_out, s_out, loc, zs, zr, ls, lr, fs, fr, cs, cr, ss, sr
):
    dp, t = lax.axis_index("dp"), lax.axis_index("tensor")
    hi, lo = dp // 2, lax.rem(dp, 2)
    core = lax.rem(t, 2)
    t_core = t + 1 - 2 * core
    t_y = lax.rem(t + 2, 4)
    t_d = lax.rem(t_core + 2, 4)
    dp_x = dp + 1 - 2 * lo

    def z_peer(s):
        return lax.rem(hi + s, n_hi) * 2 + lo

    def block(s, side):
        return lax.rem(hi - s + n_hi, n_hi) * 2 + side

    barrier = pltpu.get_barrier_semaphore()

    def greet(s, carry):
        pl.semaphore_signal(barrier, inc=1, device_id=(z_peer(s), t), device_id_type=MESH)
        return carry

    lax.fori_loop(1, n_hi, greet, 0)
    for peer in ((dp_x, t), (dp, t_y), (dp, t_core), (dp, t_d)):
        pl.semaphore_signal(barrier, inc=1, device_id=peer, device_id_type=MESH)
    pl.semaphore_wait(barrier, n_hi + 3)

    def remote(src, dst, send, recv, peer):
        return pltpu.make_async_remote_copy(
            src, dst, send, recv, device_id=peer, device_id_type=MESH
        )

    ins, outs = (a_in, u_in, d_in), (a_out, u_out, d_out)

    def small(i, peer):
        return remote(s_in, s_out.at[t], ss.at[i], sr.at[i], peer)

    small_peers = ((dp, t_core), (dp, t_y), (dp, t_d))
    small_local = pltpu.make_async_copy(s_in, s_out.at[t], loc.at[3])
    small_local.start()
    for i, peer in enumerate(small_peers):
        small(i, peer).start()

    def local(k):
        return pltpu.make_async_copy(ins[k], outs[k].at[t, dp], loc.at[k])

    def z_copy(k, s):
        return remote(ins[k], outs[k].at[t, dp], zs.at[k, s], zr.at[k, s], (z_peer(s), t))

    def line(k, s, way, src):
        b = block(s, lo)
        peer = (dp_x, t) if way == 0 else (dp, t_y)
        return remote(src, outs[k].at[t, b], ls.at[way, k, s], lr.at[way, k, s], peer)

    def fwd_x(k, s):
        where = outs[k].at[t_y, block(s, lo)]
        return remote(where, where, fs.at[k, s], fr.at[k, s], (dp_x, t))

    def fwd_y(k, s):
        where = outs[k].at[t, block(s, 1 - lo)]
        return remote(where, where, fs.at[k, s], fr.at[k, s], (dp, t_y))

    def to_core(k, s, which, src=None):
        tt = t if which < 2 else t_y
        side = lo if which % 2 == 0 else 1 - lo
        where = outs[k].at[tt, block(s, side)]
        return remote(
            where if src is None else src,
            where,
            cs.at[which, k, s],
            cr.at[which, k, s],
            (dp, t_core),
        )

    def start_z(k):
        local(k).start()

        def body(s, carry):
            z_copy(k, s).start()
            return carry

        lax.fori_loop(1, n_hi, body, 0)

    def first(k):
        line(k, 0, 0, ins[k]).start()
        line(k, 0, 1, ins[k]).start()
        to_core(k, 0, 0, ins[k]).start()

    def spread(k):
        def body(s, carry):
            z_copy(k, s).wait_recv()
            src = outs[k].at[t, block(s, lo)]
            line(k, s, 0, src).start()
            line(k, s, 1, src).start()
            to_core(k, s, 0).start()
            return carry

        lax.fori_loop(1, n_hi, body, 0)

    def forward(k):
        def body(s, carry):
            @pl.when(core == 0)
            def _():
                line(k, s, 0, ins[k]).wait_recv()
                fwd_y(k, s).start()
                to_core(k, s, 1).start()
                line(k, s, 1, ins[k]).wait_recv()
                to_core(k, s, 2).start()

            @pl.when(core == 1)
            def _():
                line(k, s, 1, ins[k]).wait_recv()
                fwd_x(k, s).start()
                to_core(k, s, 2).start()
                line(k, s, 0, ins[k]).wait_recv()
                to_core(k, s, 1).start()

            return carry

        lax.fori_loop(0, n_hi, body, 0)

    def last(k):
        def body(s, carry):
            fwd_y(k, s).wait_recv()
            to_core(k, s, 3).start()
            return carry

        lax.fori_loop(0, n_hi, body, 0)

    def finish(k):
        local(k).wait()

        def body(s, carry):
            line(k, s, 0, ins[k]).wait_send()
            line(k, s, 1, ins[k]).wait_send()
            fwd_y(k, s).wait_send()
            for which in range(4):
                to_core(k, s, which).wait_send()
                to_core(k, s, which).wait_recv()
            return carry

        lax.fori_loop(0, n_hi, body, 0)

        def zbody(s, carry):
            z_copy(k, s).wait_send()
            return carry

        lax.fori_loop(1, n_hi, zbody, 0)

    start_z(0)
    first(0)
    spread(0)
    start_z(1)
    first(1)
    forward(0)
    spread(1)
    start_z(2)
    first(2)
    last(0)
    forward(1)
    spread(2)
    last(1)
    forward(2)
    last(2)
    for k in range(3):
        finish(k)
    small_local.wait()
    for i, peer in enumerate(small_peers):
        small(i, peer).wait()


def gather_weights(a, u, d, small, n_dp):
    n_hi = n_dp // 2
    rows, width = a.shape
    whole = jax.ShapeDtypeStruct((4, n_dp, rows, width), BF16)
    dma = pltpu.SemaphoreType.DMA
    any_spec = pl.BlockSpec(memory_space=pl.ANY)
    a4, u4, d4, s4 = pl.pallas_call(
        functools.partial(gather_kernel, n_hi),
        out_shape=(whole, whole, whole, jax.ShapeDtypeStruct((4,) + small.shape, F32)),
        in_specs=[any_spec] * 4,
        out_specs=(any_spec,) * 4,
        scratch_shapes=[
            dma((4,)),
            dma((3, n_hi)),
            dma((3, n_hi)),
            dma((2, 3, n_hi)),
            dma((2, 3, n_hi)),
            dma((3, n_hi)),
            dma((3, n_hi)),
            dma((4, 3, n_hi)),
            dma((4, 3, n_hi)),
            dma((3,)),
            dma((3,)),
        ],
        compiler_params=pltpu.CompilerParams(collective_id=0, has_side_effects=True),
    )(a, u, d, small)
    flat = (4, n_dp * rows, width)
    return a4.reshape(flat), u4.reshape(flat), d4.reshape(flat), s4


def pool_matrix(pooled, length):
    i = lax.broadcasted_iota(jnp.int32, (pooled, length), 0)
    j = lax.broadcasted_iota(jnp.int32, (pooled, length), 1)
    return jnp.where(j // 2 == i, 0.5, 0.0).astype(BF16)


def lane_low(shape):
    return lax.broadcasted_iota(jnp.int32, shape, 1) < 64


def attention_kernel(
    n_seq, length, scal, x_ref, a_ref, s_ref, bo_ref, kv_ref, q_ref, p_ref, ctx_ref, hid_ref, pb_ref, bias
):
    half = length // 2
    step = pl.program_id(0)

    @pl.when(step == 0)
    def _():
        pool = pool_matrix(half, length)
        for b in range(n_seq):
            pooled = dot_nn(pool, x_ref[b * length : (b + 1) * length, :])
            hid_ref[b * half : (b + 1) * half, :] = pooled + bo_ref[...]
            pb_ref[b * half : (b + 1) * half, :] = pooled.astype(BF16)

    small = s_ref[0]
    for b in range(n_seq):
        rows = slice(b * length, (b + 1) * length)
        kv_ref[0, rows, :] = (dot_nn(x_ref[rows, :], a_ref[0, :, 0:384]) + small[3:4, 0:384]).astype(BF16)
        rows = slice(b * half, (b + 1) * half)
        q = dot_nn(pb_ref[rows, :], a_ref[0, :, 384:640]) * 0.125
        lanes = lax.broadcasted_iota(jnp.int32, q.shape, 1)
        q_ref[0, rows, :] = jnp.where(lanes < 192, q, 0.0).astype(BF16)
    for h in range(3):
        wide = jnp.broadcast_to(small[h : h + 1, :], (half, 2 * length))
        rolled = pltpu.roll(wide, length, 1, stride=2, stride_axis=0)
        bias[h] = rolled[:, :length].T
    low = lane_low((half, 128))
    keys = lax.broadcasted_iota(jnp.int32, (length, half), 0)

    def one_seq(b, carry):
        krows = pl.ds(pl.multiple_of(b * length, length), length)
        qrows = pl.ds(pl.multiple_of(b * half, half), half)
        valid = keys < scal[2 + b]
        q01 = q_ref[0, qrows, 0:128]
        zero = jnp.zeros_like(q01)
        heads = (
            (jnp.where(low, q01, zero), 0, 128),
            (jnp.where(low, zero, q01), 0, 128),
            (q_ref[0, qrows, 128:256], 256, 256),
        )
        contexts = []
        for h, (q, k_at, v_at) in enumerate(heads):
            s = dot_nt(kv_ref[0, krows, k_at : k_at + 128], q) + bias[h]
            s = jnp.where(valid, s, -1e30)
            e = jnp.exp(s - jnp.max(s, axis=0, keepdims=True))
            p = (e * (1.0 / jnp.sum(e, axis=0, keepdims=True))).astype(BF16)
            p_ref[0, b, h] = p
            contexts.append(dot_tn(kv_ref[0, krows, v_at : v_at + 128], p))
        c0, c1, c2 = contexts
        ctx01 = jnp.concatenate([c0[0:64], c1[64:128]], axis=0).T
        ctx2 = jnp.concatenate([jnp.zeros_like(c2[0:64]), c2[64:128]], axis=0).T
        ctx = jnp.concatenate([ctx2, ctx01], axis=1).astype(BF16)
        ctx_ref[0, qrows, :] = ctx
        hid_ref[qrows, :] += dot_nt(ctx, a_ref[0, :, 512:768])
        return carry

    lax.fori_loop(0, n_seq, one_seq, 0)


def attention_forward(scal, tokens, a4, s4, b_out, n_seq, length):
    half = length // 2
    width = tokens.shape[1]
    return pl.pallas_call(
        functools.partial(attention_kernel, n_seq, length),
        out_shape=(
            jax.ShapeDtypeStruct((4, n_seq * length, 384), BF16),
            jax.ShapeDtypeStruct((4, n_seq * half, 256), BF16),
            jax.ShapeDtypeStruct((4, n_seq, 3, length, half), BF16),
            jax.ShapeDtypeStruct((4, n_seq * half, 256), BF16),
            jax.ShapeDtypeStruct((n_seq * half, width), F32),
            jax.ShapeDtypeStruct((n_seq * half, width), BF16),
        ),
        grid_spec=pltpu.PrefetchScalarGridSpec(
            num_scalar_prefetch=1,
            grid=(4,),
            in_specs=[
                pl.BlockSpec((n_seq * length, width), lambda g, s: (s[0], 0)),
                pl.BlockSpec((1, width, 768), lambda g, s: (g, 0, 0)),
                pl.BlockSpec((1, 8, 1024), lambda g, s: (g, 0, 0)),
                pl.BlockSpec((1, width), lambda g, s: (0, 0)),
            ],
            out_specs=[
                pl.BlockSpec((1, n_seq * length, 384), lambda g, s: (g, 0, 0)),
                pl.BlockSpec((1, n_seq * half, 256), lambda g, s: (g, 0, 0)),
                pl.BlockSpec((1, n_seq, 3, length, half), lambda g, s: (g, 0, 0, 0, 0)),
                pl.BlockSpec((1, n_seq * half, 256), lambda g, s: (g, 0, 0)),
                pl.BlockSpec((n_seq * half, width), lambda g, s: (0, 0)),
                pl.BlockSpec((n_seq * half, width), lambda g, s: (0, 0)),
            ],
            scratch_shapes=[pltpu.VMEM((3, length, half), F32)],
        ),
        compiler_params=pltpu.CompilerParams(vmem_limit_bytes=VMEM_LIMIT),
        cost_estimate=pl.CostEstimate(flops=20 * 10**9, bytes_accessed=40 * 10**6, transcendentals=6 * 10**6),
    )(scal, tokens, a4, s4, b_out)


def row_mean(v):
    return jnp.mean(v, axis=-1, keepdims=True)


def ffn_kernel(
    n_seq, half, scal, hid_ref, cot_ref, u_ref, d_ref, s_ref, vec_ref,
    out_ref, ag_ref, gu_ref, gd_ref, gv_ref, nb_all, fg_all, act_all, pg_all, dg,
):
    b = pl.program_id(0)
    rows = pl.ds(pl.multiple_of(b * half, half), half)
    n_gain, n_shift, b_down, f_gain, f_shift = (vec_ref[i : i + 1, :] for i in range(5))

    @pl.when(b == 0)
    def _():
        gv_ref[...] = jnp.zeros_like(gv_ref)

    def add(i, v):
        gv_ref[i : i + 1, :] += jnp.sum(v, axis=0, keepdims=True)

    hid = hid_ref[...]
    centred = hid - row_mean(hid)
    inv1 = lax.rsqrt(row_mean(centred * centred) + EPS)
    unit1 = centred * inv1
    normed = unit1 * n_gain + n_shift
    nb = normed.astype(BF16)
    nb_all[rows, :] = nb
    summed = normed + b_down
    for t in range(4):
        pre = dot_nn(nb, u_ref[t]) + s_ref[t, 4:5, 0:768]
        cdf = 0.5 * (1.0 + lax.erf(pre * 0.7071067811865476))
        act = (pre * cdf).astype(BF16)
        dg[t] = cdf + pre * (0.3989422804014327 * jnp.exp(-0.5 * pre * pre))
        act_all[t, rows, :] = act
        summed = summed + dot_nt(act, d_ref[t])
    centred = summed - row_mean(summed)
    inv2 = lax.rsqrt(row_mean(centred * centred) + EPS)
    unit2 = centred * inv2
    valid = (2 * lax.broadcasted_iota(jnp.int32, (half, 1), 0) < scal[2 + b]).astype(F32)
    out_ref[...] = ((unit2 * f_gain + f_shift) * valid).astype(BF16)
    grad = cot_ref[...].astype(F32) * valid
    add(0, grad * unit2)
    add(1, grad)
    scaled = grad * f_gain
    grad_summed = inv2 * (scaled - row_mean(scaled) - unit2 * row_mean(scaled * unit2))
    add(2, grad_summed)
    fg = grad_summed.astype(BF16)
    fg_all[rows, :] = fg
    normed_grad = grad_summed
    for t in range(4):
        pg = (dot_nn(fg, d_ref[t]) * dg[t]).astype(BF16)
        pg_all[t, rows, :] = pg
        normed_grad = normed_grad + dot_nt(pg, u_ref[t])
    add(3, normed_grad * unit1)
    add(4, normed_grad)
    scaled = normed_grad * n_gain
    hidden_grad = inv1 * (scaled - row_mean(scaled) - unit1 * row_mean(scaled * unit1))
    add(5, hidden_grad)
    ag_ref[...] = hidden_grad.astype(BF16)

    @pl.when(b == n_seq - 1)
    def _():
        for i in range(2):
            t = 2 * scal[1] + i
            pg = pg_all[t]
            gu_ref[i] = dot_tn(nb_all[...], pg).astype(BF16)
            gd_ref[i] = dot_tn(fg_all[...], act_all[t]).astype(BF16)
            gv_ref[6 + i : 7 + i, :] = jnp.sum(pg.astype(F32), axis=0, keepdims=True)


def ffn(scal, hid, cotangent, u4, d4, s4, vectors, n_seq, half):
    width = hid.shape[1]
    once = pl.Buffered(1)
    return pl.pallas_call(
        functools.partial(ffn_kernel, n_seq, half),
        out_shape=(
            jax.ShapeDtypeStruct((n_seq * half, width), BF16),
            jax.ShapeDtypeStruct((n_seq * half, width), BF16),
            jax.ShapeDtypeStruct((2, width, 768), BF16),
            jax.ShapeDtypeStruct((2, width, 768), BF16),
            jax.ShapeDtypeStruct((8, width), F32),
        ),
        grid_spec=pltpu.PrefetchScalarGridSpec(
            num_scalar_prefetch=1,
            grid=(n_seq,),
            in_specs=[
                pl.BlockSpec((half, width), lambda b, s: (b, 0)),
                pl.BlockSpec((half, width), lambda b, s: (s[0] * n_seq + b, 0)),
                pl.BlockSpec((4, width, 768), lambda b, s: (0, 0, 0), pipeline_mode=once),
                pl.BlockSpec((4, width, 768), lambda b, s: (0, 0, 0), pipeline_mode=once),
                pl.BlockSpec((4, 8, 1024), lambda b, s: (0, 0, 0)),
                pl.BlockSpec((8, width), lambda b, s: (0, 0)),
            ],
            out_specs=[
                pl.BlockSpec((half, width), lambda b, s: (b, 0)),
                pl.BlockSpec((half, width), lambda b, s: (b, 0)),
                pl.BlockSpec((2, width, 768), lambda b, s: (0, 0, 0)),
                pl.BlockSpec((2, width, 768), lambda b, s: (0, 0, 0)),
                pl.BlockSpec((8, width), lambda b, s: (0, 0)),
            ],
            scratch_shapes=[
                pltpu.VMEM((n_seq * half, width), BF16),
                pltpu.VMEM((n_seq * half, width), BF16),
                pltpu.VMEM((4, n_seq * half, 768), BF16),
                pltpu.VMEM((4, n_seq * half, 768), BF16),
                pltpu.VMEM((4, half, 768), F32),
            ],
        ),
        compiler_params=pltpu.CompilerParams(vmem_limit_bytes=VMEM_LIMIT),
        cost_estimate=pl.CostEstimate(flops=24 * 10**9, bytes_accessed=30 * 10**6, transcendentals=6 * 10**6),
    )(scal, hid, cotangent, u4, d4, s4, vectors)


def backward_kernel(n_seq, length, own, scal, *refs):
    half = length // 2
    x_ref, a_ref, kv_ref, q_ref, p_ref, ctx_ref, ag_ref, pb_ref = refs[:8]
    refs = refs[8:]
    if own:
        tok_ref, pool_ref, ga_ref, tg_ref, vb_ref, kvd, qd_all, tacc = refs
    else:
        tok_in, pool_in, out_ref, tok_ref, pool_ref, kvd, qd_all = refs
    step = pl.program_id(0)

    @pl.when(step == 0)
    def _():
        if own:
            tok_ref[...] = jnp.zeros_like(tok_ref)
            pool_ref[...] = jnp.zeros_like(pool_ref)
        else:
            tok_ref[...] = tok_in[...]
            pool_ref[...] = pool_in[...]

    if own:
        tacc[...] = jnp.zeros_like(tacc)
    low = lane_low((half, 128))

    def one_seq(b, carry):
        krows = pl.ds(pl.multiple_of(b * length, length), length)
        qrows = pl.ds(pl.multiple_of(b * half, half), half)
        cg = dot_nn(ag_ref[qrows, :], a_ref[0, :, 512:768]).astype(BF16)
        q01 = q_ref[0, qrows, 0:128]
        q2 = q_ref[0, qrows, 128:256]
        cg2, cg01 = cg[:, 0:128], cg[:, 128:256]
        zero = jnp.zeros_like(q01)
        cg2 = jnp.where(low, zero, cg2)
        heads = (
            (jnp.where(low, q01, zero), jnp.where(low, cg01, zero), 0, 128),
            (jnp.where(low, zero, q01), jnp.where(low, zero, cg01), 0, 128),
            (q2, cg2, 256, 256),
        )
        kds, vds, qds = [], [], []
        for h, (q, g, k_at, v_at) in enumerate(heads):
            pb16 = p_ref[0, b, h]
            p = pb16.astype(F32)
            dp = dot_nt(kv_ref[0, krows, v_at : v_at + 128], g)
            row = jnp.sum(p * dp, axis=0, keepdims=True)
            sg = (p * (dp - row)).astype(BF16)
            if own:
                tacc[h] += sg.astype(F32)
            kds.append(dot_nn(sg, q))
            vds.append(dot_nn(pb16, g))
            qds.append(dot_tn(kv_ref[0, krows, k_at : k_at + 128], sg))
        kvd[krows, 0:128] = (kds[0] + kds[1]).astype(BF16)
        kvd[krows, 128:256] = (vds[0] + vds[1]).astype(BF16)
        kvd[krows, 256:384] = (kds[2] + vds[2]).astype(BF16)
        qd01 = jnp.concatenate([qds[0][0:64], qds[1][64:128]], axis=0).T
        qd2 = jnp.concatenate([qds[2][0:64], jnp.zeros_like(qds[2][0:64])], axis=0).T
        qd = jnp.concatenate([qd01, qd2], axis=1).astype(BF16)
        qd_all[qrows, :] = qd
        tok_ref[krows, :] += dot_nt(kvd[krows, :], a_ref[0, :, 0:384])
        pool_ref[qrows, :] += dot_nt(qd, a_ref[0, :, 384:640]) * 0.125
        return carry

    lax.fori_loop(0, n_seq, one_seq, 0)
    if own:
        ga_ref[0, :, 0:384] = dot_tn(x_ref[...], kvd[...]).astype(BF16)
        gq = dot_tn(pb_ref[...], qd_all[...]) * 0.125
        go = dot_tn(ag_ref[...], ctx_ref[0])
        ga_ref[0, :, 384:512] = gq[:, 0:128].astype(BF16)
        ga_ref[0, :, 512:640] = (gq[:, 128:256] + go[:, 0:128]).astype(BF16)
        ga_ref[0, :, 640:768] = go[:, 128:256].astype(BF16)
        vb_ref[0] = jnp.broadcast_to(jnp.sum(kvd[...].astype(F32), axis=0, keepdims=True), (8, 384))
        i = lax.broadcasted_iota(jnp.int32, (half, half), 0)
        flip = jnp.where(i + lax.broadcasted_iota(jnp.int32, (half, half), 1) == half - 1, 1.0, 0.0).astype(BF16)
        for h in range(3):
            high = tacc[h].astype(BF16)
            rest = (tacc[h] - high.astype(F32)).astype(BF16)
            turned = dot_nt(flip, high) + dot_nt(flip, rest)
            wide = jnp.concatenate([turned, jnp.zeros((half, length), F32)], axis=1)
            rolled = pltpu.roll(wide, 2, 1, stride=2, stride_axis=0)
            tg_ref[0, h : h + 1, :] = jnp.sum(rolled, axis=0, keepdims=True)
        tg_ref[0, 3:8, :] = jnp.zeros((5, 2 * length), F32)
    else:

        @pl.when(step == 1)
        def _():
            pool = pool_matrix(half, length)
            for b in range(n_seq):
                rows = slice(b * half, (b + 1) * half)
                total = (pool_ref[rows, :] + ag_ref[rows, :].astype(F32)).astype(BF16)
                rows = slice(b * length, (b + 1) * length)
                out_ref[rows, :] = (tok_ref[rows, :] + dot_tn(pool, total)).astype(BF16)


def attention_backward(own, scal, tokens, a4, kv, q, p, ctx, ag, pb, partial, n_seq, length):
    half = length // 2
    width = tokens.shape[1]
    once = pl.Buffered(1)
    n_tok, n_pool = n_seq * length, n_seq * half

    def group(g, s):
        return 2 * (s[1] if own else 1 - s[1]) + g

    def fixed(shape):
        return pl.BlockSpec(shape, lambda g, s: (0,) * len(shape), pipeline_mode=once)

    in_specs = [
        pl.BlockSpec((n_tok, width), lambda g, s: (s[0], 0), pipeline_mode=once),
        pl.BlockSpec((1, width, 768), lambda g, s: (group(g, s), 0, 0)),
        pl.BlockSpec((1, n_tok, 384), lambda g, s: (group(g, s), 0, 0)),
        pl.BlockSpec((1, n_pool, 256), lambda g, s: (group(g, s), 0, 0)),
        pl.BlockSpec((1, n_seq, 3, length, half), lambda g, s: (group(g, s), 0, 0, 0, 0)),
        pl.BlockSpec((1, n_pool, 256), lambda g, s: (group(g, s), 0, 0)),
        fixed((n_pool, width)),
        fixed((n_pool, width)),
    ]
    scratch = [pltpu.VMEM((n_tok, 384), BF16), pltpu.VMEM((n_pool, 256), BF16)]
    if own:
        out_shape = (
            jax.ShapeDtypeStruct((n_tok, width), F32),
            jax.ShapeDtypeStruct((n_pool, width), F32),
            jax.ShapeDtypeStruct((2, width, 768), BF16),
            jax.ShapeDtypeStruct((2, 8, 2 * length), F32),
            jax.ShapeDtypeStruct((2, 8, 384), F32),
        )
        out_specs = [
            fixed((n_tok, width)),
            fixed((n_pool, width)),
            pl.BlockSpec((1, width, 768), lambda g, s: (g, 0, 0)),
            pl.BlockSpec((1, 8, 2 * length), lambda g, s: (g, 0, 0)),
            pl.BlockSpec((1, 8, 384), lambda g, s: (g, 0, 0)),
        ]
        scratch.append(pltpu.VMEM((3, length, half), F32))
    else:
        in_specs += [fixed((n_tok, width)), fixed((n_pool, width))]
        out_shape = jax.ShapeDtypeStruct((n_tok, width), BF16)
        out_specs = fixed((n_tok, width))
        scratch = [pltpu.VMEM((n_tok, width), F32), pltpu.VMEM((n_pool, width), F32)] + scratch
    return pl.pallas_call(
        functools.partial(backward_kernel, n_seq, length, own),
        out_shape=out_shape,
        grid_spec=pltpu.PrefetchScalarGridSpec(
            num_scalar_prefetch=1, grid=(2,), in_specs=in_specs, out_specs=out_specs, scratch_shapes=scratch
        ),
        compiler_params=pltpu.CompilerParams(vmem_limit_bytes=VMEM_LIMIT),
        cost_estimate=pl.CostEstimate(flops=20 * 10**9, bytes_accessed=30 * 10**6, transcendentals=0),
    )(scal, tokens, a4, kv, q, p, ctx, ag, pb, *partial)


def swap(v, axis, bit, size):
    return lax.ppermute(v, axis, [(i, i ^ bit) for i in range(size)])


def reduce_groups(grads, n_dp):
    dp, t = lax.axis_index("dp"), lax.axis_index("tensor")
    core, hi, lo = t % 2, dp // 2, dp % 2
    n_hi = n_dp // 2
    mine = lax.dynamic_index_in_dim(grads, core, 0, keepdims=False)
    other = lax.dynamic_index_in_dim(grads, 1 - core, 0, keepdims=False)
    got = swap(other, "tensor", 1, 4)
    k, d, width = mine.shape
    total = (mine.astype(F32) + got.astype(F32)).astype(BF16).reshape(k, n_hi, 2, d // n_dp, width)
    keep = lax.dynamic_index_in_dim(total, lo, 2, keepdims=False)
    give = lax.dynamic_index_in_dim(total, 1 - lo, 2, keepdims=False)
    got = swap(give, "dp", 1, n_dp)
    total = (keep.astype(F32) + got.astype(F32)).astype(BF16)
    final = lax.dynamic_index_in_dim(total, hi, 1, keepdims=False).astype(F32)
    for s in range(1, n_hi):
        give = lax.dynamic_index_in_dim(total, (hi + s) % n_hi, 1, keepdims=False)
        got = lax.ppermute(give, "dp", [(i, (i + 2 * s) % n_dp) for i in range(n_dp)])
        final = final + got.astype(F32)
    return final


def reduce_small(v, n_dp):
    v = v + swap(v, "tensor", 1, 4)
    return lax.psum(v, "dp")


def shards(
    n_dp, tokens, lengths, cotangent, query_weight, key_weight, value_weight, value_bias, output_weight,
    b_out, rel_table, norm_gain, norm_shift, up_weight, hidden_bias, down_weight, b_down, final_gain, final_shift,
):
    seq_count = lengths.shape[0]
    length = tokens.shape[0] // seq_count
    half = length // 2
    n_seq = seq_count // 2
    t = lax.axis_index("tensor")
    core, y = t % 2, t // 2

    out_t = output_weight.T
    packed = jnp.concatenate(
        [
            key_weight[:, :128], value_weight[:, :128], key_weight[:, 128:], value_weight[:, 128:],
            query_weight, out_t[:, 128:], out_t[:, :128],
        ],
        axis=1,
    ).astype(BF16)
    zero = jnp.zeros((128,), F32)
    small = jnp.concatenate(
        [
            rel_table,
            jnp.concatenate([zero, value_bias[:128], zero[:64], value_bias[128:], jnp.zeros((640,), F32)])[None],
            jnp.pad(hidden_bias, (0, 256))[None],
            jnp.zeros((3, 1024), F32),
        ],
        axis=0,
    )
    a4, u4, d4, s4 = gather_weights(packed, up_weight.astype(BF16), down_weight.T.astype(BF16), small, n_dp)
    scal = jnp.concatenate([jnp.stack([core, y]), lax.dynamic_slice_in_dim(lengths, core * n_seq, n_seq)]).astype(jnp.int32)

    kv, q, p, ctx, hid, pb = attention_forward(scal, tokens, a4, s4, b_out[None], n_seq, length)
    zeros = jnp.zeros_like(norm_gain)
    vectors = jnp.stack([norm_gain, norm_shift, b_down, final_gain, final_shift, zeros, zeros, zeros])
    out_half, ag, gu, gd, gv = ffn(scal, hid, cotangent, u4, d4, s4, vectors, n_seq, half)
    tok, pool, ga, tg, vb = attention_backward(True, scal, tokens, a4, kv, q, p, ctx, ag, pb, (), n_seq, length)
    tok_half = attention_backward(False, scal, tokens, a4, kv, q, p, ctx, ag, pb, (tok, pool), n_seq, length)

    ffn_sum = reduce_groups(jnp.stack([gu, gd], axis=1), n_dp)
    a_sum = reduce_groups(ga[:, None], n_dp)[0]
    up_sum, down_sum = ffn_sum[0], ffn_sum[1].T
    key_sum = jnp.concatenate([a_sum[:, 0:128], a_sum[:, 256:320]], axis=1)
    value_sum = jnp.concatenate([a_sum[:, 128:256], a_sum[:, 320:384]], axis=1)
    query_sum = a_sum[:, 384:576]
    outw_sum = jnp.concatenate([a_sum[:, 640:768], a_sum[:, 576:640]], axis=1).T

    flat = jnp.concatenate([gv.reshape(-1), tg[:, :3].reshape(-1), vb[:, 0].reshape(-1)])
    flat = reduce_small(flat, n_dp)
    cut = gv.size
    gv = flat[:cut].reshape(gv.shape)
    tg_sum = lax.dynamic_index_in_dim(flat[cut : cut + 6 * 2 * length].reshape(2, 3, 2 * length), core, 0, keepdims=False)
    vb_sum = lax.dynamic_index_in_dim(flat[cut + 6 * 2 * length :].reshape(2, 384), core, 0, keepdims=False)
    vb_sum = jnp.concatenate([vb_sum[128:256], vb_sum[320:384]])
    ub_sum = lax.dynamic_index_in_dim(gv[6:8], core, 0, keepdims=False)

    def join(part):
        got = swap(part, "tensor", 1, 4)
        return jnp.where(core == 0, jnp.concatenate([part, got]), jnp.concatenate([got, part]))

    return (
        join(out_half), join(tok_half), query_sum, key_sum, value_sum, vb_sum, outw_sum, gv[5], tg_sum,
        gv[3], gv[4], up_sum, ub_sum, down_sum, gv[2], gv[0], gv[1],
    )


def solution(mesh):
    row, col, both, rep = P("dp", None), P("tensor", "dp"), P("dp", "tensor"), P()
    ten, table = P("tensor"), P("tensor", None)
    in_specs = (
        row, P("dp"), row, both, both, both, ten, col, rep, table, rep, rep, both, ten, col, rep, rep, rep,
    )
    out_specs = (
        row, row, both, both, both, ten, col, rep, table, rep, rep, both, ten, col, rep, rep, rep,
    )
    body = functools.partial(shards, mesh.shape["dp"])
    return jax.shard_map(body, mesh=mesh, in_specs=in_specs, out_specs=out_specs, check_vma=False)
```

time: 966 us -> 353 us (0.37)
  waiting for transfers between devices: 437 us -> 16.8 us
  Pallas kernels: 0 us -> 225 us
  matrix products: 130 us -> 0 us
  blocking collectives: 170 us -> 40.4 us
  local copies, waits for them, and re-layouts: 100 us -> 25.8 us
  other arithmetic: 107 us -> 33 us
  between operations: 16.3 us -> 0.93 us
    pallas_call x0 -> x5, Pallas kernels: none -> 225 us  [the longest x1 72.1 us: gather_weights(): pl.pallas_call(functools.partial(gather_kernel, n_hi), out_shape=(whole,...]
    psum x4 -> x0, waiting for transfers between devices: 206 us -> none  [the longest x1 68.6 us: shards(): lax.psum(normed_part, 'tensor').astype(jnp.float32)]
    reduce_scatter x3 -> x0, waiting for transfers between devices: 166 us -> none  [the longest x1 72.2 us: shards(): lax.psum_scatter(up_weight_gradient, 'dp', scatter_dimension=0, tiled=True)]
    all_gather x4 -> x0, blocking collectives: 132 us -> none  [the longest x1 34.9 us: shards(): lax.all_gather(masters[3], 'dp', axis=1, tiled=True)]
    dot_general x24 -> x0, matrix products: 130 us -> none  [the longest x1 12.1 us: shards(): jnp.einsum('pmh,ih->pmi', value_cotangent, value_weight_gathered, preferr...]
    unnamed x15 -> x0, waiting for transfers between devices: 66.1 us -> none
    reduce_sum x12 -> x0, other arithmetic: 65.8 us -> none  [the longest x1 19.9 us: shards(): jnp.mean(sequence_tokens.astype(jnp.float32).reshape(seq_count, half_len,...]
    add x4 -> x0, local copies, waits for them, and re-layouts: 45.2 us -> none  [the longest x2 22.8 us: shards(): token_part.reshape(seq_count, half_len, 2, model_width)]
  transfers between devices with their start and end apart: 12 -> 13, of which waited for: 8 -> 3; matrix products, arithmetic and copies ran while one was open for 17% -> 10% of each run, Pallas kernels for 0% -> 19%
where the time goes in v1:
time: 353 us; the launch traced here: 351 us
  Pallas kernels  225 us (64%)
  blocking collectives  40.4 us (11%)
  other arithmetic  33 us (9%)
  local copies, waits for them, and re-layouts  25.8 us (7%)
  waiting for transfers between devices  16.8 us (5%)
  starting transfers between devices  9.9 us (3%)
    pallas_call x1, Pallas kernels, gather_weights(): pl.pallas_call(functools.partial(gather_kernel, n_hi), out_shape=(whole,...  72.1 us
    pallas_call x2, Pallas kernels, attention_backward(): pl.pallas_call(functools.partial(backward_kernel, n_seq, length, own), ou...  65.8 us
    pallas_call x1, Pallas kernels, attention_forward(): pl.pallas_call(functools.partial(attention_kernel, n_seq, length), out_sh...  48 us
    psum x1, blocking collectives, reduce_small(): return lax.psum(v, 'dp')  40.4 us
    pallas_call x1, Pallas kernels, ffn(): pl.pallas_call(functools.partial(ffn_kernel, n_seq, half), out_shape=(jax...  38.8 us
    ppermute x7, waiting for transfers between devices, swap(): return lax.ppermute(v, axis, [(i, i ^ bit) for i in range(size)])  12.3 us
    select_n x2, other arithmetic, join(): jnp.where(core == 0, jnp.concatenate([part, got]), jnp.concatenate([got,...  11.6 us
    ppermute x6, starting transfers between devices, reduce_groups(): lax.ppermute(give, 'dp', [(i, (i + 2 * s) % n_dp) for i in range(n_dp)])  8.59 us
  transfers between devices with their start and end apart: 13, of which 3 were waited for; matrix products, arithmetic and copies ran while one was open for 10% of the time, Pallas kernels for 19%

profile of v1, /device:TPU:0, one launch (start us, length us, event | category | flops | bytes accessed | tf_op | source)
XLA Modules:
  0.0 351.4 jit_solution(13129167624321902300)
XLA Ops:
  0.7 0.9 convert.26
  1.6 0.9 convert.27
  2.5 1.0 copy.51
  3.5 0.7 slice.148
  4.2 0.7 slice.150
  4.9 0.9 convert.28
  5.8 1.6 convert_bitcast_fusion.d_in
  7.4 1.6 convert_element_type.104.u_in
  9.1 1.3 broadcast_in_dim.24.bo_ref
  10.3 0.7 stack.38
  11.0 0.7 stack.39
  11.7 0.7 stack.40
  12.4 0.7 stack.41
  13.1 0.7 stack.42
  13.8 0.7 dynamic_slice.65
  14.5 0.7 pad.4
  15.9 1.4 maximum_maximum_fusion.s_in
  17.3 0.8 concatenate.41.a_in
  18.1 72.1 %shard_map.305 = (bf16[4,8,96,768]{3,2,1,0:T(8,128)(2,1)}, bf16[4,8,96,768]{3,2,1,0:T(8,128)(2,1)}, bf16[4,8,96,768]{3,2,1,0:T(8,128)(2,1)}, f32[4,8,1024]{2,1,0:T(8,128)}) custom-call(bf16[96,768]{1,0:T(8,128)(2,1)} %concatenate.41.a_in, bf16[96,768]{1,0:T(8,128)(2,1)} %convert_element_type.104.u_in, bf16[96,768]{1,0:T(8,128)(2,1)} %convert_bitcast_fusion.d_in, ...), custom_call_target="tpu_custom_call" | custom-call | tf_op jit(solution)/shard_map/pallas_call | solution.py:207
  90.2 48.0 %shard_map.306 = (bf16[4,2048,384]{2,1,0:T(8,128)(2,1)}, bf16[4,1024,256]{2,1,0:T(8,128)(2,1)}, bf16[4,4,3,512,256]{4,3,2,1,0:T(8,128)(2,1)}, bf16[4,1024,256]{2...) custom-call(s32[6]{0:T(128)} %pad_add_fusion.scal, bf16[4096,768]{1,0:T(8,128)(2,1)} %refs_0_.3, ...), custom_call_target="tpu_custom_call" | custom-call | flops 20000000000 | bytes 40000000 | tf_op jit(solution)/shard_map/pallas_call | solution.py:303
  138.9 38.8 %shard_map.307 = (bf16[1024,768]{1,0:T(8,128)(2,1)}, bf16[1024,768]{1,0:T(8,128)(2,1)}, bf16[2,768,768]{2,1,0:T(8,128)(2,1)}, bf16[2,768,768]{2,1,0:T(8,128)(2,1)}, f32[8,768]{1,0:T(8,128)}) custom-call(s32[6]{0:T(128)} %pad_add_fusion.scal, f32[1024,768]{1,0:T(8,128)} %get-tuple-element.39.hid_ref, bf16[2048,768]{1,0:T(8,128)(2,1)} %cot_ref.1, ...), custom_call_target="tpu_custom_call" | custom-call | flops 24000000000 | bytes 30000000 | tf_op jit(solution)/shard_map/pallas_call | solution.py:409
  177.8 3.3 fusion.2
  181.2 34.8 %shard_map.308 = (f32[2048,768]{1,0:T(8,128)}, f32[1024,768]{1,0:T(8,128)}, bf16[2,768,768]{2,1,0:T(8,128)(2,1)}, f32[2,8,1024]{2,1,0:T(8,128)}, f32[2,8,384]{2,1,0:T(8,128)}) custom-call(s32[6]{0:T(128)} %pad_add_fusion.scal, bf16[4096,768]{1,0:T(8,128)(2,1)} %refs_0_.3, bf16[4,768,768]{2,1,0:T(8,128)(2,1)} %bitcast.85, ...), custom_call_target="tpu_custom_call" | custom-call | flops 20000000000 | bytes 30000000 | tf_op jit(solution)/shard_map/pallas_call | solution.py:584
  216.0 1.4 constant_dynamic-slice_fusion.3
  218.6 0.8 slice_reduce_fusion
  220.6 31.0 %shard_map.309 = bf16[2048,768]{1,0:T(8,128)(2,1)} custom-call(s32[6]{0:T(128)} %pad_add_fusion.scal, bf16[4096,768]{1,0:T(8,128)(2,1)} %refs_0_.3, bf16[4,768,768]{2,1,0:T(8,128)(2,1)} %bitcast.86, bf16[4,2048,384]{2,1,0:T(8,128)(2,1)} %get-tuple-element.43.refs_2_, bf16[4,1024,256]{2,1,0:T(8,128)(2,1)} %get-tuple-element.44.refs_3_, ...), custom_call_target="tpu_custom_call" | custom-call | flops 20000000000 | bytes 30000000 | tf_op jit(solution)/shard_map/pallas_call | solution.py:584
  252.2 1.5 add.144
  253.6 40.4 %psum.7 = f32[13056]{0:T(1024)} all-reduce(f32[13056]{0:T(1024)} %add.144), channel_id=1, replica_groups=mesh['dp'=8,'tensor'=4] {'dp'}, use_global_device_ids=true, to_apply=%region_0.1 | all-reduce | flops 13056 | bytes 104448 | tf_op jit(solution)/shard_map/psum | solution.py:622
  294.0 1.6 add_convert_fusion
  295.6 0.9 dynamic-slice_bitcast_fusion
  297.7 1.4 reshape.139
  299.7 1.3 fusion.12
  301.7 1.3 dynamic-slice_bitcast_fusion.7
  303.0 3.6 %collective-permute-done.3 = bf16[1,4,96,768]{3,2,1,0:T(8,128)(2,1)} collective-permute-done((bf16[1,4,96,768]{3,2,1,0:T(8,128)(2,1)}, bf16[1,4,96,768]{3,2,1,0:T(8,128)(2,1)}, u32[]{:S(2)}, u32[]{:S(2)}) %collective-permute-start.3) | collective-permute-done | bytes 589856 | tf_op jit(solution)/shard_map/ppermute | solution.py:596
  306.6 1.2 fusion.6
  308.0 1.1 collective-permute-start.5
  309.0 2.8 collective-permute-start.6
  311.8 2.5 fusion
  314.7 4.5 %maximum_select_fusion.1 = bf16[2048,768]{1,0:T(8,128)(2,1)} fusion(bf16[1024,768]{1,0:T(8,128)(2,1)} %collective-permute-done, bf16[1024,768]{1,0:T(8,128)(2,1)} %get-tuple-element.42, pred[]{:T(512)S(6)} %eq.16), kind=kLoop, calls=%fused_computation.7 | loop fusion | flops 14155776 | bytes 6291457 | tf_op jit(solution)/shard_map/jit(_where)/select_n | solution.py:683
  320.6 0.7 fusion.14
  322.0 1.6 copy.55
  323.6 1.6 pad_maximum_fusion
  325.1 8.6 %collective-permute-done.9 = bf16[2,4,96,768]{3,2,0,1:T(8,128)(2,1)S(1)} collective-permute-done((bf16[2,4,96,768]{3,2,0,1:T(8,128)(2,1)S(1)}, bf16[2,4,96,768]{3,2,0,1:T(8,128)(2,1)S(1)}, u32[]{:S(2)}, u32[]{:S(2)}) %collective-permute-start.9) | collective-permute-done | bytes 1179680 | tf_op jit(solution)/shard_map/ppermute | solution.py:596
  334.7 1.2 collective-permute-start.11
  336.0 2.8 collective-permute-start.12
  338.8 7.1 %maximum_select_fusion = bf16[4096,768]{1,0:T(8,128)(2,1)} fusion(bf16[2048,768]{1,0:T(8,128)(2,1)} %collective-permute-done.1, bf16[2048,768]{1,0:T(8,128)(2,1)S(1)} %copy-done.1, pred[]{:T(512)S(6)} %eq.16), kind=kLoop, calls=%fused_computation | loop fusion | flops 28311552 | bytes 12582913 | tf_op jit(solution)/shard_map/jit(_where)/select_n | solution.py:683
  346.0 4.5 %collective-permute-done.11 = bf16[2,96,768]{2,1,0:T(8,128)(2,1)S(1)} collective-permute-done((bf16[2,96,768]{2,1,0:T(8,128)(2,1)S(1)}, bf16[2,96,768]{2,1,0:T(8,128)(2,1)S(1)}, u32[]{:S(2)}, u32[]{:S(2)}) %collective-permute-start.11) | collective-permute-done | bytes 294944 | tf_op jit(solution)/shard_map/ppermute | solution.py:615
  350.6 0.8 slice_bitcast_fusion
  (72 shorter events, 10.7 us)
Async XLA Ops:
  181.1 128.0 %collective-permute-start.8 = (bf16[2,768,768]{2,1,0:T(8,128)(2,1)}, bf16[2,768,768]{2,1,0:T(8,128)(2,1)}, u32[]{:S(2)}, u32[]{:S(2)}) collective-permute-start(bf16[2,768,768]{2,1,0:T(8,128)(2,1)} %fusion.2), channel_id=1, source_target_pairs={{0,1},{1,0},{2,3},{3,2},{4,5},{5,4},{6,7},{7,6},{8,9},{9,8},{10,11... | collective-permute-start | bytes 7077896 | tf_op jit(solution)/shard_map/ppermute | solution.py:596
  216.0 1.9 copy-start.5
  216.0 1.9 copy-start.4
  217.4 76.6 %collective-permute-start.2 = (bf16[1,768,768]{2,1,0:T(8,128)(2,1)S(1)}, bf16[1,768,768]{2,1,0:T(8,128)(2,1)}, u32[]{:S(2)}, u32[]{:S(2)}) collective-permute-start(bf16[1,768,768]{2,1,0:T(8,128)(2,1)S(1)} %constant_dynamic-slice_fusion.3), channel_id=1, source_target_pairs={{0,1},{1,0},{2,3},{3,2},{4,5},{5,4},{6,7},{7,6},{8,9},{9,8},{10,11... | collective-permute-start | bytes 3538952 | tf_op jit(solution)/shard_map/ppermute | solution.py:596
  220.6 31.6 %collective-permute-start.7 = (f32[13056]{0:T(1024)}, f32[13056]{0:T(1024)}, u32[]{:S(2)}, u32[]{:S(2)}) collective-permute-start(f32[13056]{0:T(1024)} %constant_dynamic-update-slice_fusion), channel_id=1, source_target_pairs={{0,1},{1,0},{2,3},{3,2},{4,5},{5,4},{6,7},{7,6},{8,9},{9,8},{10,11... | collective-permute-start | bytes 156680 | tf_op jit(solution)/shard_map/ppermute | solution.py:596
  220.6 73.4 %copy-start.2 = (bf16[2,768,768]{2,1,0:T(8,128)(2,1)S(1)}, bf16[2,768,768]{2,1,0:T(8,128)(2,1)}, u32[]{:S(2)}) copy-start(bf16[2,768,768]{2,1,0:T(8,128)(2,1)} %get-tuple-element.51) | copy-start | bytes 7077892
  251.6 87.2 %collective-permute-start.1 = (bf16[2048,768]{1,0:T(8,128)(2,1)}, bf16[2048,768]{1,0:T(8,128)(2,1)}, u32[]{:S(2)}, u32[]{:S(2)}) collective-permute-start(bf16[2048,768]{1,0:T(8,128)(2,1)} %shard_map.309), channel_id=1, source_target_pairs={{0,1},{1,0},{2,3},{3,2},{4,5},{5,4},{6,7},{7,6},{8,9},{9,8},{10,11... | collective-permute-start | bytes 9437192 | tf_op jit(solution)/shard_map/ppermute | solution.py:596
  252.1 62.5 %collective-permute-start = (bf16[1024,768]{1,0:T(8,128)(2,1)}, bf16[1024,768]{1,0:T(8,128)(2,1)}, u32[]{:S(2)}, u32[]{:S(2)}) collective-permute-start(bf16[1024,768]{1,0:T(8,128)(2,1)} %get-tuple-element.42), channel_id=1, source_target_pairs={{0,1},{1,0},{2,3},{3,2},{4,5},{5,4},{6,7},{7,6},{8,9},{9,8},{10,11... | collective-permute-start | bytes 4718600 | tf_op jit(solution)/shard_map/ppermute | solution.py:596
  294.0 2.5 copy-start.3
  295.6 16.2 %copy-start = (bf16[2,768,768]{2,1,0:T(8,128)(2,1)S(1)}, bf16[2,768,768]{2,1,0:T(8,128)(2,1)}, u32[]{:S(2)}) copy-start(bf16[2,768,768]{2,1,0:T(8,128)(2,1)} %get-tuple-element.55) | copy-start | bytes 7077892
  296.4 10.2 %collective-permute-start.3 = (bf16[1,4,96,768]{3,2,1,0:T(8,128)(2,1)}, bf16[1,4,96,768]{3,2,1,0:T(8,128)(2,1)}, u32[]{:S(2)}, u32[]{:S(2)}) collective-permute-start(bf16[1,4,96,768]{3,2,1,0:T(8,128)(2,1)} %dynamic-slice_bitcast_fusion), channel_id=1, source_target_pairs={{0,4},{4,0},{8,12},{12,8},{16,20},{20,16},{24,28},{28,24},{1,5},{5... | collective-permute-start | bytes 1769480 | tf_op jit(solution)/shard_map/ppermute | solution.py:596
  307.9 11.3 %collective-permute-start.4 = (bf16[1,96,768]{2,1,0:T(8,128)(2,1)S(1)}, bf16[1,96,768]{2,1,0:T(8,128)(2,1)S(1)}, u32[]{:S(2)}, u32[]{:S(2)}) collective-permute-start(bf16[1,96,768]{2,1,0:T(8,128)(2,1)S(1)} %get-tuple-element.115), channel_id=1, source_target_pairs={{0,8},{4,12},{8,16},{12,20},{16,24},{20,28},{24,0},{28,4},{1,9},{5... | collective-permute-start | bytes 442376 | tf_op jit(solution)/shard_map/ppermute | solution.py:615
  308.0 11.3 %collective-permute-start.5 = (bf16[1,96,768]{2,1,0:T(8,128)(2,1)S(1)}, bf16[1,96,768]{2,1,0:T(8,128)(2,1)S(1)}, u32[]{:S(2)}, u32[]{:S(2)}) collective-permute-start(bf16[1,96,768]{2,1,0:T(8,128)(2,1)S(1)} %get-tuple-element.117), channel_id=1, source_target_pairs={{0,16},{4,20},{8,24},{12,28},{16,0},{20,4},{24,8},{28,12},{1,17},{... | collective-permute-start | bytes 442376 | tf_op jit(solution)/shard_map/ppermute | solution.py:615
  309.0 10.2 %collective-permute-start.6 = (bf16[1,96,768]{2,1,0:T(8,128)(2,1)S(1)}, bf16[1,96,768]{2,1,0:T(8,128)(2,1)S(1)}, u32[]{:S(2)}, u32[]{:S(2)}) collective-permute-start(bf16[1,96,768]{2,1,0:T(8,128)(2,1)S(1)} %get-tuple-element.116), channel_id=1, source_target_pairs={{0,24},{4,28},{8,0},{12,4},{16,8},{20,12},{24,16},{28,20},{1,25},{... | collective-permute-start | bytes 442376 | tf_op jit(solution)/shard_map/ppermute | solution.py:615
  314.6 19.2 %collective-permute-start.9 = (bf16[2,4,96,768]{3,2,0,1:T(8,128)(2,1)S(1)}, bf16[2,4,96,768]{3,2,0,1:T(8,128)(2,1)S(1)}, u32[]{:S(2)}, u32[]{:S(2)}) collective-permute-start(bf16[2,4,96,768]{3,2,0,1:T(8,128)(2,1)S(1)} %bitcast.79), channel_id=1, source_target_pairs={{0,4},{4,0},{8,12},{12,8},{16,20},{20,16},{24,28},{28,24},{1,5},{5... | collective-permute-start | bytes 3538952 | tf_op jit(solution)/shard_map/ppermute | solution.py:596
  333.8 5.1 %copy-start.1 = (bf16[2048,768]{1,0:T(8,128)(2,1)S(1)}, bf16[2048,768]{1,0:T(8,128)(2,1)}, u32[]{:S(2)}) copy-start(bf16[2048,768]{1,0:T(8,128)(2,1)} %shard_map.309) | copy-start | bytes 9437188
  334.1 11.8 %collective-permute-start.10 = (bf16[2,96,768]{2,1,0:T(8,128)(2,1)S(1)}, bf16[2,96,768]{2,1,0:T(8,128)(2,1)S(1)}, u32[]{:S(2)}, u32[]{:S(2)}) collective-permute-start(bf16[2,96,768]{2,1,0:T(8,128)(2,1)S(1)} %get-tuple-element.110), channel_id=1, source_target_pairs={{0,8},{4,12},{8,16},{12,20},{16,24},{20,28},{24,0},{28,4},{1,9},{5... | collective-permute-start | bytes 884744 | tf_op jit(solution)/shard_map/ppermute | solution.py:615
  334.7 15.7 %collective-permute-start.11 = (bf16[2,96,768]{2,1,0:T(8,128)(2,1)S(1)}, bf16[2,96,768]{2,1,0:T(8,128)(2,1)S(1)}, u32[]{:S(2)}, u32[]{:S(2)}) collective-permute-start(bf16[2,96,768]{2,1,0:T(8,128)(2,1)S(1)} %get-tuple-element.112), channel_id=1, source_target_pairs={{0,16},{4,20},{8,24},{12,28},{16,0},{20,4},{24,8},{28,12},{1,17},{... | collective-permute-start | bytes 884744 | tf_op jit(solution)/shard_map/ppermute | solution.py:615
  336.0 14.5 %collective-permute-start.12 = (bf16[2,96,768]{2,1,0:T(8,128)(2,1)S(1)}, bf16[2,96,768]{2,1,0:T(8,128)(2,1)S(1)}, u32[]{:S(2)}, u32[]{:S(2)}) collective-permute-start(bf16[2,96,768]{2,1,0:T(8,128)(2,1)S(1)} %get-tuple-element.111), channel_id=1, source_target_pairs={{0,24},{4,28},{8,0},{12,4},{16,8},{20,12},{24,16},{28,20},{1,25},{... | collective-permute-start | bytes 884744 | tf_op jit(solution)/shard_map/ppermute | solution.py:615

commit v2 on v1

v2 whole, which is shorter than its diff:
```python
import functools

import jax
import jax.numpy as jnp
from jax import lax
from jax.experimental import pallas as pl
from jax.experimental.pallas import tpu as pltpu
from jax.sharding import PartitionSpec as P

MESH = pl.DeviceIdType.MESH
F32 = jnp.float32
BF16 = jnp.bfloat16
EPS = 1e-06
VMEM_LIMIT = 58 * 2**20


def dot_nn(a, b):
    return lax.dot_general(a, b, (((1,), (0,)), ((), ())), preferred_element_type=F32)


def dot_nt(a, b):
    return lax.dot_general(a, b, (((1,), (1,)), ((), ())), preferred_element_type=F32)


def dot_tn(a, b):
    return lax.dot_general(a, b, (((0,), (0,)), ((), ())), preferred_element_type=F32)


class Gather:
    def __init__(self, n_hi, ins, outs, s_in, s_out, sems):
        self.n_hi, self.ins, self.outs, self.s_in, self.s_out = n_hi, ins, outs, s_in, s_out
        self.loc, self.zs, self.zr, self.ls, self.lr, self.fs, self.fr, self.cs, self.cr, self.ss, self.sr = sems
        self.dp, self.t = lax.axis_index("dp"), lax.axis_index("tensor")
        self.hi, self.lo = self.dp // 2, lax.rem(self.dp, 2)
        self.core = lax.rem(self.t, 2)
        t_core = self.t + 1 - 2 * self.core
        self.to_x = (self.dp + 1 - 2 * self.lo, self.t)
        self.to_y = (self.dp, lax.rem(self.t + 2, 4))
        self.to_c = (self.dp, t_core)
        self.to_d = (self.dp, lax.rem(t_core + 2, 4))

    def z_peer(self, s):
        return (lax.rem(self.hi + s, self.n_hi) * 2 + self.lo, self.t)

    def block(self, s, side):
        return lax.rem(self.hi - s + self.n_hi, self.n_hi) * 2 + side

    def greet(self):
        barrier = pltpu.get_barrier_semaphore()

        def body(s, carry):
            pl.semaphore_signal(barrier, inc=1, device_id=self.z_peer(s), device_id_type=MESH)
            return carry

        lax.fori_loop(1, self.n_hi, body, 0)
        for peer in (self.to_x, self.to_y, self.to_c, self.to_d):
            pl.semaphore_signal(barrier, inc=1, device_id=peer, device_id_type=MESH)
        pl.semaphore_wait(barrier, self.n_hi + 3)

    def remote(self, src, dst, send, recv, peer):
        return pltpu.make_async_remote_copy(src, dst, send, recv, device_id=peer, device_id_type=MESH)

    def small(self):
        core = self.core
        return (
            pltpu.make_async_copy(self.s_in, self.s_out.at[core], self.loc.at[3]),
            self.remote(self.s_in, self.s_out.at[core], self.ss.at[0], self.sr.at[0], self.to_c),
            self.remote(self.s_in, self.s_out.at[2 + core], self.ss.at[1], self.sr.at[1], self.to_y),
            self.remote(self.s_in, self.s_out.at[2 + core], self.ss.at[2], self.sr.at[2], self.to_d),
        )

    def local(self, k):
        return pltpu.make_async_copy(self.ins[k], self.outs[k].at[self.core, self.dp], self.loc.at[k])

    def z_copy(self, k, s):
        return self.remote(
            self.ins[k], self.outs[k].at[self.core, self.dp], self.zs.at[k, s], self.zr.at[k, s], self.z_peer(s)
        )

    def line(self, k, s, way, own=False):
        out, b = self.outs[k], self.block(s, self.lo)
        src = self.ins[k] if own else out.at[self.core, b]
        dst = out.at[self.core if way == 0 else 2 + self.core, b]
        return self.remote(
            src, dst, self.ls.at[way, k, s], self.lr.at[way, k, s], self.to_x if way == 0 else self.to_y
        )

    def onward(self, k, s, way):
        out = self.outs[k]
        if way == 0:
            src = dst = out.at[2 + self.core, self.block(s, self.lo)]
        else:
            b = self.block(s, 1 - self.lo)
            src, dst = out.at[self.core, b], out.at[2 + self.core, b]
        return self.remote(src, dst, self.fs.at[k, s], self.fr.at[k, s], self.to_x if way == 0 else self.to_y)

    def to_core(self, k, s, which, own=False):
        out = self.outs[k]
        side = self.lo if which % 2 == 0 else 1 - self.lo
        where = out.at[self.core if which < 2 else 2 + self.core, self.block(s, side)]
        return self.remote(
            self.ins[k] if own else where, where, self.cs.at[which, k, s], self.cr.at[which, k, s], self.to_c
        )

    def each(self, first, body):
        def step(s, carry):
            body(s)
            return carry

        lax.fori_loop(first, self.n_hi, step, 0)

    def start(self, k):
        self.local(k).start()
        self.each(1, lambda s: self.z_copy(k, s).start())
        self.line(k, 0, 0, True).start()
        self.line(k, 0, 1, True).start()
        self.to_core(k, 0, 0, True).start()

    def spread(self, k):
        def body(s):
            self.z_copy(k, s).wait_recv()
            self.line(k, s, 0).start()
            self.line(k, s, 1).start()
            self.to_core(k, s, 0).start()

        self.each(1, body)

    def pass_on(self, k, order):
        def over_x(s):
            self.line(k, s, 0).wait_recv()
            self.onward(k, s, 1).start()
            self.to_core(k, s, 1).start()

        def over_y(s):
            self.line(k, s, 1).wait_recv()
            self.onward(k, s, 0).start()
            self.to_core(k, s, 2).start()

        if order == 0:
            self.each(0, over_x)
        elif order == 1:
            self.each(0, over_y)
        else:
            pl.when(self.core == 0)(lambda: self.each(0, over_x))
            pl.when(self.core == 1)(lambda: self.each(0, over_y))

    def complete(self, k, order):
        def late_y(s):
            self.line(k, s, 1).wait_recv()
            self.to_core(k, s, 2).start()

        def late_x(s):
            self.line(k, s, 0).wait_recv()
            self.to_core(k, s, 1).start()

        def diagonal(s):
            self.onward(k, s, 0).wait_recv()
            self.to_core(k, s, 3).start()

        if order == 0:
            self.each(0, late_y)
        elif order == 1:
            self.each(0, late_x)
        else:
            pl.when(self.core == 0)(lambda: self.each(0, late_y))
            pl.when(self.core == 1)(lambda: self.each(0, late_x))
        self.each(0, diagonal)

    def arrived(self, k, whiches):
        def body(s):
            for which in whiches:
                self.to_core(k, s, which).wait_recv()

        self.each(0, body)

    def sent(self, k):
        self.each(1, lambda s: self.z_copy(k, s).wait_send())

        def body(s):
            self.line(k, s, 0).wait_send()
            self.line(k, s, 1).wait_send()
            self.onward(k, s, 0).wait_send()
            for which in range(4):
                self.to_core(k, s, which).wait_send()

        self.each(0, body)


def gather_scratch(n_hi):
    dma = pltpu.SemaphoreType.DMA
    return [
        dma((4,)), dma((3, n_hi)), dma((3, n_hi)), dma((2, 3, n_hi)), dma((2, 3, n_hi)), dma((3, n_hi)),
        dma((3, n_hi)), dma((4, 3, n_hi)), dma((4, 3, n_hi)), dma((3,)), dma((3,)),
    ]


def pool_matrix(pooled, length):
    i = lax.broadcasted_iota(jnp.int32, (pooled, length), 0)
    j = lax.broadcasted_iota(jnp.int32, (pooled, length), 1)
    return jnp.where(j // 2 == i, 0.5, 0.0).astype(BF16)


def lane_low(shape):
    return lax.broadcasted_iota(jnp.int32, shape, 1) < 64


ORDERS = (0, 1, 2)


def attention_kernel(n_seq, length, n_dp, comm, *refs):
    half = length // 2
    group, b = pl.program_id(0), pl.program_id(1)
    step = group * n_seq + b
    core = lax.rem(lax.axis_index("tensor"), 2)
    len_ref, x_ref, bo_ref = refs[:3]
    refs = refs[3:]
    if comm:
        (kw, vw, qw, ow, uw, dw, tab, vbias, hbias) = refs[:9]
        kv_ref, q_ref, p_ref, ctx_ref, hid_ref, pb_ref, a_out, u_out, d_out, s_out = refs[9:19]
        bias, a_in, u_in, d_in, s_in, a_all, s_all, a_sem, s_sem = refs[19:28]
        net = Gather(n_dp // 2, (a_in, u_in, d_in), (a_all, u_out, d_out), s_in, s_all, refs[28:])

        def a_copy(g):
            return pltpu.make_async_copy(a_all.at[g], a_out.at[g], a_sem.at[g])

        s_copy = pltpu.make_async_copy(s_all, s_out, s_sem)

        @pl.when(step == 0)
        def _():
            k, v, o = kw[...], vw[...], ow[...].T
            parts = (k[:, :128], v[:, :128], k[:, 128:], v[:, 128:], qw[...], o[:, 128:], o[:, :128])
            a_in[...] = jnp.concatenate(parts, axis=1).astype(BF16)
            s_in[...] = jnp.zeros_like(s_in)
            s_in[0:3, :] = tab[...]
            s_in[3:4, 128:256] = vbias[:, 0:128]
            s_in[3:4, 320:384] = vbias[:, 128:192]
            s_in[4:5, 0 : hbias.shape[1]] = hbias[...]
            net.greet()
            for copy in net.small():
                copy.start()
            net.start(0)
            u_in[...] = uw[...].astype(BF16)
            d_in[...] = dw[...].T.astype(BF16)
            net.spread(0)
            net.start(1)
            net.pass_on(0, ORDERS[0])
            small = net.small()
            small[0].wait()
            for copy in small[1:]:
                copy.wait()
            s_copy.start()
            net.local(0).wait()
            net.arrived(0, (0, 1))

        def at(n, action):
            pl.when(step == n)(action)

        @pl.when(step == 2)
        def _():
            net.spread(1)
            net.start(2)

        pl.when(step == 5)(lambda: net.complete(0, ORDERS[0]))
        pl.when(step == 7)(lambda: net.spread(2))

        @pl.when(step == 8)
        def _():
            net.arrived(0, (2, 3))
            for g in range(4):
                a_copy(g).start()

        pl.when(step == 9)(lambda: net.pass_on(1, ORDERS[1]))
        pl.when(step == 11)(lambda: net.complete(1, ORDERS[1]))
        pl.when(step == 13)(lambda: net.pass_on(2, ORDERS[2]))

        def weights(lanes):
            return a_all[group, :, :, lanes].reshape(-1, lanes.stop - lanes.start)

        def small_row(i):
            return s_all[group, i : i + 1, :]
    else:
        a_ref, s_ref = refs[:2]
        kv_ref, q_ref, p_ref, ctx_ref, hid_ref, pb_ref, bias = refs[2:]

        def weights(lanes):
            return a_ref[0, :, lanes]

        def small_row(i):
            return s_ref[0, i : i + 1, :]

    krows = pl.ds(pl.multiple_of(b * length, length), length)
    qrows = pl.ds(pl.multiple_of(b * half, half), half)

    @pl.when(group == 0)
    def _():
        pooled = dot_nn(pool_matrix(half, length), x_ref[krows, :])
        hid_ref[qrows, :] = pooled + bo_ref[...]
        pb_ref[qrows, :] = pooled.astype(BF16)

    @pl.when(b == 0)
    def _():
        for h in range(3):
            wide = jnp.broadcast_to(small_row(h), (half, 2 * length))
            bias[h] = pltpu.roll(wide, length, 1, stride=2, stride_axis=0)[:, :length].T

    kv_ref[0] = (dot_nn(x_ref[krows, :], weights(slice(0, 384))) + small_row(3)[:, 0:384]).astype(BF16)
    q = dot_nn(pb_ref[qrows, :], weights(slice(384, 640))) * 0.125
    lanes = lax.broadcasted_iota(jnp.int32, q.shape, 1)
    q = jnp.where(lanes < 192, q, 0.0).astype(BF16)
    q_ref[0] = q
    low = lane_low((half, 128))
    valid = lax.broadcasted_iota(jnp.int32, (length, half), 0) < len_ref[core * n_seq + b]
    q01 = q[:, 0:128]
    zero = jnp.zeros_like(q01)
    heads = (
        (jnp.where(low, q01, zero), 0, 128),
        (jnp.where(low, zero, q01), 0, 128),
        (q[:, 128:256], 256, 256),
    )
    contexts = []
    for h, (qh, k_at, v_at) in enumerate(heads):
        s = dot_nt(kv_ref[0, :, k_at : k_at + 128], qh) + bias[h]
        s = jnp.where(valid, s, -1e30)
        e = jnp.exp(s - jnp.max(s, axis=0, keepdims=True))
        p = (e * (1.0 / jnp.sum(e, axis=0, keepdims=True))).astype(BF16)
        p_ref[0, 0, h] = p
        contexts.append(dot_tn(kv_ref[0, :, v_at : v_at + 128], p))
    c0, c1, c2 = contexts
    ctx01 = jnp.concatenate([c0[0:64], c1[64:128]], axis=0).T
    ctx2 = jnp.concatenate([jnp.zeros_like(c2[0:64]), c2[64:128]], axis=0).T
    ctx = jnp.concatenate([ctx2, ctx01], axis=1).astype(BF16)
    ctx_ref[0] = ctx
    hid_ref[qrows, :] += dot_nt(ctx, weights(slice(512, 768)))

    if comm:

        @pl.when(step == 4 * n_seq - 1)
        def _():
            net.complete(2, ORDERS[2])
            for k in range(3):
                net.sent(k)
            for k in (1, 2):
                net.local(k).wait()
                net.arrived(k, (0, 1, 2, 3))
            for g in range(4):
                a_copy(g).wait()
            s_copy.wait()


def my_core():
    return lax.rem(lax.axis_index("tensor"), 2)


def attention_forward(lengths, tokens, b_out, weights, n_dp, comm):
    n_seq = lengths.shape[0] // 2
    length = tokens.shape[0] // lengths.shape[0]
    half = length // 2
    width = tokens.shape[1]
    once = pl.Buffered(1)

    def fixed(shape):
        return pl.BlockSpec(shape, lambda g, b: (0,) * len(shape), pipeline_mode=once)

    in_specs = [
        pl.BlockSpec(memory_space=pltpu.SMEM),
        pl.BlockSpec((n_seq * length, width), lambda g, b: (my_core(), 0), pipeline_mode=once),
        fixed((1, width)),
    ]
    out_shape = [
        jax.ShapeDtypeStruct((4, n_seq * length, 384), BF16),
        jax.ShapeDtypeStruct((4, n_seq * half, 256), BF16),
        jax.ShapeDtypeStruct((4, n_seq, 3, length, half), BF16),
        jax.ShapeDtypeStruct((4, n_seq * half, 256), BF16),
        jax.ShapeDtypeStruct((n_seq * half, width), F32),
        jax.ShapeDtypeStruct((n_seq * half, width), BF16),
    ]
    out_specs = [
        pl.BlockSpec((1, length, 384), lambda g, b: (g, b, 0)),
        pl.BlockSpec((1, half, 256), lambda g, b: (g, b, 0)),
        pl.BlockSpec((1, 1, 3, length, half), lambda g, b: (g, b, 0, 0, 0)),
        pl.BlockSpec((1, half, 256), lambda g, b: (g, b, 0)),
        fixed((n_seq * half, width)),
        fixed((n_seq * half, width)),
    ]
    scratch = [pltpu.VMEM((3, length, half), F32)]
    params = {"vmem_limit_bytes": VMEM_LIMIT}
    if comm:
        rows = width // n_dp
        in_specs += [fixed(w.shape) for w in weights]
        whole = jax.ShapeDtypeStruct((4, n_dp, rows, width), BF16)
        small = jax.ShapeDtypeStruct((4, 8, 2 * length), F32)
        out_shape += [whole, whole, whole, small]
        out_specs += [pl.BlockSpec(memory_space=pl.ANY)] * 4
        scratch += [pltpu.VMEM((rows, width), BF16)] * 3
        scratch += [
            pltpu.VMEM((8, 2 * length), F32),
            pltpu.VMEM((4, n_dp, rows, width), BF16),
            pltpu.VMEM((4, 8, 2 * length), F32),
            pltpu.SemaphoreType.DMA((4,)),
            pltpu.SemaphoreType.DMA,
        ]
        scratch += gather_scratch(n_dp // 2)
        params.update(collective_id=0, has_side_effects=True)
    else:
        in_specs += [
            pl.BlockSpec((1, width, 768), lambda g, b: (g, 0, 0)),
            pl.BlockSpec((1, 8, 2 * length), lambda g, b: (g, 0, 0)),
        ]
    outs = pl.pallas_call(
        functools.partial(attention_kernel, n_seq, length, n_dp, comm),
        out_shape=out_shape,
        grid=(4, n_seq),
        in_specs=in_specs,
        out_specs=out_specs,
        scratch_shapes=scratch,
        compiler_params=pltpu.CompilerParams(**params),
        cost_estimate=pl.CostEstimate(flops=20 * 10**9, bytes_accessed=40 * 10**6, transcendentals=6 * 10**6),
    )(lengths, tokens, b_out, *weights)
    if comm:
        flat = (4, width, width)
        outs = list(outs)
        outs = outs[:6] + [w.reshape(flat) for w in outs[6:9]] + outs[9:]
    return outs


def row_mean(v):
    return jnp.mean(v, axis=-1, keepdims=True)


def ffn_kernel(
    n_seq, half, len_ref, hid_ref, cot_ref, u_ref, d_ref, s_ref, vec_ref,
    out_ref, ag_ref, gu_ref, gd_ref, gv_ref, nb_all, fg_all, act_all, pg_all, dg,
):
    b = pl.program_id(0)
    rows = pl.ds(pl.multiple_of(b * half, half), half)
    n_gain, n_shift, b_down, f_gain, f_shift = (vec_ref[i : i + 1, :] for i in range(5))

    @pl.when(b == 0)
    def _():
        gv_ref[...] = jnp.zeros_like(gv_ref)

    def add(i, v):
        gv_ref[i : i + 1, :] += jnp.sum(v, axis=0, keepdims=True)

    hid = hid_ref[...]
    centred = hid - row_mean(hid)
    inv1 = lax.rsqrt(row_mean(centred * centred) + EPS)
    unit1 = centred * inv1
    normed = unit1 * n_gain + n_shift
    nb = normed.astype(BF16)
    nb_all[rows, :] = nb
    summed = normed + b_down
    for t in range(4):
        pre = dot_nn(nb, u_ref[t]) + s_ref[t, 4:5, 0:768]
        cdf = 0.5 * (1.0 + lax.erf(pre * 0.7071067811865476))
        act = (pre * cdf).astype(BF16)
        dg[t] = cdf + pre * (0.3989422804014327 * jnp.exp(-0.5 * pre * pre))
        act_all[t, rows, :] = act
        summed = summed + dot_nt(act, d_ref[t])
    centred = summed - row_mean(summed)
    inv2 = lax.rsqrt(row_mean(centred * centred) + EPS)
    unit2 = centred * inv2
    valid = (2 * lax.broadcasted_iota(jnp.int32, (half, 1), 0) < len_ref[my_core() * n_seq + b]).astype(F32)
    out_ref[...] = ((unit2 * f_gain + f_shift) * valid).astype(BF16)
    grad = cot_ref[...].astype(F32) * valid
    add(0, grad * unit2)
    add(1, grad)
    scaled = grad * f_gain
    grad_summed = inv2 * (scaled - row_mean(scaled) - unit2 * row_mean(scaled * unit2))
    add(2, grad_summed)
    fg = grad_summed.astype(BF16)
    fg_all[rows, :] = fg
    normed_grad = grad_summed
    for t in range(4):
        pg = (dot_nn(fg, d_ref[t]) * dg[t]).astype(BF16)
        pg_all[t, rows, :] = pg
        normed_grad = normed_grad + dot_nt(pg, u_ref[t])
    add(3, normed_grad * unit1)
    add(4, normed_grad)
    scaled = normed_grad * n_gain
    hidden_grad = inv1 * (scaled - row_mean(scaled) - unit1 * row_mean(scaled * unit1))
    add(5, hidden_grad)
    ag_ref[...] = hidden_grad.astype(BF16)

    @pl.when(b == n_seq - 1)
    def _():
        for i in range(2):
            pg = pg_all[i]
            gu_ref[i] = dot_tn(nb_all[...], pg).astype(BF16)
            gd_ref[i] = dot_tn(fg_all[...], act_all[i]).astype(BF16)
            gv_ref[6 + i : 7 + i, :] = jnp.sum(pg.astype(F32), axis=0, keepdims=True)


def ffn(lengths, hid, cotangent, u4, d4, s4, vectors, n_seq, half):
    width = hid.shape[1]
    once = pl.Buffered(1)
    return pl.pallas_call(
        functools.partial(ffn_kernel, n_seq, half),
        out_shape=(
            jax.ShapeDtypeStruct((n_seq * half, width), BF16),
            jax.ShapeDtypeStruct((n_seq * half, width), BF16),
            jax.ShapeDtypeStruct((2, width, 768), BF16),
            jax.ShapeDtypeStruct((2, width, 768), BF16),
            jax.ShapeDtypeStruct((8, width), F32),
        ),
        grid=(n_seq,),
        in_specs=[
            pl.BlockSpec(memory_space=pltpu.SMEM),
            pl.BlockSpec((half, width), lambda b: (b, 0)),
            pl.BlockSpec((half, width), lambda b: (my_core() * n_seq + b, 0)),
            pl.BlockSpec((4, width, 768), lambda b: (0, 0, 0), pipeline_mode=once),
            pl.BlockSpec((4, width, 768), lambda b: (0, 0, 0), pipeline_mode=once),
            pl.BlockSpec(s4.shape, lambda b: (0, 0, 0), pipeline_mode=once),
            pl.BlockSpec(vectors.shape, lambda b: (0, 0), pipeline_mode=once),
        ],
        out_specs=[
            pl.BlockSpec((half, width), lambda b: (b, 0)),
            pl.BlockSpec((half, width), lambda b: (b, 0)),
            pl.BlockSpec((2, width, 768), lambda b: (0, 0, 0), pipeline_mode=once),
            pl.BlockSpec((2, width, 768), lambda b: (0, 0, 0), pipeline_mode=once),
            pl.BlockSpec((8, width), lambda b: (0, 0), pipeline_mode=once),
        ],
        scratch_shapes=[
            pltpu.VMEM((n_seq * half, width), BF16),
            pltpu.VMEM((n_seq * half, width), BF16),
            pltpu.VMEM((4, n_seq * half, 768), BF16),
            pltpu.VMEM((4, n_seq * half, 768), BF16),
            pltpu.VMEM((4, half, 768), F32),
        ],
        compiler_params=pltpu.CompilerParams(vmem_limit_bytes=VMEM_LIMIT),
        cost_estimate=pl.CostEstimate(flops=24 * 10**9, bytes_accessed=30 * 10**6, transcendentals=6 * 10**6),
    )(lengths, hid, cotangent, u4, d4, s4, vectors)


class Net:
    def __init__(self, n_hi):
        self.n_hi = n_hi
        self.dp, self.t = lax.axis_index("dp"), lax.axis_index("tensor")
        self.hi, self.lo = self.dp // 2, lax.rem(self.dp, 2)
        self.core = lax.rem(self.t, 2)
        self.to_x = (self.dp + 1 - 2 * self.lo, self.t)
        self.to_c = (self.dp, self.t + 1 - 2 * self.core)

    def place(self, s):
        return lax.rem(self.hi + s, self.n_hi)

    def z_peer(self, s):
        return (self.place(s) * 2 + self.lo, self.t)

    def greet(self):
        barrier = pltpu.get_barrier_semaphore()
        peers = [self.z_peer(s) for s in range(1, self.n_hi)] + [self.to_x, self.to_c]
        for peer in peers:
            pl.semaphore_signal(barrier, inc=1, device_id=peer, device_id_type=MESH)
        pl.semaphore_wait(barrier, len(peers))

    def remote(self, src, dst, send, recv, peer):
        return pltpu.make_async_remote_copy(src, dst, send, recv, device_id=peer, device_id_type=MESH)


class Scatter:
    def __init__(self, net, mine, other, bufs):
        self.net, self.mine, self.other = net, mine, other
        self.r1, self.t1, self.r2, self.t2, self.r3, self.sem, self.zs, self.zr = bufs

    @staticmethod
    def scratch(n_hi, rows, width, stages="cxz"):
        block = (rows, width)
        dma = pltpu.SemaphoreType.DMA
        both = (n_hi, 2) + block if "c" in stages else (8, 128)
        half = (n_hi,) + block
        return [
            pltpu.VMEM(both, BF16), pltpu.VMEM(both, BF16), pltpu.VMEM(half if "x" in stages else (8, 128), BF16),
            pltpu.VMEM(half, BF16), pltpu.VMEM(half if "z" in stages else (8, 128), BF16),
            dma((4,)), dma((n_hi,)), dma((n_hi,)),
        ]

    def over_core(self):
        return self.net.remote(self.other, self.r1, self.sem.at[0], self.sem.at[1], self.net.to_c)

    def over_x(self):
        return self.net.remote(
            self.t1.at[:, 1 - self.net.lo], self.r2, self.sem.at[2], self.sem.at[3], self.net.to_x
        )

    def over_z(self, s):
        return self.net.remote(
            self.t2.at[self.net.place(s)], self.r3.at[s], self.zs.at[s], self.zr.at[s], self.net.z_peer(s)
        )

    def core_to_x(self):
        self.over_core().wait_recv()
        self.t1[...] = self.mine + self.r1[...]
        self.over_x().start()

    def x_sum(self, out):
        self.over_x().wait_recv()
        out[...] = self.t1[:, self.net.lo] + self.r2[...]

    def start_z(self):
        for s in range(1, self.net.n_hi):
            self.over_z(s).start()

    def finish_z(self, out):
        total = self.t2[self.net.hi].astype(F32)
        for s in range(1, self.net.n_hi):
            self.over_z(s).wait_recv()
            total += self.r3[s].astype(F32)
        out[...] = total
        for s in range(1, self.net.n_hi):
            self.over_z(s).wait_send()

    def sent(self):
        self.over_core().wait_send()
        self.over_x().wait_send()


class SmallSum:
    def __init__(self, net, mine, other, bufs):
        self.net, self.mine, self.other = net, mine, other
        self.rc, self.v1, self.rx, self.v2, self.sem, self.zs, self.zr = bufs

    @staticmethod
    def scratch(n_hi, shape):
        dma = pltpu.SemaphoreType.DMA
        return [
            pltpu.VMEM(shape, F32), pltpu.VMEM(shape, F32), pltpu.VMEM(shape, F32), pltpu.VMEM((n_hi,) + shape, F32),
            dma((4,)), dma((n_hi,)), dma((n_hi,)),
        ]

    def over_core(self):
        return self.net.remote(self.other, self.rc, self.sem.at[0], self.sem.at[1], self.net.to_c)

    def over_x(self):
        return self.net.remote(self.v1, self.rx, self.sem.at[2], self.sem.at[3], self.net.to_x)

    def over_z(self, s):
        here = self.v2.at[self.net.hi]
        return self.net.remote(here, here, self.zs.at[s], self.zr.at[s], self.net.z_peer(s))

    def core_to_x(self):
        self.over_core().wait_recv()
        self.v1[...] = self.mine[...] + self.rc[...]
        self.over_x().start()

    def x_to_z(self):
        self.over_x().wait_recv()
        self.v2[self.net.hi] = self.v1[...] + self.rx[...]
        for s in range(1, self.net.n_hi):
            self.over_z(s).start()

    def finish(self, out):
        for s in range(1, self.net.n_hi):
            self.over_z(s).wait()
        out[...] = jnp.sum(self.v2[...], axis=0)
        self.over_core().wait_send()
        self.over_x().wait_send()


def backward_step(half, own, step_refs):
    kv_ref, q_ref, p_ref, ag, a_of, tacc, kvd, qd_ref = step_refs
    low = lane_low((half, 128))
    cg = dot_nn(ag, a_of(slice(512, 768))).astype(BF16)
    q01 = q_ref[0, :, 0:128]
    cg2, cg01 = cg[:, 0:128], cg[:, 128:256]
    zero = jnp.zeros_like(q01)
    heads = (
        (jnp.where(low, q01, zero), jnp.where(low, cg01, zero), 0, 128),
        (jnp.where(low, zero, q01), jnp.where(low, zero, cg01), 0, 128),
        (q_ref[0, :, 128:256], jnp.where(low, zero, cg2), 256, 256),
    )
    kds, vds, qds = [], [], []
    for h, (q, g, k_at, v_at) in enumerate(heads):
        pb16 = p_ref[0, 0, h]
        p = pb16.astype(F32)
        dp = dot_nt(kv_ref[0, :, v_at : v_at + 128], g)
        row = jnp.sum(p * dp, axis=0, keepdims=True)
        sg = (p * (dp - row)).astype(BF16)
        if own:
            tacc[h] += sg.astype(F32)
        kds.append(dot_nn(sg, q))
        vds.append(dot_nn(pb16, g))
        qds.append(dot_tn(kv_ref[0, :, k_at : k_at + 128], sg))
    kvd[:, 0:128] = (kds[0] + kds[1]).astype(BF16)
    kvd[:, 128:256] = (vds[0] + vds[1]).astype(BF16)
    kvd[:, 256:384] = (kds[2] + vds[2]).astype(BF16)
    qd01 = jnp.concatenate([qds[0][0:64], qds[1][64:128]], axis=0).T
    qd2 = jnp.concatenate([qds[2][0:64], jnp.zeros_like(qds[2][0:64])], axis=0).T
    qd = jnp.concatenate([qd01, qd2], axis=1).astype(BF16)
    qd_ref[...] = qd
    return dot_nt(kvd[...], a_of(slice(0, 384))), dot_nt(qd, a_of(slice(384, 640))) * 0.125


def own_kernel(n_seq, length, n_dp, comm, *refs):
    half = length // 2
    n_hi = n_dp // 2
    b, g = pl.program_id(0), pl.program_id(1)
    step = 2 * b + g
    x_ref, a_ref, kv_ref, q_ref, p_ref, ctx_ref, ag_ref, pb_ref = refs[:8]
    refs = refs[8:]
    if comm:
        gu_mine, gd_mine, gu_any, gd_any, gv_ref, half_any = refs[:6]
        tok_ref, pool_ref, ga_ref, sm_ref, up_out, gd_out, gv_out, out_any = refs[6:14]
        kvd, qd_all, tacc = refs[14:17]
        refs = refs[17:]
        net = Net(n_hi)
        other = 1 - net.core
        up = Scatter(net, gu_mine[0], gu_any.at[other], refs[0:8])
        down = Scatter(net, gd_mine[0], gd_any.at[other], refs[8:16])
        vec = SmallSum(net, gv_ref, gv_ref, refs[16:23])
        o_sem = refs[23]
        n_rows = n_seq * half
        there = out_any.at[pl.ds(pl.multiple_of(net.core * n_rows, n_rows), n_rows), :]
        o_local = pltpu.make_async_copy(half_any, there, o_sem.at[0])
        o_core = net.remote(half_any, there, o_sem.at[1], o_sem.at[2], net.to_c)

        @pl.when(step == 0)
        def _():
            net.greet()
            up.over_core().start()
            vec.over_core().start()
            down.over_core().start()
            o_core.start()
            o_local.start()

        @pl.when(step == 1)
        def _():
            up.core_to_x()
            vec.core_to_x()
            down.core_to_x()

        pl.when(step == 2)(vec.x_to_z)

        @pl.when(step == 5)
        def _():
            up.x_sum(up.t2)
            up.start_z()
    else:
        tok_ref, pool_ref, ga_ref, sm_ref, kvd, qd_all, tacc = refs

    @pl.when(b == 0)
    def _():
        tacc[g] = jnp.zeros_like(tacc[g])

    krows = pl.ds(pl.multiple_of(b * length, length), length)
    qrows = pl.ds(pl.multiple_of(b * half, half), half)
    tok, pool = backward_step(
        half,
        True,
        (kv_ref, q_ref, p_ref, ag_ref[qrows, :], lambda lanes: a_ref[g, :, lanes], tacc.at[g], kvd.at[g, krows],
         qd_all.at[g, qrows]),
    )

    @pl.when(g == 0)
    def _():
        tok_ref[...] = tok
        pool_ref[...] = pool

    @pl.when(g == 1)
    def _():
        tok_ref[...] += tok
        pool_ref[...] += pool

    @pl.when(b == n_seq - 1)
    def _():
        ga_ref[g, :, 0:384] = dot_tn(x_ref[...], kvd[g]).astype(BF16)
        gq = dot_tn(pb_ref[...], qd_all[g]) * 0.125
        go = dot_tn(ag_ref[...], ctx_ref[g])
        ga_ref[g, :, 384:512] = gq[:, 0:128].astype(BF16)
        ga_ref[g, :, 512:640] = (gq[:, 128:256] + go[:, 0:128]).astype(BF16)
        ga_ref[g, :, 640:768] = go[:, 128:256].astype(BF16)
        sm_ref[g, 3:8, :] = jnp.zeros((5, 2 * length), F32)
        sm_ref[g, 3:4, 0:384] = jnp.sum(kvd[g].astype(F32), axis=0, keepdims=True)
        i = lax.broadcasted_iota(jnp.int32, (half, half), 0)
        flip = jnp.where(i + lax.broadcasted_iota(jnp.int32, (half, half), 1) == half - 1, 1.0, 0.0).astype(BF16)
        for h in range(3):
            high = tacc[g, h].astype(BF16)
            rest = (tacc[g, h] - high.astype(F32)).astype(BF16)
            turned = dot_nt(flip, high) + dot_nt(flip, rest)
            wide = jnp.concatenate([turned, jnp.zeros((half, length), F32)], axis=1)
            rolled = pltpu.roll(wide, 2, 1, stride=2, stride_axis=0)
            sm_ref[g, h : h + 1, :] = jnp.sum(rolled, axis=0, keepdims=True)

    if comm:

        @pl.when(step == 2 * n_seq - 1)
        def _():
            down.x_sum(gd_out)
            vec.finish(gv_out)
            up.finish_z(up_out)
            up.sent()
            down.sent()
            o_local.wait()
            o_core.wait()


def rest_kernel(n_seq, length, n_dp, comm, *refs):
    half = length // 2
    n_hi = n_dp // 2
    b, g = pl.program_id(0), pl.program_id(1)
    step = 2 * b + g
    a_ref, kv_ref, q_ref, p_ref, ag_ref, tok_in, pool_in = refs[:7]
    refs = refs[7:]
    if comm:
        ga_mine, ga_any, gd_in, sm_mine, sm_any = refs[:5]
        tok_any, ga_out, down_out, sm_out = refs[5:9]
        kvd, qd, tok, pool, stage, t_sem = refs[9:15]
        refs = refs[15:]
        net = Net(n_hi)
        other = 1 - net.core
        att = Scatter(net, ga_mine[0], ga_any.at[other], refs[0:8])
        down = Scatter(net, None, None, refs[8:11] + (gd_in,) + refs[12:16])
        vec = SmallSum(net, sm_mine.at[0], sm_any.at[other], refs[16:23])

        def tok_copies(i):
            row = pl.multiple_of((net.core * n_seq + i) * length, length)
            there = tok_any.at[pl.ds(row, length), :]
            return (
                pltpu.make_async_copy(stage.at[i], there, t_sem.at[0, i]),
                net.remote(stage.at[i], there, t_sem.at[1, i], t_sem.at[2, i], net.to_c),
            )

        @pl.when(step == 0)
        def _():
            net.greet()
            att.over_core().start()
            vec.over_core().start()
            down.start_z()

        @pl.when(step == 1)
        def _():
            att.core_to_x()
            vec.core_to_x()

        pl.when(step == 2)(vec.x_to_z)

        @pl.when(step == 5)
        def _():
            att.x_sum(att.t2)
            att.start_z()
    else:
        tok_out, kvd, qd, tok, pool = refs

    tok_add, pool_add = backward_step(
        half, False, (kv_ref, q_ref, p_ref, ag_ref[...], lambda lanes: a_ref[g, :, lanes], None, kvd, qd)
    )

    @pl.when(g == 0)
    def _():
        tok[...] = tok_in[...] + tok_add
        pool[...] = pool_in[...] + pool_add

    @pl.when(g == 1)
    def _():
        total = (pool[...] + pool_add + ag_ref[...].astype(F32)).astype(BF16)
        final = (tok[...] + tok_add + dot_tn(pool_matrix(half, length), total)).astype(BF16)
        if comm:
            stage[b] = final
            for copy in tok_copies(b):
                copy.start()
        else:
            tok_out[...] = final

    if comm:

        @pl.when(step == 2 * n_seq - 1)
        def _():
            down.finish_z(down_out)
            vec.finish(sm_out)
            att.finish_z(ga_out)
            att.sent()
            for i in range(n_seq):
                for copy in tok_copies(i):
                    copy.wait()


def fixed(shape, first=None):
    def index(*grid):
        head = 0 if first is None else first()
        return (head,) + (0,) * (len(shape) - 1)

    return pl.BlockSpec(shape, index, pipeline_mode=pl.Buffered(1))


ANY = pl.BlockSpec(memory_space=pl.ANY)


def backward_specs(n_seq, length, width, own):
    half = length // 2
    at = 0 if own else 2
    return (
        fixed((2, width, 768), (lambda: 0) if own else (lambda: 1)),
        pl.BlockSpec((1, length, 384), lambda b, g: (at + g, b, 0)),
        pl.BlockSpec((1, half, 256), lambda b, g: (at + g, b, 0)),
        pl.BlockSpec((1, 1, 3, length, half), lambda b, g: (at + g, b, 0, 0, 0)),
    )


def backward_own(tokens, a4, kv, q, p, ctx, ag, pb, gu, gd, gv, out_half, n_seq, n_dp, comm):
    length = kv.shape[1] // n_seq
    half = length // 2
    width = tokens.shape[1]
    n_tok, n_pool = n_seq * length, n_seq * half
    a_spec, kv_spec, q_spec, p_spec = backward_specs(n_seq, length, width, True)
    in_specs = [
        fixed((n_tok, width), my_core), a_spec, kv_spec, q_spec, p_spec, fixed((2, n_pool, 256)),
        fixed((n_pool, width)), fixed((n_pool, width)),
    ]
    args = [tokens, a4, kv, q, p, ctx, ag, pb]
    out_shape = [
        jax.ShapeDtypeStruct((n_tok, width), F32),
        jax.ShapeDtypeStruct((n_pool, width), F32),
        jax.ShapeDtypeStruct((2, width, 768), BF16),
        jax.ShapeDtypeStruct((2, 8, 2 * length), F32),
    ]
    out_specs = [
        pl.BlockSpec((length, width), lambda b, g: (b, 0)),
        pl.BlockSpec((half, width), lambda b, g: (b, 0)),
        fixed((2, width, 768)),
        fixed((2, 8, 2 * length)),
    ]
    scratch = [
        pltpu.VMEM((2, n_tok, 384), BF16), pltpu.VMEM((2, n_pool, 256), BF16), pltpu.VMEM((2, 3, length, half), F32),
    ]
    params = {"vmem_limit_bytes": VMEM_LIMIT}
    if comm:
        n_hi, rows = n_dp // 2, width // n_dp
        split = (2, n_hi, 2, rows, width)
        gu, gd = gu.reshape(split), gd.reshape(split)
        in_specs += [fixed((1,) + split[1:], my_core)] * 2 + [ANY, ANY, fixed(gv.shape), ANY]
        args += [gu, gd, gu, gd, gv, out_half]
        out_shape += [
            jax.ShapeDtypeStruct((rows, width), F32),
            jax.ShapeDtypeStruct((n_hi, rows, width), BF16),
            jax.ShapeDtypeStruct(gv.shape, F32),
            jax.ShapeDtypeStruct((2 * n_pool, width), BF16),
        ]
        out_specs += [fixed((rows, width)), fixed((n_hi, rows, width)), fixed(gv.shape), ANY]
        scratch += Scatter.scratch(n_hi, rows, width) + Scatter.scratch(n_hi, rows, width, "cx")
        scratch += SmallSum.scratch(n_hi, gv.shape) + [pltpu.SemaphoreType.DMA((3,))]
        params.update(collective_id=1, has_side_effects=True)
    return pl.pallas_call(
        functools.partial(own_kernel, n_seq, length, n_dp, comm),
        out_shape=out_shape,
        grid=(n_seq, 2),
        in_specs=in_specs,
        out_specs=out_specs,
        scratch_shapes=scratch,
        compiler_params=pltpu.CompilerParams(**params),
        cost_estimate=pl.CostEstimate(flops=20 * 10**9, bytes_accessed=30 * 10**6, transcendentals=0),
    )(*args)


def backward_rest(a4, kv, q, p, ag, tok, pool, ga, gd, sm, n_seq, n_dp, comm):
    length = kv.shape[1] // n_seq
    half = length // 2
    width = ag.shape[1]
    n_tok = n_seq * length
    in_specs = list(backward_specs(n_seq, length, width, False)) + [
        pl.BlockSpec((half, width), lambda b, g: (b, 0)),
        pl.BlockSpec((length, width), lambda b, g: (b, 0)),
        pl.BlockSpec((half, width), lambda b, g: (b, 0)),
    ]
    args = [a4, kv, q, p, ag, tok, pool]
    scratch = [
        pltpu.VMEM((length, 384), BF16), pltpu.VMEM((half, 256), BF16), pltpu.VMEM((length, width), F32),
        pltpu.VMEM((half, width), F32),
    ]
    params = {"vmem_limit_bytes": VMEM_LIMIT}
    if comm:
        n_hi, rows = n_dp // 2, width // n_dp
        split = (2, n_hi, 2, rows, width)
        ga = ga.reshape(split)
        small = sm.shape[1:]
        in_specs += [
            fixed((1,) + split[1:], my_core), ANY, fixed((n_hi, rows, width)), fixed((1,) + small, my_core), ANY,
        ]
        args += [ga, ga, gd, sm, sm]
        out_shape = [
            jax.ShapeDtypeStruct((2 * n_tok, width), BF16),
            jax.ShapeDtypeStruct((rows, width), F32),
            jax.ShapeDtypeStruct((rows, width), F32),
            jax.ShapeDtypeStruct(small, F32),
        ]
        out_specs = [ANY, fixed((rows, width)), fixed((rows, width)), fixed(small)]
        scratch += [pltpu.VMEM((n_seq, length, width), BF16), pltpu.SemaphoreType.DMA((3, n_seq))]
        scratch += Scatter.scratch(n_hi, rows, width) + Scatter.scratch(n_hi, rows, width, "z")
        scratch += SmallSum.scratch(n_hi, small)
        params.update(collective_id=2, has_side_effects=True)
    else:
        out_shape = jax.ShapeDtypeStruct((n_tok, width), BF16)
        out_specs = pl.BlockSpec((length, width), lambda b, g: (b, 0))
    return pl.pallas_call(
        functools.partial(rest_kernel, n_seq, length, n_dp, comm),
        out_shape=out_shape,
        grid=(n_seq, 2),
        in_specs=in_specs,
        out_specs=out_specs,
        scratch_shapes=scratch,
        compiler_params=pltpu.CompilerParams(**params),
        cost_estimate=pl.CostEstimate(flops=20 * 10**9, bytes_accessed=30 * 10**6, transcendentals=0),
    )(*args)


def unpack(a_sum):
    key = jnp.concatenate([a_sum[:, 0:128], a_sum[:, 256:320]], axis=1)
    value = jnp.concatenate([a_sum[:, 128:256], a_sum[:, 320:384]], axis=1)
    out = jnp.concatenate([a_sum[:, 640:768], a_sum[:, 576:640]], axis=1).T
    return a_sum[:, 384:576], key, value, out


def gather_plain(weights, length):
    kw, vw, qw, ow, uw, dw, tab, vbias, hbias = weights
    ot = ow.T
    packed = jnp.concatenate([kw[:, :128], vw[:, :128], kw[:, 128:], vw[:, 128:], qw, ot[:, 128:], ot[:, :128]], axis=1)
    small = jnp.zeros((8, 2 * length), F32).at[0:3].set(tab).at[3, 128:256].set(vbias[0, :128])
    small = small.at[3, 320:384].set(vbias[0, 128:]).at[4, : hbias.shape[1]].set(hbias[0])
    first = 2 * (lax.axis_index("tensor") // 2)

    def groups(v):
        every = lax.all_gather(v, "tensor")
        return lax.dynamic_slice_in_dim(jnp.concatenate([every, every]), first, 4)

    wide = jnp.stack([packed, uw, dw.T], axis=1).astype(BF16)
    wide = groups(lax.all_gather(wide, "dp", axis=0, tiled=True))
    return wide[:, :, 0], wide[:, :, 1], wide[:, :, 2], groups(small)


def sum_plain(grads, n_dp):
    core = my_core()
    mine = lax.dynamic_index_in_dim(grads, core, 0, keepdims=False).astype(F32)
    other = lax.dynamic_index_in_dim(grads, 1 - core, 0, keepdims=False)
    total = mine + lax.ppermute(other, "tensor", [(i, i ^ 1) for i in range(4)]).astype(F32)
    return lax.psum_scatter(total, "dp", scatter_dimension=0, tiled=True)


def shards(
    n_dp, tokens, lengths, cotangent, query_weight, key_weight, value_weight, value_bias, output_weight,
    b_out, rel_table, norm_gain, norm_shift, up_weight, hidden_bias, down_weight, b_down, final_gain, final_shift,
):
    seq_count = lengths.shape[0]
    length = tokens.shape[0] // seq_count
    half = length // 2
    n_seq = seq_count // 2
    core = my_core()
    n_hi, rows = n_dp // 2, tokens.shape[1] // n_dp
    comm = rows % 16 == 0 and n_hi <= 4

    weights = (
        key_weight, value_weight, query_weight, output_weight, up_weight, down_weight, rel_table,
        value_bias[None], hidden_bias[None],
    )
    if not comm:
        weights = gather_plain(weights, length)
        a4, u4, d4, s4 = weights
        weights = (a4, s4)
    kv, q, p, ctx, hid, pb, *gathered = attention_forward(lengths, tokens, b_out[None], weights, n_dp, comm)
    if comm:
        a4, u4, d4, s4 = gathered
    vectors = jnp.stack([norm_gain, norm_shift, b_down, final_gain, final_shift])
    out_half, ag, gu, gd, gv = ffn(lengths, hid, cotangent, u4, d4, s4, vectors, n_seq, half)
    tok, pool, ga, sm, *sums = backward_own(tokens, a4, kv, q, p, ctx, ag, pb, gu, gd, gv, out_half, n_seq, n_dp, comm)
    if comm:
        up_sum, gd, gv, output = sums
        tokens_grad, a_sum, down_sum, sm = backward_rest(a4, kv, q, p, ag, tok, pool, ga, gd, sm, n_seq, n_dp, comm)
    else:
        tok_half = backward_rest(a4, kv, q, p, ag, tok, pool, ga, gd, sm, n_seq, n_dp, comm)
        up_sum, down_sum, a_sum = (sum_plain(v, n_dp) for v in (gu, gd, ga))
        sm, gv = lax.psum((sm, gv), "dp")

        def over_core(v):
            return lax.ppermute(v, "tensor", [(i, i ^ 1) for i in range(4)])

        gv = gv + over_core(gv)
        mine = lax.dynamic_index_in_dim(sm, core, 0, keepdims=False)
        sm = mine + over_core(lax.dynamic_index_in_dim(sm, 1 - core, 0, keepdims=False))

        def join(part):
            got = over_core(part)
            return jnp.where(core == 0, jnp.concatenate([part, got]), jnp.concatenate([got, part]))

        output, tokens_grad = join(out_half), join(tok_half)
    query_sum, key_sum, value_sum, outw_sum = unpack(a_sum)
    vbias_sum = jnp.concatenate([sm[3, 128:256], sm[3, 320:384]])
    ubias_sum = lax.dynamic_index_in_dim(gv[6:8], core, 0, keepdims=False)
    return (
        output, tokens_grad, query_sum, key_sum, value_sum, vbias_sum, outw_sum, gv[5], sm[0:3],
        gv[3], gv[4], up_sum, ubias_sum, down_sum.T, gv[2], gv[0], gv[1],
    )


def solution(mesh):
    row, col, both, rep = P("dp", None), P("tensor", "dp"), P("dp", "tensor"), P()
    ten, table = P("tensor"), P("tensor", None)
    in_specs = (
        row, P("dp"), row, both, both, both, ten, col, rep, table, rep, rep, both, ten, col, rep, rep, rep,
    )
    out_specs = (
        row, row, both, both, both, ten, col, rep, table, rep, rep, both, ten, col, rep, rep, rep,
    )
    body = functools.partial(shards, mesh.shape["dp"])
    return jax.shard_map(body, mesh=mesh, in_specs=in_specs, out_specs=out_specs, check_vma=False)
```

time: 353 us -> 267 us (0.76)
  blocking collectives: 40.4 us -> 0 us
  other arithmetic: 33 us -> 1.27 us
  Pallas kernels: 225 us -> 242 us
  waiting for transfers between devices: 16.8 us -> 0 us
  starting transfers between devices: 9.9 us -> 0 us
    psum x1 -> x0, blocking collectives: 40.4 us -> none  [reduce_small(): return lax.psum(v, 'dp')]
    pallas_call x4 -> x3, Pallas kernels: 186 us -> 203 us  [the longest x1 95.5 us: attention_forward(): pl.pallas_call(functools.partial(attention_kernel, n_seq, length, n_dp, c...]
    ppermute x13 -> x0, waiting for transfers between devices: 16.8 us -> none  [the longest x7 12.3 us: swap(): return lax.ppermute(v, axis, [(i, i ^ bit) for i in range(size)])]
    select_n x2 -> x0, other arithmetic: 11.6 us -> none  [join(): jnp.where(core == 0, jnp.concatenate([part, got]), jnp.concatenate([got,...]
    ppermute x13 -> x0, starting transfers between devices: 9.9 us -> none  [the longest x6 8.59 us: reduce_groups(): lax.ppermute(give, 'dp', [(i, (i + 2 * s) % n_dp) for i in range(n_dp)])]
    convert_element_type x6 -> x0, other arithmetic: 8.87 us -> none  [the longest x2 4.12 us: reduce_groups(): (mine.astype(F32) + got.astype(F32)).astype(BF16)]
    unnamed x16 -> x24, local copies, waits for them, and re-layouts: 3.87 us -> 10.7 us
  transfers between devices with their start and end apart: 13 -> 0, of which waited for: 3 -> 0; matrix products, arithmetic and copies ran while one was open for 10% -> 0% of each run, Pallas kernels for 19% -> 0%
where the time goes in v2:
time: 267 us; the launch traced here: 266 us
  Pallas kernels  242 us (91%)
  local copies, waits for them, and re-layouts  22.4 us (8%)
    pallas_call x1, Pallas kernels, attention_forward(): pl.pallas_call(functools.partial(attention_kernel, n_seq, length, n_dp, c...  95.5 us
    pallas_call x1, Pallas kernels, backward_own(): pl.pallas_call(functools.partial(own_kernel, n_seq, length, n_dp, comm),...  61.8 us
    pallas_call x1, Pallas kernels, backward_rest(): pl.pallas_call(functools.partial(rest_kernel, n_seq, length, n_dp, comm),...  46 us
    pallas_call x1, Pallas kernels, ffn(): pl.pallas_call(functools.partial(ffn_kernel, n_seq, half), out_shape=(jax...  38.1 us
    unnamed x24, local copies, waits for them, and re-layouts  10.7 us

profile of v2, /device:TPU:0, one launch (start us, length us, event | category | flops | bytes accessed | tf_op | source)
XLA Modules:
  0.0 266.0 jit_solution(16081316100410884051)
XLA Ops:
  0.7 1.9 copy.35.refs_8_
  2.5 1.3 broadcast_in_dim.11.refs_11_
  3.8 1.3 broadcast_in_dim.9.refs_2_
  5.1 0.0 copy-start.4
  5.1 0.0 copy-start.5
  5.1 0.0 copy-start.6
  5.1 0.0 copy-start.7
  5.1 0.0 copy-start.8
  5.1 95.5 %shard_map.305 = (bf16[4,2048,384]{2,1,0:T(8,128)(2,1)}, bf16[4,1024,256]{2,1,0:T(8,128)(2,1)}, bf16[4,4,3,512,256]{4,3,2,1,0:T(8,128)(2,1)}, bf16[4,1024,256]{2...) custom-call(s32[8]{0:T(128)} %len_ref.1, ...), custom_call_target="tpu_custom_call" | custom-call | flops 20000000000 | bytes 40000000 | tf_op jit(solution)/shard_map/pallas_call | solution.py:409
  100.6 0.0 copy-done.4
  100.7 0.0 copy-done.5
  100.7 0.0 copy-done.6
  100.7 0.0 copy-done.7
  100.7 0.0 copy-done.8
  100.7 0.6 stack.23.vec_ref
  101.4 38.1 %shard_map.306 = (bf16[1024,768]{1,0:T(8,128)(2,1)}, bf16[1024,768]{1,0:T(8,128)(2,1)}, bf16[2,768,768]{2,1,0:T(8,128)(2,1)}, bf16[2,768,768]{2,1,0:T(8,128)(2,1)}, f32[8,768]{1,0:T(8,128)}) custom-call(s32[8]{0:T(128)} %len_ref.1, f32[1024,768]{1,0:T(8,128)} %get-tuple-element.49.hid_ref, bf16[2048,768]{1,0:T(8,128)(2,1)} %cot_ref.1, ...), custom_call_target="tpu_custom_call" | custom-call | flops 24000000000 | bytes 30000000 | tf_op jit(solution)/shard_map/pallas_call | solution.py:497
  139.5 61.8 %shard_map.307 = (f32[2048,768]{1,0:T(8,128)}, f32[1024,768]{1,0:T(8,128)}, bf16[2,768,768]{2,1,0:T(8,128)(2,1)}, f32[2,8,1024]{2,1,0:T(8,128)}, f32[96,768]{1,0...) custom-call(bf16[4096,768]{1,0:T(8,128)(2,1)} %refs_0_.3, ...), custom_call_target="tpu_custom_call" | custom-call | flops 20000000000 | bytes 30000000 | tf_op jit(solution)/shard_map/pallas_call | solution.py:942
  201.4 0.7 slice.64
  202.1 1.6 slice_reduce_fusion
  203.7 0.0 copy-start.1
  203.7 46.0 %shard_map.308 = (bf16[4096,768]{1,0:T(8,128)(2,1)}, f32[96,768]{1,0:T(8,128)}, f32[96,768]{1,0:T(8,128)}, f32[8,1024]{1,0:T(8,128)}) custom-call(bf16[4,768,768]{2,1,0:T(8,128)(2,1)} %bitcast.17, bf16[4,2048,384]{2,1,0:T(8,128)(2,1)} %get-tuple-element.45.refs_2_.refs_1_, bf16[4,1024,256]{2,1,0:T(8,128)(2,1)} %get-tuple-element.46.refs_3_.refs_2_, ...), custom_call_target="tpu_custom_call" | custom-call | flops 20000000000 | bytes 30000000 | tf_op jit(solution)/shard_map/pallas_call | solution.py:993
  249.8 0.9 fusion
  250.6 1.0 fusion.1
  251.6 0.7 copy.36
  252.4 0.8 slice_bitcast_fusion
  253.1 0.7 slice_bitcast_fusion.1
  253.8 0.6 pad_maximum_fusion.2
  254.4 0.7 pad_maximum_fusion
  255.0 1.5 slice.51
  256.6 1.4 slice.61
  258.0 0.0 copy-done.1
  258.0 0.0 copy-start
  258.0 1.7 copy.41
  259.6 2.3 copy-done
  261.9 0.0 copy-start.2
  261.9 0.0 copy-start.3
  261.9 2.7 %copy.42 = bf16[4096,768]{1,0:T(8,128)(2,1)} copy(bf16[4096,768]{1,0:T(8,128)(2,1)S(1)} %copy-done) | data formatting | bytes 12582912
  264.6 0.0 copy-done.2
  264.6 0.7 copy.43
  265.3 0.0 copy-done.3
  265.3 0.7 copy.44
  (6 shorter events, 0.0 us)
Async XLA Ops:
  5.1 95.6 %copy-start.4 = (f32[768]{0:T(1024)S(1)}, f32[768]{0:T(1024)}, u32[]{:S(2)}) copy-start(f32[768]{0:T(1024)} %param.28) | copy-start | bytes 9220
  5.1 95.6 %copy-start.5 = (f32[768]{0:T(1024)S(1)}, f32[768]{0:T(1024)}, u32[]{:S(2)}) copy-start(f32[768]{0:T(1024)} %param.29) | copy-start | bytes 9220
  5.1 95.6 %copy-start.6 = (f32[768]{0:T(1024)S(1)}, f32[768]{0:T(1024)}, u32[]{:S(2)}) copy-start(f32[768]{0:T(1024)} %param.33) | copy-start | bytes 9220
  5.1 95.6 %copy-start.7 = (f32[768]{0:T(1024)S(1)}, f32[768]{0:T(1024)}, u32[]{:S(2)}) copy-start(f32[768]{0:T(1024)} %param.34) | copy-start | bytes 9220
  5.1 95.6 %copy-start.8 = (f32[768]{0:T(1024)S(1)}, f32[768]{0:T(1024)}, u32[]{:S(2)}) copy-start(f32[768]{0:T(1024)} %param.35) | copy-start | bytes 9220
  203.7 54.2 %copy-start.1 = (bf16[2048,768]{1,0:T(8,128)(2,1)S(1)}, bf16[2048,768]{1,0:T(8,128)(2,1)}, u32[]{:S(2)}) copy-start(bf16[2048,768]{1,0:T(8,128)(2,1)} %get-tuple-element.120) | copy-start | bytes 9437188
  258.0 3.9 %copy-start = (bf16[4096,768]{1,0:T(8,128)(2,1)S(1)}, bf16[4096,768]{1,0:T(8,128)(2,1)}, u32[]{:S(2)}) copy-start(bf16[4096,768]{1,0:T(8,128)(2,1)} %get-tuple-element.121) | copy-start | bytes 18874372
  261.9 2.7 %copy-start.2 = (f32[96,768]{1,0:T(8,128)S(1)}, f32[96,768]{1,0:T(8,128)}, u32[]{:S(2)}) copy-start(f32[96,768]{1,0:T(8,128)} %get-tuple-element.131) | copy-start | bytes 884740
  261.9 3.4 %copy-start.3 = (f32[96,768]{1,0:T(8,128)S(1)}, f32[96,768]{1,0:T(8,128)}, u32[]{:S(2)}) copy-start(f32[96,768]{1,0:T(8,128)} %get-tuple-element.70) | copy-start | bytes 884740

commit v3 on v2

--- a/solution.py
+++ b/solution.py
@@ -47,12 +47,8 @@
 
     def greet(self):
         barrier = pltpu.get_barrier_semaphore()
-
-        def body(s, carry):
+        for s in range(1, self.n_hi):
             pl.semaphore_signal(barrier, inc=1, device_id=self.z_peer(s), device_id_type=MESH)
-            return carry
-
-        lax.fori_loop(1, self.n_hi, body, 0)
         for peer in (self.to_x, self.to_y, self.to_c, self.to_d):
             pl.semaphore_signal(barrier, inc=1, device_id=peer, device_id_type=MESH)
         pl.semaphore_wait(barrier, self.n_hi + 3)
@@ -102,88 +98,71 @@
             self.ins[k] if own else where, where, self.cs.at[which, k, s], self.cr.at[which, k, s], self.to_c
         )
 
-    def each(self, first, body):
-        def step(s, carry):
-            body(s)
-            return carry
-
-        lax.fori_loop(first, self.n_hi, step, 0)
-
     def start(self, k):
         self.local(k).start()
-        self.each(1, lambda s: self.z_copy(k, s).start())
+        for s in range(1, self.n_hi):
+            self.z_copy(k, s).start()
         self.line(k, 0, 0, True).start()
         self.line(k, 0, 1, True).start()
         self.to_core(k, 0, 0, True).start()
 
-    def spread(self, k):
-        def body(s):
-            self.z_copy(k, s).wait_recv()
-            self.line(k, s, 0).start()
-            self.line(k, s, 1).start()
-            self.to_core(k, s, 0).start()
-
-        self.each(1, body)
-
-    def pass_on(self, k, order):
-        def over_x(s):
-            self.line(k, s, 0).wait_recv()
-            self.onward(k, s, 1).start()
-            self.to_core(k, s, 1).start()
-
-        def over_y(s):
-            self.line(k, s, 1).wait_recv()
-            self.onward(k, s, 0).start()
-            self.to_core(k, s, 2).start()
-
-        if order == 0:
-            self.each(0, over_x)
-        elif order == 1:
-            self.each(0, over_y)
+    def spread(self, k, s):
+        self.z_copy(k, s).wait_recv()
+        self.line(k, s, 0).start()
+        self.line(k, s, 1).start()
+        self.to_core(k, s, 0).start()
+
+    def over_x(self, k, s):
+        self.line(k, s, 0).wait_recv()
+        self.onward(k, s, 1).start()
+        self.to_core(k, s, 1).start()
+
+    def over_y(self, k, s):
+        self.line(k, s, 1).wait_recv()
+        self.onward(k, s, 0).start()
+        self.to_core(k, s, 2).start()
+
+    def late_x(self, k, s):
+        self.line(k, s, 0).wait_recv()
+        self.to_core(k, s, 1).start()
+
+    def late_y(self, k, s):
+        self.line(k, s, 1).wait_recv()
+        self.to_core(k, s, 2).start()
+
+    def pass_on(self, k, s):
+        if k == 2:
+            pl.when(self.core == 0)(lambda: self.over_x(k, s))
+            pl.when(self.core == 1)(lambda: self.over_y(k, s))
         else:
-            pl.when(self.core == 0)(lambda: self.each(0, over_x))
-            pl.when(self.core == 1)(lambda: self.each(0, over_y))
-
-    def complete(self, k, order):
-        def late_y(s):
-            self.line(k, s, 1).wait_recv()
-            self.to_core(k, s, 2).start()
-
-        def late_x(s):
-            self.line(k, s, 0).wait_recv()
-            self.to_core(k, s, 1).start()
-
-        def diagonal(s):
-            self.onward(k, s, 0).wait_recv()
-            self.to_core(k, s, 3).start()
-
-        if order == 0:
-            self.each(0, late_y)
-        elif order == 1:
-            self.each(0, late_x)
-        else:
-            pl.when(self.core == 0)(lambda: self.each(0, late_y))
-            pl.when(self.core == 1)(lambda: self.each(0, late_x))
-        self.each(0, diagonal)
+            (self.over_x, self.over_y)[k](k, s)
+
+    def late(self, k):
+        for s in range(self.n_hi):
+            if k == 2:
+                pl.when(self.core == 0)(lambda: self.late_y(k, s))
+                pl.when(self.core == 1)(lambda: self.late_x(k, s))
+            else:
+                (self.late_y, self.late_x)[k](k, s)
+
+    def diagonal(self, k, s):
+        self.onward(k, s, 0).wait_recv()
+        self.to_core(k, s, 3).start()
 
     def arrived(self, k, whiches):
-        def body(s):
+        for s in range(self.n_hi):
             for which in whiches:
                 self.to_core(k, s, which).wait_recv()
 
-        self.each(0, body)
-
     def sent(self, k):
-        self.each(1, lambda s: self.z_copy(k, s).wait_send())
-
-        def body(s):
+        for s in range(self.n_hi):
+            if s > 0:
+                self.z_copy(k, s).wait_send()
             self.line(k, s, 0).wait_send()
             self.line(k, s, 1).wait_send()
             self.onward(k, s, 0).wait_send()
             for which in range(4):
                 self.to_core(k, s, which).wait_send()
-
-        self.each(0, body)
 
 
 def gather_scratch(n_hi):
@@ -204,21 +183,33 @@
     return lax.broadcasted_iota(jnp.int32, shape, 1) < 64
 
 
-ORDERS = (0, 1, 2)
-
-
 def attention_kernel(n_seq, length, n_dp, comm, *refs):
     half = length // 2
     group, b = pl.program_id(0), pl.program_id(1)
     step = group * n_seq + b
     core = lax.rem(lax.axis_index("tensor"), 2)
-    len_ref, x_ref, bo_ref = refs[:3]
+    len_ref, x_any, bo_ref = refs[:3]
     refs = refs[3:]
     if comm:
         (kw, vw, qw, ow, uw, dw, tab, vbias, hbias) = refs[:9]
         kv_ref, q_ref, p_ref, ctx_ref, hid_ref, pb_ref, a_out, u_out, d_out, s_out = refs[9:19]
-        bias, a_in, u_in, d_in, s_in, a_all, s_all, a_sem, s_sem = refs[19:28]
-        net = Gather(n_dp // 2, (a_in, u_in, d_in), (a_all, u_out, d_out), s_in, s_all, refs[28:])
+        bias, x_ref, x_sem, a_in, u_in, d_in, s_in, a_all, s_all, a_sem, s_sem = refs[19:30]
+        net = Gather(n_dp // 2, (a_in, u_in, d_in), (a_all, u_out, d_out), s_in, s_all, refs[30:])
+    else:
+        a_ref, s_ref = refs[:2]
+        kv_ref, q_ref, p_ref, ctx_ref, hid_ref, pb_ref, bias, x_ref, x_sem = refs[2:]
+    n_tok = n_seq * length
+    x_copy = pltpu.make_async_copy(x_any.at[pl.ds(pl.multiple_of(core * n_tok, n_tok), n_tok), :], x_ref, x_sem)
+
+    def pool_rows():
+        x_copy.wait()
+        pool = pool_matrix(half, length)
+        for i in range(n_seq):
+            pooled = dot_nn(pool, x_ref[i * length : (i + 1) * length, :])
+            hid_ref[i * half : (i + 1) * half, :] = pooled + bo_ref[...]
+            pb_ref[i * half : (i + 1) * half, :] = pooled.astype(BF16)
+
+    if comm:
 
         def a_copy(g):
             return pltpu.make_async_copy(a_all.at[g], a_out.at[g], a_sem.at[g])
@@ -227,6 +218,7 @@
 
         @pl.when(step == 0)
         def _():
+            x_copy.start()
             k, v, o = kw[...], vw[...], ow[...].T
             parts = (k[:, :128], v[:, :128], k[:, 128:], v[:, 128:], qw[...], o[:, 128:], o[:, :128])
             a_in[...] = jnp.concatenate(parts, axis=1).astype(BF16)
@@ -241,9 +233,12 @@
             net.start(0)
             u_in[...] = uw[...].astype(BF16)
             d_in[...] = dw[...].T.astype(BF16)
-            net.spread(0)
+            for s in range(1, n_dp // 2):
+                net.spread(0, s)
+                net.pass_on(0, s - 1)
             net.start(1)
-            net.pass_on(0, ORDERS[0])
+            net.pass_on(0, n_dp // 2 - 1)
+            pool_rows()
             small = net.small()
             small[0].wait()
             for copy in small[1:]:
@@ -252,26 +247,37 @@
             net.local(0).wait()
             net.arrived(0, (0, 1))
 
-        def at(n, action):
-            pl.when(step == n)(action)
-
-        @pl.when(step == 2)
-        def _():
-            net.spread(1)
-            net.start(2)
-
-        pl.when(step == 5)(lambda: net.complete(0, ORDERS[0]))
-        pl.when(step == 7)(lambda: net.spread(2))
-
-        @pl.when(step == 8)
-        def _():
-            net.arrived(0, (2, 3))
-            for g in range(4):
-                a_copy(g).start()
-
-        pl.when(step == 9)(lambda: net.pass_on(1, ORDERS[1]))
-        pl.when(step == 11)(lambda: net.complete(1, ORDERS[1]))
-        pl.when(step == 13)(lambda: net.pass_on(2, ORDERS[2]))
+        n_hi = n_dp // 2
+        plan = {}
+
+        def at(n, action, *args):
+            plan.setdefault(min(n, 4 * n_seq - 1), []).append(functools.partial(action, *args))
+
+        for s in range(1, n_hi):
+            at(s, net.spread, 1, s)
+        at(3, net.start, 2)
+        at(4, net.late, 0)
+        for s in range(n_hi):
+            at(4, net.diagonal, 0, s)
+        for s in range(1, n_hi):
+            at((5, 7, 8)[s - 1], net.spread, 2, s)
+        for s in range(n_hi):
+            at((5, 6, 7, 9)[s], net.pass_on, 1, s)
+        at(2 * n_seq, net.arrived, 0, (2, 3))
+        for g in range(4):
+            at(2 * n_seq, lambda i: a_copy(i).start(), g)
+        at(9, net.late, 1)
+        for s in range(n_hi):
+            at(10 + s, net.pass_on, 2, s)
+        for s in range(n_hi):
+            at((11, 11, 12, 13)[s], net.diagonal, 1, s)
+        at(14, net.late, 2)
+        for n, actions in plan.items():
+
+            @pl.when(step == n)
+            def _():
+                for action in actions:
+                    action()
 
         def weights(lanes):
             return a_all[group, :, :, lanes].reshape(-1, lanes.stop - lanes.start)
@@ -279,8 +285,11 @@
         def small_row(i):
             return s_all[group, i : i + 1, :]
     else:
-        a_ref, s_ref = refs[:2]
-        kv_ref, q_ref, p_ref, ctx_ref, hid_ref, pb_ref, bias = refs[2:]
+
+        @pl.when(step == 0)
+        def _():
+            x_copy.start()
+            pool_rows()
 
         def weights(lanes):
             return a_ref[0, :, lanes]
@@ -290,12 +299,6 @@
 
     krows = pl.ds(pl.multiple_of(b * length, length), length)
     qrows = pl.ds(pl.multiple_of(b * half, half), half)
-
-    @pl.when(group == 0)
-    def _():
-        pooled = dot_nn(pool_matrix(half, length), x_ref[krows, :])
-        hid_ref[qrows, :] = pooled + bo_ref[...]
-        pb_ref[qrows, :] = pooled.astype(BF16)
 
     @pl.when(b == 0)
     def _():
@@ -336,7 +339,8 @@
 
         @pl.when(step == 4 * n_seq - 1)
         def _():
-            net.complete(2, ORDERS[2])
+            for s in range(n_hi):
+                net.diagonal(2, s)
             for k in range(3):
                 net.sent(k)
             for k in (1, 2):
@@ -363,7 +367,7 @@
 
     in_specs = [
         pl.BlockSpec(memory_space=pltpu.SMEM),
-        pl.BlockSpec((n_seq * length, width), lambda g, b: (my_core(), 0), pipeline_mode=once),
+        pl.BlockSpec(memory_space=pl.ANY),
         fixed((1, width)),
     ]
     out_shape = [
@@ -382,7 +386,9 @@
         fixed((n_seq * half, width)),
         fixed((n_seq * half, width)),
     ]
-    scratch = [pltpu.VMEM((3, length, half), F32)]
+    scratch = [
+        pltpu.VMEM((3, length, half), F32), pltpu.VMEM((n_seq * length, width), BF16), pltpu.SemaphoreType.DMA,
+    ]
     params = {"vmem_limit_bytes": VMEM_LIMIT}
     if comm:
         rows = width // n_dp
@@ -559,60 +565,63 @@
 
 
 class Scatter:
+    PARTS = 2
+
     def __init__(self, net, mine, other, bufs):
         self.net, self.mine, self.other = net, mine, other
-        self.r1, self.t1, self.r2, self.t2, self.r3, self.sem, self.zs, self.zr = bufs
+        self.t1, self.t2, self.r3, self.sem, self.xs, self.xr, self.zs, self.zr = bufs
+        self.rows = self.t2.shape[1] // self.PARTS
 
     @staticmethod
-    def scratch(n_hi, rows, width, stages="cxz"):
-        block = (rows, width)
+    def scratch(n_hi, rows, width):
         dma = pltpu.SemaphoreType.DMA
-        both = (n_hi, 2) + block if "c" in stages else (8, 128)
-        half = (n_hi,) + block
-        return [
-            pltpu.VMEM(both, BF16), pltpu.VMEM(both, BF16), pltpu.VMEM(half if "x" in stages else (8, 128), BF16),
-            pltpu.VMEM(half, BF16), pltpu.VMEM(half if "z" in stages else (8, 128), BF16),
-            dma((4,)), dma((n_hi,)), dma((n_hi,)),
-        ]
+        both, half = pltpu.VMEM((n_hi, 2, rows, width), BF16), pltpu.VMEM((n_hi, rows, width), BF16)
+        parts = Scatter.PARTS
+        return [both, half, half, dma((2,)), dma((parts,)), dma((parts,)), dma((parts, n_hi)), dma((parts, n_hi))]
+
+    def part(self, i):
+        return pl.ds(i * self.rows, self.rows)
 
     def over_core(self):
-        return self.net.remote(self.other, self.r1, self.sem.at[0], self.sem.at[1], self.net.to_c)
-
-    def over_x(self):
-        return self.net.remote(
-            self.t1.at[:, 1 - self.net.lo], self.r2, self.sem.at[2], self.sem.at[3], self.net.to_x
-        )
-
-    def over_z(self, s):
-        return self.net.remote(
-            self.t2.at[self.net.place(s)], self.r3.at[s], self.zs.at[s], self.zr.at[s], self.net.z_peer(s)
-        )
+        return self.net.remote(self.other, self.t1, self.sem.at[0], self.sem.at[1], self.net.to_c)
+
+    def over_x(self, i):
+        src = self.t1.at[:, 1 - self.net.lo, self.part(i)]
+        return self.net.remote(src, self.t2.at[:, self.part(i)], self.xs.at[i], self.xr.at[i], self.net.to_x)
+
+    def over_z(self, i, s):
+        src = self.t2.at[self.net.place(s), self.part(i)]
+        dst = self.r3.at[s, self.part(i)]
+        return self.net.remote(src, dst, self.zs.at[i, s], self.zr.at[i, s], self.net.z_peer(s))
 
     def core_to_x(self):
         self.over_core().wait_recv()
-        self.t1[...] = self.mine + self.r1[...]
-        self.over_x().start()
-
-    def x_sum(self, out):
-        self.over_x().wait_recv()
-        out[...] = self.t1[:, self.net.lo] + self.r2[...]
-
-    def start_z(self):
+        self.t1[...] += self.mine[...]
+        for i in range(self.PARTS):
+            self.over_x(i).start()
+
+    def x_to_z(self, i):
+        self.over_x(i).wait_recv()
+        rows = self.part(i)
+        self.t2[:, rows] += self.t1[:, self.net.lo, rows]
         for s in range(1, self.net.n_hi):
-            self.over_z(s).start()
-
-    def finish_z(self, out):
-        total = self.t2[self.net.hi].astype(F32)
-        for s in range(1, self.net.n_hi):
-            self.over_z(s).wait_recv()
-            total += self.r3[s].astype(F32)
-        out[...] = total
-        for s in range(1, self.net.n_hi):
-            self.over_z(s).wait_send()
+            self.over_z(i, s).start()
+
+    def finish(self, out):
+        for i in range(self.PARTS):
+            rows = self.part(i)
+            total = self.t2[self.net.hi, rows].astype(F32)
+            for s in range(1, self.net.n_hi):
+                self.over_z(i, s).wait_recv()
+                total += self.r3[s, rows].astype(F32)
+            out[rows, :] = total
 
     def sent(self):
         self.over_core().wait_send()
-        self.over_x().wait_send()
+        for i in range(self.PARTS):
+            self.over_x(i).wait_send()
+            for s in range(1, self.net.n_hi):
+                self.over_z(i, s).wait_send()
 
 
 class SmallSum:
@@ -655,7 +664,6 @@
         out[...] = jnp.sum(self.v2[...], axis=0)
         self.over_core().wait_send()
         self.over_x().wait_send()
-
 
 def backward_step(half, own, step_refs):
     kv_ref, q_ref, p_ref, ag, a_of, tacc, kvd, qd_ref = step_refs
@@ -691,184 +699,188 @@
     return dot_nt(kvd[...], a_of(slice(0, 384))), dot_nt(qd, a_of(slice(384, 640))) * 0.125
 
 
-def own_kernel(n_seq, length, n_dp, comm, *refs):
+def backward_kernel(n_seq, length, n_dp, comm, *refs):
     half = length // 2
     n_hi = n_dp // 2
-    b, g = pl.program_id(0), pl.program_id(1)
-    step = 2 * b + g
-    x_ref, a_ref, kv_ref, q_ref, p_ref, ctx_ref, ag_ref, pb_ref = refs[:8]
+    step = pl.program_id(0)
+    n_own = 2 * n_seq
+    own = step < n_own
+    b, g = lax.rem(step, n_own) // 2, 2 * (step // n_own) + lax.rem(step, 2)
+    x_any, a_ref, kv_ref, q_ref, p_ref, ctx_any, ag_ref, pb_any = refs[:8]
     refs = refs[8:]
     if comm:
-        gu_mine, gd_mine, gu_any, gd_any, gv_ref, half_any = refs[:6]
-        tok_ref, pool_ref, ga_ref, sm_ref, up_out, gd_out, gv_out, out_any = refs[6:14]
-        kvd, qd_all, tacc = refs[14:17]
-        refs = refs[17:]
+        gu_any, gd_any, gv_ref, half_ref = refs[:4]
+        out_any, tok_any, up_out, down_out, a_out, gv_out, sm_out = refs[4:11]
+        refs = refs[11:]
+    else:
+        tok_out, ga_ref, sm_ref = refs[:3]
+        refs = refs[3:]
+    kvd, qd_all, tacc, tok, pool, x_ref, ctx_ref, pb_ref, fetch = refs[:9]
+    refs = refs[9:]
+    core = my_core()
+    n_tok = n_seq * length
+    late = (
+        pltpu.make_async_copy(x_any.at[pl.ds(pl.multiple_of(core * n_tok, n_tok), n_tok), :], x_ref, fetch.at[0]),
+        pltpu.make_async_copy(ctx_any.at[0:2], ctx_ref, fetch.at[1]),
+        pltpu.make_async_copy(pb_any, pb_ref, fetch.at[2]),
+    )
+    last = step == 2 * n_own - 1
+
+    def at(n, *actions):
+        @pl.when(step == n)
+        def _():
+            for action in actions:
+                action()
+
+    if comm:
+        ga_ref, sm_ref, gu_mine, gd_mine, stage = refs[:5]
         net = Net(n_hi)
-        other = 1 - net.core
-        up = Scatter(net, gu_mine[0], gu_any.at[other], refs[0:8])
-        down = Scatter(net, gd_mine[0], gd_any.at[other], refs[8:16])
-        vec = SmallSum(net, gv_ref, gv_ref, refs[16:23])
-        o_sem = refs[23]
+        other = 1 - core
+        up = Scatter(net, gu_mine, gu_any.at[other], refs[5:13])
+        down = Scatter(net, gd_mine, gd_any.at[other], refs[13:21])
+        att = Scatter(net, ga_ref.at[core], ga_ref.at[other], refs[21:29])
+        vec = SmallSum(net, gv_ref, gv_ref, refs[29:36])
+        small = SmallSum(net, sm_ref.at[core], sm_ref.at[other], refs[36:43])
+        o_sem, t_sem = refs[43:45]
         n_rows = n_seq * half
-        there = out_any.at[pl.ds(pl.multiple_of(net.core * n_rows, n_rows), n_rows), :]
-        o_local = pltpu.make_async_copy(half_any, there, o_sem.at[0])
-        o_core = net.remote(half_any, there, o_sem.at[1], o_sem.at[2], net.to_c)
+        there = out_any.at[pl.ds(pl.multiple_of(core * n_rows, n_rows), n_rows), :]
+        o_copies = (
+            pltpu.make_async_copy(half_ref, there, o_sem.at[0]),
+            net.remote(half_ref, there, o_sem.at[1], o_sem.at[2], net.to_c),
+        )
+        mine = (
+            pltpu.make_async_copy(gu_any.at[core], gu_mine, fetch.at[3]),
+            pltpu.make_async_copy(gd_any.at[core], gd_mine, fetch.at[4]),
+        )
+
+        def tok_copies(i):
+            row = pl.multiple_of((core * n_seq + i) * length, length)
+            where = tok_any.at[pl.ds(row, length), :]
+            return (
+                pltpu.make_async_copy(stage.at[i], where, t_sem.at[0, i]),
+                net.remote(stage.at[i], where, t_sem.at[1, i], t_sem.at[2, i], net.to_c),
+            )
 
         @pl.when(step == 0)
         def _():
+            for copy in mine:
+                copy.start()
             net.greet()
+            vec.over_core().start()
             up.over_core().start()
-            vec.over_core().start()
             down.over_core().start()
-            o_core.start()
-            o_local.start()
-
-        @pl.when(step == 1)
-        def _():
-            up.core_to_x()
-            vec.core_to_x()
-            down.core_to_x()
-
-        pl.when(step == 2)(vec.x_to_z)
-
-        @pl.when(step == 5)
-        def _():
-            up.x_sum(up.t2)
-            up.start_z()
-    else:
-        tok_ref, pool_ref, ga_ref, sm_ref, kvd, qd_all, tacc = refs
-
-    @pl.when(b == 0)
+            for copy in o_copies:
+                copy.start()
+
+        at(1, vec.core_to_x)
+        at(2, mine[0].wait, up.core_to_x, mine[1].wait, down.core_to_x)
+        at(4, lambda: up.x_to_z(0))
+        at(6, lambda: up.x_to_z(1), vec.x_to_z)
+        at(7, lambda: down.x_to_z(0))
+        at(8, att.over_core().start, small.over_core().start)
+        at(9, small.core_to_x, lambda: down.x_to_z(1), att.core_to_x)
+        at(13, lambda: att.x_to_z(0))
+        at(15, small.x_to_z)
+    @pl.when(step == 0)
     def _():
-        tacc[g] = jnp.zeros_like(tacc[g])
+        for copy in late:
+            copy.start()
 
     krows = pl.ds(pl.multiple_of(b * length, length), length)
     qrows = pl.ds(pl.multiple_of(b * half, half), half)
-    tok, pool = backward_step(
-        half,
-        True,
-        (kv_ref, q_ref, p_ref, ag_ref[qrows, :], lambda lanes: a_ref[g, :, lanes], tacc.at[g], kvd.at[g, krows],
-         qd_all.at[g, qrows]),
-    )
-
-    @pl.when(g == 0)
+
+    def run(is_own):
+        gg = lax.rem(g, 2) if is_own else 0
+        kv_at, q_at = (kvd.at[gg, krows], qd_all.at[gg, qrows]) if is_own else (kvd.at[0, krows], qd_all.at[0, qrows])
+        return backward_step(
+            half,
+            is_own,
+            (kv_ref, q_ref, p_ref, ag_ref[qrows, :], lambda lanes: a_ref[g, :, lanes],
+             tacc.at[gg] if is_own else None, kv_at, q_at),
+        )
+
+    @pl.when(own)
     def _():
-        tok_ref[...] = tok
-        pool_ref[...] = pool
-
-    @pl.when(g == 1)
+        @pl.when(b == 0)
+        def _():
+            tacc[g] = jnp.zeros_like(tacc[g])
+
+        tok_add, pool_add = run(True)
+
+        @pl.when(g == 0)
+        def _():
+            tok[krows, :] = tok_add
+            pool[qrows, :] = pool_add
+
+        @pl.when(g == 1)
+        def _():
+            tok[krows, :] += tok_add
+            pool[qrows, :] += pool_add
+
+        @pl.when(step == n_own - 2)
+        def _():
+            for copy in late:
+                copy.wait()
+
+        @pl.when(b == n_seq - 1)
+        def _():
+            def store(lanes, v):
+                v = v.astype(BF16)
+                ga_ref[g, ..., lanes] = v.reshape(ga_ref.shape[1:-1] + v.shape[-1:])
+
+            store(slice(0, 384), dot_tn(x_ref[...], kvd[g]))
+            gq = dot_tn(pb_ref[...], qd_all[g]) * 0.125
+            go = dot_tn(ag_ref[...], ctx_ref[g])
+            store(slice(384, 512), gq[:, 0:128])
+            store(slice(512, 640), gq[:, 128:256] + go[:, 0:128])
+            store(slice(640, 768), go[:, 128:256])
+            sm_ref[g, 3:8, :] = jnp.zeros((5, 2 * length), F32)
+            sm_ref[g, 3:4, 0:384] = jnp.sum(kvd[g].astype(F32), axis=0, keepdims=True)
+            i = lax.broadcasted_iota(jnp.int32, (half, half), 0)
+            j = lax.broadcasted_iota(jnp.int32, (half, half), 1)
+            flip = jnp.where(i + j == half - 1, 1.0, 0.0).astype(BF16)
+            for h in range(3):
+                high = tacc[g, h].astype(BF16)
+                rest = (tacc[g, h] - high.astype(F32)).astype(BF16)
+                turned = dot_nt(flip, high) + dot_nt(flip, rest)
+                wide = jnp.concatenate([turned, jnp.zeros((half, length), F32)], axis=1)
+                rolled = pltpu.roll(wide, 2, 1, stride=2, stride_axis=0)
+                sm_ref[g, h : h + 1, :] = jnp.sum(rolled, axis=0, keepdims=True)
+
+    @pl.when(jnp.logical_not(own))
     def _():
-        tok_ref[...] += tok
-        pool_ref[...] += pool
-
-    @pl.when(b == n_seq - 1)
-    def _():
-        ga_ref[g, :, 0:384] = dot_tn(x_ref[...], kvd[g]).astype(BF16)
-        gq = dot_tn(pb_ref[...], qd_all[g]) * 0.125
-        go = dot_tn(ag_ref[...], ctx_ref[g])
-        ga_ref[g, :, 384:512] = gq[:, 0:128].astype(BF16)
-        ga_ref[g, :, 512:640] = (gq[:, 128:256] + go[:, 0:128]).astype(BF16)
-        ga_ref[g, :, 640:768] = go[:, 128:256].astype(BF16)
-        sm_ref[g, 3:8, :] = jnp.zeros((5, 2 * length), F32)
-        sm_ref[g, 3:4, 0:384] = jnp.sum(kvd[g].astype(F32), axis=0, keepdims=True)
-        i = lax.broadcasted_iota(jnp.int32, (half, half), 0)
-        flip = jnp.where(i + lax.broadcasted_iota(jnp.int32, (half, half), 1) == half - 1, 1.0, 0.0).astype(BF16)
-        for h in range(3):
-            high = tacc[g, h].astype(BF16)
-            rest = (tacc[g, h] - high.astype(F32)).astype(BF16)
-            turned = dot_nt(flip, high) + dot_nt(flip, rest)
-            wide = jnp.concatenate([turned, jnp.zeros((half, length), F32)], axis=1)
-            rolled = pltpu.roll(wide, 2, 1, stride=2, stride_axis=0)
-            sm_ref[g, h : h + 1, :] = jnp.sum(rolled, axis=0, keepdims=True)
+        tok_add, pool_add = run(False)
+
+        @pl.when(g == 2)
+        def _():
+            tok[krows, :] += tok_add
+            pool[qrows, :] += pool_add
+
+        @pl.when(g == 3)
+        def _():
+            total = (pool[qrows, :] + pool_add + ag_ref[qrows, :].astype(F32)).astype(BF16)
+            final = (tok[krows, :] + tok_add + dot_tn(pool_matrix(half, length), total)).astype(BF16)
+            if comm:
+                stage[b] = final
+                for copy in tok_copies(b):
+                    copy.start()
+            else:
+                tok_out[...] = final
 
     if comm:
 
-        @pl.when(step == 2 * n_seq - 1)
-        def _():
-            down.x_sum(gd_out)
+        @pl.when(last)
+        def _():
             vec.finish(gv_out)
-            up.finish_z(up_out)
-            up.sent()
-            down.sent()
-            o_local.wait()
-            o_core.wait()
-
-
-def rest_kernel(n_seq, length, n_dp, comm, *refs):
-    half = length // 2
-    n_hi = n_dp // 2
-    b, g = pl.program_id(0), pl.program_id(1)
-    step = 2 * b + g
-    a_ref, kv_ref, q_ref, p_ref, ag_ref, tok_in, pool_in = refs[:7]
-    refs = refs[7:]
-    if comm:
-        ga_mine, ga_any, gd_in, sm_mine, sm_any = refs[:5]
-        tok_any, ga_out, down_out, sm_out = refs[5:9]
-        kvd, qd, tok, pool, stage, t_sem = refs[9:15]
-        refs = refs[15:]
-        net = Net(n_hi)
-        other = 1 - net.core
-        att = Scatter(net, ga_mine[0], ga_any.at[other], refs[0:8])
-        down = Scatter(net, None, None, refs[8:11] + (gd_in,) + refs[12:16])
-        vec = SmallSum(net, sm_mine.at[0], sm_any.at[other], refs[16:23])
-
-        def tok_copies(i):
-            row = pl.multiple_of((net.core * n_seq + i) * length, length)
-            there = tok_any.at[pl.ds(row, length), :]
-            return (
-                pltpu.make_async_copy(stage.at[i], there, t_sem.at[0, i]),
-                net.remote(stage.at[i], there, t_sem.at[1, i], t_sem.at[2, i], net.to_c),
-            )
-
-        @pl.when(step == 0)
-        def _():
-            net.greet()
-            att.over_core().start()
-            vec.over_core().start()
-            down.start_z()
-
-        @pl.when(step == 1)
-        def _():
-            att.core_to_x()
-            vec.core_to_x()
-
-        pl.when(step == 2)(vec.x_to_z)
-
-        @pl.when(step == 5)
-        def _():
-            att.x_sum(att.t2)
-            att.start_z()
-    else:
-        tok_out, kvd, qd, tok, pool = refs
-
-    tok_add, pool_add = backward_step(
-        half, False, (kv_ref, q_ref, p_ref, ag_ref[...], lambda lanes: a_ref[g, :, lanes], None, kvd, qd)
-    )
-
-    @pl.when(g == 0)
-    def _():
-        tok[...] = tok_in[...] + tok_add
-        pool[...] = pool_in[...] + pool_add
-
-    @pl.when(g == 1)
-    def _():
-        total = (pool[...] + pool_add + ag_ref[...].astype(F32)).astype(BF16)
-        final = (tok[...] + tok_add + dot_tn(pool_matrix(half, length), total)).astype(BF16)
-        if comm:
-            stage[b] = final
-            for copy in tok_copies(b):
-                copy.start()
-        else:
-            tok_out[...] = final
-
-    if comm:
-
-        @pl.when(step == 2 * n_seq - 1)
-        def _():
-            down.finish_z(down_out)
-            vec.finish(sm_out)
-            att.finish_z(ga_out)
-            att.sent()
+            att.x_to_z(1)
+            up.finish(up_out)
+            down.finish(down_out)
+            small.finish(sm_out)
+            att.finish(a_out)
+            for each in (up, down, att):
+                each.sent()
+            for copy in o_copies:
+                copy.wait()
             for i in range(n_seq):
                 for copy in tok_copies(i):
                     copy.wait()
@@ -885,120 +897,73 @@
 ANY = pl.BlockSpec(memory_space=pl.ANY)
 
 
-def backward_specs(n_seq, length, width, own):
-    half = length // 2
-    at = 0 if own else 2
-    return (
-        fixed((2, width, 768), (lambda: 0) if own else (lambda: 1)),
-        pl.BlockSpec((1, length, 384), lambda b, g: (at + g, b, 0)),
-        pl.BlockSpec((1, half, 256), lambda b, g: (at + g, b, 0)),
-        pl.BlockSpec((1, 1, 3, length, half), lambda b, g: (at + g, b, 0, 0, 0)),
-    )
-
-
-def backward_own(tokens, a4, kv, q, p, ctx, ag, pb, gu, gd, gv, out_half, n_seq, n_dp, comm):
+def attention_backward(tokens, a4, kv, q, p, ctx, ag, pb, gu, gd, gv, out_half, n_seq, n_dp, comm):
     length = kv.shape[1] // n_seq
     half = length // 2
     width = tokens.shape[1]
     n_tok, n_pool = n_seq * length, n_seq * half
-    a_spec, kv_spec, q_spec, p_spec = backward_specs(n_seq, length, width, True)
+    n_own = 2 * n_seq
+    n_hi, rows = n_dp // 2, width // n_dp
+
+    def place(n):
+        return 2 * (n // n_own) + lax.rem(n, 2), lax.rem(n, n_own) // 2
+
     in_specs = [
-        fixed((n_tok, width), my_core), a_spec, kv_spec, q_spec, p_spec, fixed((2, n_pool, 256)),
-        fixed((n_pool, width)), fixed((n_pool, width)),
+        ANY,
+        fixed((4, width, 768)),
+        pl.BlockSpec((1, length, 384), lambda n: place(n) + (0,)),
+        pl.BlockSpec((1, half, 256), lambda n: place(n) + (0,)),
+        pl.BlockSpec((1, 1, 3, length, half), lambda n: place(n) + (0, 0, 0)),
+        ANY,
+        fixed((n_pool, width)),
+        ANY,
     ]
     args = [tokens, a4, kv, q, p, ctx, ag, pb]
-    out_shape = [
-        jax.ShapeDtypeStruct((n_tok, width), F32),
-        jax.ShapeDtypeStruct((n_pool, width), F32),
-        jax.ShapeDtypeStruct((2, width, 768), BF16),
-        jax.ShapeDtypeStruct((2, 8, 2 * length), F32),
-    ]
-    out_specs = [
-        pl.BlockSpec((length, width), lambda b, g: (b, 0)),
-        pl.BlockSpec((half, width), lambda b, g: (b, 0)),
-        fixed((2, width, 768)),
-        fixed((2, 8, 2 * length)),
-    ]
     scratch = [
         pltpu.VMEM((2, n_tok, 384), BF16), pltpu.VMEM((2, n_pool, 256), BF16), pltpu.VMEM((2, 3, length, half), F32),
+        pltpu.VMEM((n_tok, width), F32), pltpu.VMEM((n_pool, width), F32),
+        pltpu.VMEM((n_tok, width), BF16), pltpu.VMEM((2, n_pool, 256), BF16), pltpu.VMEM((n_pool, width), BF16),
+        pltpu.SemaphoreType.DMA((5,)),
     ]
     params = {"vmem_limit_bytes": VMEM_LIMIT}
+    small = (8, 2 * length)
     if comm:
-        n_hi, rows = n_dp // 2, width // n_dp
         split = (2, n_hi, 2, rows, width)
-        gu, gd = gu.reshape(split), gd.reshape(split)
-        in_specs += [fixed((1,) + split[1:], my_core)] * 2 + [ANY, ANY, fixed(gv.shape), ANY]
-        args += [gu, gd, gu, gd, gv, out_half]
-        out_shape += [
-            jax.ShapeDtypeStruct((rows, width), F32),
-            jax.ShapeDtypeStruct((n_hi, rows, width), BF16),
-            jax.ShapeDtypeStruct(gv.shape, F32),
-            jax.ShapeDtypeStruct((2 * n_pool, width), BF16),
+        in_specs += [ANY, ANY, fixed(gv.shape), fixed(out_half.shape)]
+        args += [gu.reshape(split), gd.reshape(split), gv, out_half]
+        shares = [jax.ShapeDtypeStruct((rows, width), F32)] * 3
+        out_shape = [
+            jax.ShapeDtypeStruct((2 * n_pool, width), BF16), jax.ShapeDtypeStruct((2 * n_tok, width), BF16), *shares,
+            jax.ShapeDtypeStruct(gv.shape, F32), jax.ShapeDtypeStruct(small, F32),
         ]
-        out_specs += [fixed((rows, width)), fixed((n_hi, rows, width)), fixed(gv.shape), ANY]
-        scratch += Scatter.scratch(n_hi, rows, width) + Scatter.scratch(n_hi, rows, width, "cx")
-        scratch += SmallSum.scratch(n_hi, gv.shape) + [pltpu.SemaphoreType.DMA((3,))]
+        out_specs = [ANY, ANY] + [fixed((rows, width))] * 3 + [fixed(gv.shape), fixed(small)]
+        scratch += [
+            pltpu.VMEM(split, BF16), pltpu.VMEM((2,) + small, F32), pltpu.VMEM(split[1:], BF16),
+            pltpu.VMEM(split[1:], BF16), pltpu.VMEM((n_seq, length, width), BF16),
+        ]
+        for _ in range(3):
+            scratch += Scatter.scratch(n_hi, rows, width)
+        scratch += SmallSum.scratch(n_hi, gv.shape) + SmallSum.scratch(n_hi, small)
+        scratch += [pltpu.SemaphoreType.DMA((3,)), pltpu.SemaphoreType.DMA((3, n_seq))]
         params.update(collective_id=1, has_side_effects=True)
+    else:
+        out_shape = [
+            jax.ShapeDtypeStruct((n_tok, width), BF16), jax.ShapeDtypeStruct((2, width, 768), BF16),
+            jax.ShapeDtypeStruct((2,) + small, F32),
+        ]
+        out_specs = [
+            pl.BlockSpec((length, width), lambda n: (jnp.maximum(n - n_own, 0) // 2, 0)), fixed((2, width, 768)),
+            fixed((2,) + small),
+        ]
     return pl.pallas_call(
-        functools.partial(own_kernel, n_seq, length, n_dp, comm),
+        functools.partial(backward_kernel, n_seq, length, n_dp, comm),
         out_shape=out_shape,
-        grid=(n_seq, 2),
+        grid=(2 * n_own,),
         in_specs=in_specs,
         out_specs=out_specs,
         scratch_shapes=scratch,
         compiler_params=pltpu.CompilerParams(**params),
-        cost_estimate=pl.CostEstimate(flops=20 * 10**9, bytes_accessed=30 * 10**6, transcendentals=0),
-    )(*args)
-
-
-def backward_rest(a4, kv, q, p, ag, tok, pool, ga, gd, sm, n_seq, n_dp, comm):
-    length = kv.shape[1] // n_seq
-    half = length // 2
-    width = ag.shape[1]
-    n_tok = n_seq * length
-    in_specs = list(backward_specs(n_seq, length, width, False)) + [
-        pl.BlockSpec((half, width), lambda b, g: (b, 0)),
-        pl.BlockSpec((length, width), lambda b, g: (b, 0)),
-        pl.BlockSpec((half, width), lambda b, g: (b, 0)),
-    ]
-    args = [a4, kv, q, p, ag, tok, pool]
-    scratch = [
-        pltpu.VMEM((length, 384), BF16), pltpu.VMEM((half, 256), BF16), pltpu.VMEM((length, width), F32),
-        pltpu.VMEM((half, width), F32),
-    ]
-    params = {"vmem_limit_bytes": VMEM_LIMIT}
-    if comm:
-        n_hi, rows = n_dp // 2, width // n_dp
-        split = (2, n_hi, 2, rows, width)
-        ga = ga.reshape(split)
-        small = sm.shape[1:]
-        in_specs += [
-            fixed((1,) + split[1:], my_core), ANY, fixed((n_hi, rows, width)), fixed((1,) + small, my_core), ANY,
-        ]
-        args += [ga, ga, gd, sm, sm]
-        out_shape = [
-            jax.ShapeDtypeStruct((2 * n_tok, width), BF16),
-            jax.ShapeDtypeStruct((rows, width), F32),
-            jax.ShapeDtypeStruct((rows, width), F32),
-            jax.ShapeDtypeStruct(small, F32),
-        ]
-        out_specs = [ANY, fixed((rows, width)), fixed((rows, width)), fixed(small)]
-        scratch += [pltpu.VMEM((n_seq, length, width), BF16), pltpu.SemaphoreType.DMA((3, n_seq))]
-        scratch += Scatter.scratch(n_hi, rows, width) + Scatter.scratch(n_hi, rows, width, "z")
-        scratch += SmallSum.scratch(n_hi, small)
-        params.update(collective_id=2, has_side_effects=True)
-    else:
-        out_shape = jax.ShapeDtypeStruct((n_tok, width), BF16)
-        out_specs = pl.BlockSpec((length, width), lambda b, g: (b, 0))
-    return pl.pallas_call(
-        functools.partial(rest_kernel, n_seq, length, n_dp, comm),
-        out_shape=out_shape,
-        grid=(n_seq, 2),
-        in_specs=in_specs,
-        out_specs=out_specs,
-        scratch_shapes=scratch,
-        compiler_params=pltpu.CompilerParams(**params),
-        cost_estimate=pl.CostEstimate(flops=20 * 10**9, bytes_accessed=30 * 10**6, transcendentals=0),
+        cost_estimate=pl.CostEstimate(flops=40 * 10**9, bytes_accessed=30 * 10**6, transcendentals=0),
     )(*args)
 
 
@@ -1059,12 +1024,11 @@
         a4, u4, d4, s4 = gathered
     vectors = jnp.stack([norm_gain, norm_shift, b_down, final_gain, final_shift])
     out_half, ag, gu, gd, gv = ffn(lengths, hid, cotangent, u4, d4, s4, vectors, n_seq, half)
-    tok, pool, ga, sm, *sums = backward_own(tokens, a4, kv, q, p, ctx, ag, pb, gu, gd, gv, out_half, n_seq, n_dp, comm)
+    sums = attention_backward(tokens, a4, kv, q, p, ctx, ag, pb, gu, gd, gv, out_half, n_seq, n_dp, comm)
     if comm:
-        up_sum, gd, gv, output = sums
-        tokens_grad, a_sum, down_sum, sm = backward_rest(a4, kv, q, p, ag, tok, pool, ga, gd, sm, n_seq, n_dp, comm)
+        output, tokens_grad, up_sum, down_sum, a_sum, gv, sm = sums
     else:
-        tok_half = backward_rest(a4, kv, q, p, ag, tok, pool, ga, gd, sm, n_seq, n_dp, comm)
+        tok_half, ga, sm = sums
         up_sum, down_sum, a_sum = (sum_plain(v, n_dp) for v in (gu, gd, ga))
         sm, gv = lax.psum((sm, gv), "dp")
 

time: 267 us -> 223 us (0.84)
  Pallas kernels: 242 us -> 197 us
    pallas_call x2 -> x1, Pallas kernels: 108 us -> 72.2 us  [attention_backward(): pl.pallas_call(functools.partial(backward_kernel, n_seq, length, n_dp, co...]
    pallas_call x1, Pallas kernels: 95.5 us -> 86.3 us  [attention_forward(): pl.pallas_call(functools.partial(attention_kernel, n_seq, length, n_dp, c...]
    unnamed x24 -> x22, local copies, waits for them, and re-layouts: 10.7 us -> 11.6 us
where the time goes in v3:
time: 223 us; the launch traced here: 222 us
  Pallas kernels  197 us (88%)
  local copies, waits for them, and re-layouts  23.4 us (10%)
    pallas_call x1, Pallas kernels, attention_forward(): pl.pallas_call(functools.partial(attention_kernel, n_seq, length, n_dp, c...  86.3 us
    pallas_call x1, Pallas kernels, attention_backward(): pl.pallas_call(functools.partial(backward_kernel, n_seq, length, n_dp, co...  72.2 us
    pallas_call x1, Pallas kernels, ffn(): pl.pallas_call(functools.partial(ffn_kernel, n_seq, half), out_shape=(jax...  38.1 us
    unnamed x22, local copies, waits for them, and re-layouts  11.6 us

profile of v3, /device:TPU:0, one launch (start us, length us, event | category | flops | bytes accessed | tf_op | source)
XLA Modules:
  0.0 222.1 jit_solution(16479256555597223721)
XLA Ops:
  0.7 1.9 copy.35.refs_8_
  2.5 1.3 broadcast_in_dim.11.refs_11_
  3.8 1.3 broadcast_in_dim.9.refs_2_
  5.1 0.0 copy-start.3
  5.1 0.0 copy-start.4
  5.1 0.0 copy-start.5
  5.1 0.0 copy-start.6
  5.1 0.0 copy-start.7
  5.1 86.3 %shard_map.305 = (bf16[4,2048,384]{2,1,0:T(8,128)(2,1)}, bf16[4,1024,256]{2,1,0:T(8,128)(2,1)}, bf16[4,4,3,512,256]{4,3,2,1,0:T(8,128)(2,1)}, bf16[4,1024,256]{2...) custom-call(s32[8]{0:T(128)} %len_ref.1, ...), custom_call_target="tpu_custom_call" | custom-call | flops 20000000000 | bytes 40000000 | tf_op jit(solution)/shard_map/pallas_call | solution.py:415
  91.4 0.0 copy-done.3
  91.5 0.0 copy-done.4
  91.5 0.0 copy-done.5
  91.5 0.0 copy-done.6
  91.5 0.0 copy-done.7
  91.5 0.6 stack.23.vec_ref
  92.2 38.1 %shard_map.306 = (bf16[1024,768]{1,0:T(8,128)(2,1)}, bf16[1024,768]{1,0:T(8,128)(2,1)}, bf16[2,768,768]{2,1,0:T(8,128)(2,1)}, bf16[2,768,768]{2,1,0:T(8,128)(2,1)}, f32[8,768]{1,0:T(8,128)}) custom-call(s32[8]{0:T(128)} %len_ref.1, f32[1024,768]{1,0:T(8,128)} %get-tuple-element.44.hid_ref, bf16[2048,768]{1,0:T(8,128)(2,1)} %cot_ref.1, ...), custom_call_target="tpu_custom_call" | custom-call | flops 24000000000 | bytes 30000000 | tf_op jit(solution)/shard_map/pallas_call | solution.py:503
  130.3 72.2 %shard_map.307 = (bf16[2048,768]{1,0:T(8,128)(2,1)}, bf16[4096,768]{1,0:T(8,128)(2,1)}, f32[96,768]{1,0:T(8,128)}, f32[96,768]{1,0:T(8,128)}, f32[96,768]{1,0:T(...) custom-call(bf16[4096,768]{1,0:T(8,128)(2,1)} %refs_0_.3, bf16[4,768,768]{2,1,0:T(8,128)(2,1)} %bitcast.15, ...), custom_call_target="tpu_custom_call" | custom-call | flops 40000000000 | bytes 30000000 | tf_op jit(solution)/shard_map/pallas_call | solution.py:958
  202.5 0.7 slice.64
  203.3 1.6 slice_reduce_fusion
  204.9 0.9 fusion
  205.7 1.0 fusion.1
  206.7 0.7 copy.36
  207.5 0.8 slice_bitcast_fusion
  208.2 0.7 slice_bitcast_fusion.1
  208.9 0.6 pad_maximum_fusion.2
  209.5 0.7 pad_maximum_fusion
  210.2 1.5 slice.51
  211.7 1.4 slice.61
  213.1 0.0 copy-start
  213.1 3.9 %copy.41 = bf16[2048,768]{1,0:T(8,128)(2,1)} copy(bf16[2048,768]{1,0:T(8,128)(2,1)} %get-tuple-element.110) | data formatting | bytes 6291456
  217.0 1.0 copy-done
  217.9 0.0 copy-start.2
  217.9 0.0 copy-start.1
  217.9 2.7 %copy.42 = bf16[4096,768]{1,0:T(8,128)(2,1)} copy(bf16[4096,768]{1,0:T(8,128)(2,1)S(1)} %copy-done) | data formatting | bytes 12582912
  220.6 0.0 copy-done.2
  220.6 0.7 copy.43
  221.4 0.0 copy-done.1
  221.4 0.7 copy.44
  (6 shorter events, 0.0 us)
Async XLA Ops:
  5.1 86.4 %copy-start.3 = (f32[768]{0:T(1024)S(1)}, f32[768]{0:T(1024)}, u32[]{:S(2)}) copy-start(f32[768]{0:T(1024)} %param.28) | copy-start | bytes 9220
  5.1 86.4 %copy-start.4 = (f32[768]{0:T(1024)S(1)}, f32[768]{0:T(1024)}, u32[]{:S(2)}) copy-start(f32[768]{0:T(1024)} %param.29) | copy-start | bytes 9220
  5.1 86.4 %copy-start.5 = (f32[768]{0:T(1024)S(1)}, f32[768]{0:T(1024)}, u32[]{:S(2)}) copy-start(f32[768]{0:T(1024)} %param.33) | copy-start | bytes 9220
  5.1 86.4 %copy-start.6 = (f32[768]{0:T(1024)S(1)}, f32[768]{0:T(1024)}, u32[]{:S(2)}) copy-start(f32[768]{0:T(1024)} %param.34) | copy-start | bytes 9220
  5.1 86.4 %copy-start.7 = (f32[768]{0:T(1024)S(1)}, f32[768]{0:T(1024)}, u32[]{:S(2)}) copy-start(f32[768]{0:T(1024)} %param.35) | copy-start | bytes 9220
  213.1 4.9 %copy-start = (bf16[4096,768]{1,0:T(8,128)(2,1)S(1)}, bf16[4096,768]{1,0:T(8,128)(2,1)}, u32[]{:S(2)}) copy-start(bf16[4096,768]{1,0:T(8,128)(2,1)} %get-tuple-element.111) | copy-start | bytes 18874372
  217.9 2.7 %copy-start.2 = (f32[96,768]{1,0:T(8,128)S(1)}, f32[96,768]{1,0:T(8,128)}, u32[]{:S(2)}) copy-start(f32[96,768]{1,0:T(8,128)} %get-tuple-element.121) | copy-start | bytes 884740
  217.9 3.4 %copy-start.1 = (f32[96,768]{1,0:T(8,128)S(1)}, f32[96,768]{1,0:T(8,128)}, u32[]{:S(2)}) copy-start(f32[96,768]{1,0:T(8,128)} %get-tuple-element.60) | copy-start | bytes 884740

commit v4 on v3

--- a/solution.py
+++ b/solution.py
@@ -39,19 +39,25 @@
         self.to_c = (self.dp, t_core)
         self.to_d = (self.dp, lax.rem(t_core + 2, 4))
 
-    def z_peer(self, s):
-        return (lax.rem(self.hi + s, self.n_hi) * 2 + self.lo, self.t)
-
     def block(self, s, side):
         return lax.rem(self.hi - s + self.n_hi, self.n_hi) * 2 + side
 
     def greet(self):
         barrier = pltpu.get_barrier_semaphore()
-        for s in range(1, self.n_hi):
-            pl.semaphore_signal(barrier, inc=1, device_id=self.z_peer(s), device_id_type=MESH)
+        for up, exists in ((0, self.hi < self.n_hi - 1), (1, self.hi > 0)):
+
+            @pl.when(exists)
+            def _():
+                pl.semaphore_signal(barrier, inc=1, device_id=self.z_next(up), device_id_type=MESH)
+
         for peer in (self.to_x, self.to_y, self.to_c, self.to_d):
             pl.semaphore_signal(barrier, inc=1, device_id=peer, device_id_type=MESH)
-        pl.semaphore_wait(barrier, self.n_hi + 3)
+        along_z = jnp.where(self.hi < self.n_hi - 1, 1, 0) + jnp.where(self.hi > 0, 1, 0)
+        pl.semaphore_wait(barrier, 4 + along_z)
+
+    def z_next(self, down):
+        hi = jnp.maximum(self.hi - 1, 0) if down else jnp.minimum(self.hi + 1, self.n_hi - 1)
+        return (hi * 2 + self.lo, self.t)
 
     def remote(self, src, dst, send, recv, peer):
         return pltpu.make_async_remote_copy(src, dst, send, recv, device_id=peer, device_id_type=MESH)
@@ -68,10 +74,17 @@
     def local(self, k):
         return pltpu.make_async_copy(self.ins[k], self.outs[k].at[self.core, self.dp], self.loc.at[k])
 
-    def z_copy(self, k, s):
-        return self.remote(
-            self.ins[k], self.outs[k].at[self.core, self.dp], self.zs.at[k, s], self.zr.at[k, s], self.z_peer(s)
-        )
+    def z_send(self, k, d, down):
+        b = self.block(self.n_hi - d if down else d, self.lo)
+        dst = self.outs[k].at[self.core, b]
+        src = self.ins[k] if d == 0 else dst
+        return self.remote(src, dst, self.zs.at[down, k, d], self.zr.at[down, k, d], self.z_next(down))
+
+    def z_more(self, down):
+        return self.hi > 0 if down else self.hi < self.n_hi - 1
+
+    def z_came(self, d, down):
+        return self.hi + d < self.n_hi if down else self.hi >= d
 
     def line(self, k, s, way, own=False):
         out, b = self.outs[k], self.block(s, self.lo)
@@ -99,18 +112,38 @@
         )
 
     def start(self, k):
+        for down in range(2):
+            pl.when(self.z_more(down))(lambda: self.z_send(k, 0, down).start())
+        self.line(k, 0, 0, True).start()
+        if k == 0:
+            self.line(k, 0, 1, True).start()
+        self.to_core(k, 0, 0, True).start()
         self.local(k).start()
-        for s in range(1, self.n_hi):
-            self.z_copy(k, s).start()
-        self.line(k, 0, 0, True).start()
-        self.line(k, 0, 1, True).start()
-        self.to_core(k, 0, 0, True).start()
-
-    def spread(self, k, s):
-        self.z_copy(k, s).wait_recv()
-        self.line(k, s, 0).start()
-        self.line(k, s, 1).start()
-        self.to_core(k, s, 0).start()
+
+    def lines_y(self, k):
+        for s in range(self.n_hi):
+            self.line(k, s, 1, s == 0).start()
+
+    def near(self, d, action):
+        if d == 0:
+            action(0)
+            return
+        pl.when(self.z_came(d, 0))(lambda: action(d))
+        pl.when(self.z_came(d, 1))(lambda: action(self.n_hi - d))
+
+    def spread(self, k, d):
+        for down in range(2):
+
+            @pl.when(self.z_came(d, down))
+            def _():
+                self.z_send(k, d - 1, down).wait_recv()
+                if d < self.n_hi - 1:
+                    pl.when(self.z_more(down))(lambda: self.z_send(k, d, down).start())
+                s = self.n_hi - d if down else d
+                self.line(k, s, 0).start()
+                if k == 0:
+                    self.line(k, s, 1).start()
+                self.to_core(k, s, 0).start()
 
     def over_x(self, k, s):
         self.line(k, s, 0).wait_recv()
@@ -130,12 +163,13 @@
         self.line(k, s, 1).wait_recv()
         self.to_core(k, s, 2).start()
 
-    def pass_on(self, k, s):
+    def pass_on(self, k, d, core=None):
         if k == 2:
-            pl.when(self.core == 0)(lambda: self.over_x(k, s))
-            pl.when(self.core == 1)(lambda: self.over_y(k, s))
+            way = (self.over_x, self.over_y)[core]
+            pl.when(self.core == core)(lambda: self.near(d, lambda s: way(k, s)))
         else:
-            (self.over_x, self.over_y)[k](k, s)
+            way = (self.over_x, self.over_y)[k]
+            self.near(d, lambda s: way(k, s))
 
     def late(self, k):
         for s in range(self.n_hi):
@@ -155,9 +189,11 @@
                 self.to_core(k, s, which).wait_recv()
 
     def sent(self, k):
+        for down in range(2):
+            for d in range(self.n_hi - 1):
+                came = self.z_more(down) if d == 0 else jnp.logical_and(self.z_more(down), self.z_came(d, down))
+                pl.when(came)(lambda: self.z_send(k, d, down).wait_send())
         for s in range(self.n_hi):
-            if s > 0:
-                self.z_copy(k, s).wait_send()
             self.line(k, s, 0).wait_send()
             self.line(k, s, 1).wait_send()
             self.onward(k, s, 0).wait_send()
@@ -168,7 +204,7 @@
 def gather_scratch(n_hi):
     dma = pltpu.SemaphoreType.DMA
     return [
-        dma((4,)), dma((3, n_hi)), dma((3, n_hi)), dma((2, 3, n_hi)), dma((2, 3, n_hi)), dma((3, n_hi)),
+        dma((4,)), dma((2, 3, n_hi)), dma((2, 3, n_hi)), dma((2, 3, n_hi)), dma((2, 3, n_hi)), dma((3, n_hi)),
         dma((3, n_hi)), dma((4, 3, n_hi)), dma((4, 3, n_hi)), dma((3,)), dma((3,)),
     ]
 
@@ -206,7 +242,7 @@
         pool = pool_matrix(half, length)
         for i in range(n_seq):
             pooled = dot_nn(pool, x_ref[i * length : (i + 1) * length, :])
-            hid_ref[i * half : (i + 1) * half, :] = pooled + bo_ref[...]
+            hid_ref[i * half : (i + 1) * half, :] = pooled + bo_ref[...].reshape(1, -1)
             pb_ref[i * half : (i + 1) * half, :] = pooled.astype(BF16)
 
     if comm:
@@ -224,15 +260,16 @@
             a_in[...] = jnp.concatenate(parts, axis=1).astype(BF16)
             s_in[...] = jnp.zeros_like(s_in)
             s_in[0:3, :] = tab[...]
-            s_in[3:4, 128:256] = vbias[:, 0:128]
-            s_in[3:4, 320:384] = vbias[:, 128:192]
-            s_in[4:5, 0 : hbias.shape[1]] = hbias[...]
+            vb = vbias[...].reshape(1, -1)
+            s_in[3:4, 128:256] = vb[:, 0:128]
+            s_in[3:4, 320:384] = vb[:, 128:192]
+            s_in[4:5, 0 : hbias.shape[0]] = hbias[...].reshape(1, -1)
             net.greet()
             for copy in net.small():
                 copy.start()
             net.start(0)
             u_in[...] = uw[...].astype(BF16)
-            d_in[...] = dw[...].T.astype(BF16)
+            d_in[...] = dw[...].astype(BF16)
             for s in range(1, n_dp // 2):
                 net.spread(0, s)
                 net.pass_on(0, s - 1)
@@ -253,24 +290,23 @@
         def at(n, action, *args):
             plan.setdefault(min(n, 4 * n_seq - 1), []).append(functools.partial(action, *args))
 
-        for s in range(1, n_hi):
-            at(s, net.spread, 1, s)
+        for d in range(1, n_hi):
+            at((1, 2, 3)[d - 1], net.spread, 1, d)
+            at((5, 6, 7)[d - 1], net.spread, 2, d)
         at(3, net.start, 2)
         at(4, net.late, 0)
-        for s in range(n_hi):
-            at(4, net.diagonal, 0, s)
-        for s in range(1, n_hi):
-            at((5, 7, 8)[s - 1], net.spread, 2, s)
-        for s in range(n_hi):
-            at((5, 6, 7, 9)[s], net.pass_on, 1, s)
+        for d in range(n_hi):
+            at(4, net.diagonal, 0, d)
+            at((6, 7, 8, 9)[d], net.pass_on, 1, d)
+            at((10, 10, 11, 11)[d], net.pass_on, 2, d, 0)
+            at((11, 12, 13, 14)[d], net.pass_on, 2, d, 1)
+            at((11, 12, 13, 13)[d], lambda i: net.near(i, lambda s: net.diagonal(1, s)), d)
+        at(3, net.lines_y, 1)
         at(2 * n_seq, net.arrived, 0, (2, 3))
         for g in range(4):
             at(2 * n_seq, lambda i: a_copy(i).start(), g)
+        at(7, net.lines_y, 2)
         at(9, net.late, 1)
-        for s in range(n_hi):
-            at(10 + s, net.pass_on, 2, s)
-        for s in range(n_hi):
-            at((11, 11, 12, 13)[s], net.diagonal, 1, s)
         at(14, net.late, 2)
         for n, actions in plan.items():
 
@@ -368,7 +404,7 @@
     in_specs = [
         pl.BlockSpec(memory_space=pltpu.SMEM),
         pl.BlockSpec(memory_space=pl.ANY),
-        fixed((1, width)),
+        fixed((width,)),
     ]
     out_shape = [
         jax.ShapeDtypeStruct((4, n_seq * length, 384), BF16),
@@ -434,12 +470,12 @@
 
 
 def ffn_kernel(
-    n_seq, half, len_ref, hid_ref, cot_ref, u_ref, d_ref, s_ref, vec_ref,
+    n_seq, half, len_ref, hid_ref, cot_ref, u_ref, d_ref, s_ref, v0, v1, v2, v3, v4,
     out_ref, ag_ref, gu_ref, gd_ref, gv_ref, nb_all, fg_all, act_all, pg_all, dg,
 ):
     b = pl.program_id(0)
     rows = pl.ds(pl.multiple_of(b * half, half), half)
-    n_gain, n_shift, b_down, f_gain, f_shift = (vec_ref[i : i + 1, :] for i in range(5))
+    n_gain, n_shift, b_down, f_gain, f_shift = (v[...].reshape(1, -1) for v in (v0, v1, v2, v3, v4))
 
     @pl.when(b == 0)
     def _():
@@ -517,8 +553,8 @@
             pl.BlockSpec((4, width, 768), lambda b: (0, 0, 0), pipeline_mode=once),
             pl.BlockSpec((4, width, 768), lambda b: (0, 0, 0), pipeline_mode=once),
             pl.BlockSpec(s4.shape, lambda b: (0, 0, 0), pipeline_mode=once),
-            pl.BlockSpec(vectors.shape, lambda b: (0, 0), pipeline_mode=once),
-        ],
+        ]
+        + [pl.BlockSpec((width,), lambda b: (0,), pipeline_mode=once)] * 5,
         out_specs=[
             pl.BlockSpec((half, width), lambda b: (b, 0)),
             pl.BlockSpec((half, width), lambda b: (b, 0)),
@@ -535,7 +571,7 @@
         ],
         compiler_params=pltpu.CompilerParams(vmem_limit_bytes=VMEM_LIMIT),
         cost_estimate=pl.CostEstimate(flops=24 * 10**9, bytes_accessed=30 * 10**6, transcendentals=6 * 10**6),
-    )(lengths, hid, cotangent, u4, d4, s4, vectors)
+    )(lengths, hid, cotangent, u4, d4, s4, *vectors)
 
 
 class Net:
@@ -967,26 +1003,79 @@
     )(*args)
 
 
-def unpack(a_sum):
-    key = jnp.concatenate([a_sum[:, 0:128], a_sum[:, 256:320]], axis=1)
-    value = jnp.concatenate([a_sum[:, 128:256], a_sum[:, 320:384]], axis=1)
-    out = jnp.concatenate([a_sum[:, 640:768], a_sum[:, 576:640]], axis=1).T
-    return a_sum[:, 384:576], key, value, out
+def finish_kernel(big, a_ref, up_ref, down_ref, gv_ref, sm_ref, *refs):
+    n = len(big)
+    moves = [
+        [
+            (
+                pltpu.make_async_copy(src.at[pl.ds(i * chunk, chunk)], buf.at[i], sem.at[0, i]),
+                pltpu.make_async_copy(buf.at[i], dst.at[pl.ds(i * chunk, chunk)], sem.at[1, i]),
+            )
+            for i in range(count)
+        ]
+        for (count, chunk), src, dst, buf, sem in zip(
+            big, refs[:n], refs[n : 2 * n], refs[2 * n + 15 :: 2], refs[2 * n + 16 :: 2]
+        )
+    ]
+    moves = sum(moves, [])
+    for come, _ in moves:
+        come.start()
+    query, key, value, out, up, down, table, vbias, ubias, *vectors = refs[2 * n : 2 * n + 15]
+    query[...] = a_ref[:, 384:576]
+    key[:, 0:128] = a_ref[:, 0:128]
+    key[:, 128:192] = a_ref[:, 256:320]
+    value[:, 0:128] = a_ref[:, 128:256]
+    value[:, 128:192] = a_ref[:, 320:384]
+    out[0:128, :] = a_ref[:, 640:768].T
+    out[128:192, :] = a_ref[:, 512:640].T[64:128]
+    up[...] = up_ref[...]
+    down[...] = down_ref[...]
+    table[...] = sm_ref[0:3, :]
+    vbias[0:128] = sm_ref[3, 128:256]
+    vbias[128:192] = sm_ref[3, 320:384]
+    ubias[...] = jnp.where(my_core() == 0, gv_ref[6, :], gv_ref[7, :])
+    for i, vec in enumerate(vectors):
+        vec[...] = gv_ref[i, :]
+    for come, go in moves:
+        come.wait()
+        go.start()
+    for _, go in moves:
+        go.wait()
+
+
+def finish(big, a_sum, up_sum, down_sum, gv, sm, length):
+    rows, width = a_sum.shape
+    shapes = [(rows, 192)] * 3 + [(192, rows), (rows, 768), (rows, 768), (3, 2 * length), (192,), (768,)] + [(width,)] * 6
+    cuts, scratch = [], []
+    for v in big:
+        count = v.shape[0] // 512
+        cuts.append((count, 512))
+        scratch += [pltpu.VMEM((count, 512, v.shape[1]), v.dtype), pltpu.SemaphoreType.DMA((2, count))]
+    whole = pl.BlockSpec(memory_space=pltpu.VMEM)
+    return pl.pallas_call(
+        functools.partial(finish_kernel, tuple(cuts)),
+        out_shape=[jax.ShapeDtypeStruct(v.shape, v.dtype) for v in big]
+        + [jax.ShapeDtypeStruct(shape, F32) for shape in shapes],
+        in_specs=[whole] * 5 + [ANY] * len(big),
+        out_specs=[ANY] * len(big) + [whole] * len(shapes),
+        scratch_shapes=scratch,
+        compiler_params=pltpu.CompilerParams(vmem_limit_bytes=VMEM_LIMIT),
+    )(a_sum, up_sum, down_sum, gv, sm, *big)
 
 
 def gather_plain(weights, length):
     kw, vw, qw, ow, uw, dw, tab, vbias, hbias = weights
     ot = ow.T
     packed = jnp.concatenate([kw[:, :128], vw[:, :128], kw[:, 128:], vw[:, 128:], qw, ot[:, 128:], ot[:, :128]], axis=1)
-    small = jnp.zeros((8, 2 * length), F32).at[0:3].set(tab).at[3, 128:256].set(vbias[0, :128])
-    small = small.at[3, 320:384].set(vbias[0, 128:]).at[4, : hbias.shape[1]].set(hbias[0])
+    small = jnp.zeros((8, 2 * length), F32).at[0:3].set(tab).at[3, 128:256].set(vbias[:128])
+    small = small.at[3, 320:384].set(vbias[128:]).at[4, : hbias.shape[0]].set(hbias)
     first = 2 * (lax.axis_index("tensor") // 2)
 
     def groups(v):
         every = lax.all_gather(v, "tensor")
         return lax.dynamic_slice_in_dim(jnp.concatenate([every, every]), first, 4)
 
-    wide = jnp.stack([packed, uw, dw.T], axis=1).astype(BF16)
+    wide = jnp.stack([packed, uw, dw], axis=1).astype(BF16)
     wide = groups(lax.all_gather(wide, "dp", axis=0, tiled=True))
     return wide[:, :, 0], wide[:, :, 1], wide[:, :, 2], groups(small)
 
@@ -1012,17 +1101,17 @@
     comm = rows % 16 == 0 and n_hi <= 4
 
     weights = (
-        key_weight, value_weight, query_weight, output_weight, up_weight, down_weight, rel_table,
-        value_bias[None], hidden_bias[None],
+        key_weight, value_weight, query_weight, output_weight, up_weight, down_weight.T, rel_table,
+        value_bias, hidden_bias,
     )
     if not comm:
         weights = gather_plain(weights, length)
         a4, u4, d4, s4 = weights
         weights = (a4, s4)
-    kv, q, p, ctx, hid, pb, *gathered = attention_forward(lengths, tokens, b_out[None], weights, n_dp, comm)
+    kv, q, p, ctx, hid, pb, *gathered = attention_forward(lengths, tokens, b_out, weights, n_dp, comm)
     if comm:
         a4, u4, d4, s4 = gathered
-    vectors = jnp.stack([norm_gain, norm_shift, b_down, final_gain, final_shift])
+    vectors = (norm_gain, norm_shift, b_down, final_gain, final_shift)
     out_half, ag, gu, gd, gv = ffn(lengths, hid, cotangent, u4, d4, s4, vectors, n_seq, half)
     sums = attention_backward(tokens, a4, kv, q, p, ctx, ag, pb, gu, gd, gv, out_half, n_seq, n_dp, comm)
     if comm:
@@ -1044,12 +1133,12 @@
             return jnp.where(core == 0, jnp.concatenate([part, got]), jnp.concatenate([got, part]))
 
         output, tokens_grad = join(out_half), join(tok_half)
-    query_sum, key_sum, value_sum, outw_sum = unpack(a_sum)
-    vbias_sum = jnp.concatenate([sm[3, 128:256], sm[3, 320:384]])
-    ubias_sum = lax.dynamic_index_in_dim(gv[6:8], core, 0, keepdims=False)
+    output, tokens_grad, *cut = finish((output, tokens_grad), a_sum, up_sum, down_sum, gv, sm, length)
+    query_sum, key_sum, value_sum, outw_sum, up_sum, down_sum, table_sum, vbias, ubias = cut[:9]
+    fgain, fshift, dbias, ngain, nshift, obias = cut[9:]
     return (
-        output, tokens_grad, query_sum, key_sum, value_sum, vbias_sum, outw_sum, gv[5], sm[0:3],
-        gv[3], gv[4], up_sum, ubias_sum, down_sum.T, gv[2], gv[0], gv[1],
+        output, tokens_grad, query_sum, key_sum, value_sum, vbias, outw_sum, obias, table_sum,
+        ngain, nshift, up_sum, ubias, down_sum.T, dbias, fgain, fshift,
     )
 
 

time: 223 us -> 204 us (0.915)
  local copies, waits for them, and re-layouts: 23.4 us -> 0 us
  Pallas kernels: 197 us -> 203 us
    unnamed x22 -> x0, local copies, waits for them, and re-layouts: 11.6 us -> none
    pallas_call x0 -> x1, Pallas kernels: none -> 9.3 us  [finish(): pl.pallas_call(functools.partial(finish_kernel, tuple(cuts)), out_shape=[...]
    slice x6 -> x0, local copies, waits for them, and re-layouts: 7.09 us -> none  [the longest x2 1.82 us: unpack(): out = jnp.concatenate([a_sum[:, 640:768], a_sum[:, 576:640]], axis=1).T]
    pallas_call x1, Pallas kernels: 86.3 us -> 82.9 us  [attention_forward(): pl.pallas_call(functools.partial(attention_kernel, n_seq, length, n_dp, c...]
    broadcast_in_dim x2 -> x0, local copies, waits for them, and re-layouts: 2.53 us -> none  [the longest x1 1.27 us: shards(): b_out[None]]
where the time goes in v4:
time: 204 us
  Pallas kernels  203 us (100%)
    pallas_call x1, Pallas kernels, attention_forward(): pl.pallas_call(functools.partial(attention_kernel, n_seq, length, n_dp, c...  82.9 us
    pallas_call x1, Pallas kernels, attention_backward(): pl.pallas_call(functools.partial(backward_kernel, n_seq, length, n_dp, co...  72.2 us
    pallas_call x1, Pallas kernels, ffn(): pl.pallas_call(functools.partial(ffn_kernel, n_seq, half), out_shape=(jax...  38.4 us
    pallas_call x1, Pallas kernels, finish(): pl.pallas_call(functools.partial(finish_kernel, tuple(cuts)), out_shape=[...  9.3 us

profile of v4, /device:TPU:0, one launch (start us, length us, event | category | flops | bytes accessed | tf_op | source)
XLA Modules:
  0.0 203.6 jit_solution(5639335457626124525)
XLA Ops:
  0.7 82.9 %shard_map.305 = (bf16[4,2048,384]{2,1,0:T(8,128)(2,1)}, bf16[4,1024,256]{2,1,0:T(8,128)(2,1)}, bf16[4,4,3,512,256]{4,3,2,1,0:T(8,128)(2,1)}, bf16[4,1024,256]{2...) custom-call(s32[8]{0:T(128)} %len_ref.1, ...), custom_call_target="tpu_custom_call" | custom-call | flops 20000000000 | bytes 40000000 | tf_op jit(solution)/shard_map/pallas_call | solution.py:451
  83.6 38.4 %shard_map.306 = (bf16[1024,768]{1,0:T(8,128)(2,1)}, bf16[1024,768]{1,0:T(8,128)(2,1)}, bf16[2,768,768]{2,1,0:T(8,128)(2,1)}, bf16[2,768,768]{2,1,0:T(8,128)(2,1)}, f32[8,768]{1,0:T(8,128)}) custom-call(s32[8]{0:T(128)} %len_ref.1, f32[1024,768]{1,0:T(8,128)} %get-tuple-element.61.hid_ref, bf16[2048,768]{1,0:T(8,128)(2,1)} %cot_ref.1, ...), custom_call_target="tpu_custom_call" | custom-call | flops 24000000000 | bytes 30000000 | tf_op jit(solution)/shard_map/pallas_call | solution.py:539
  122.0 72.2 %shard_map.307 = (bf16[2048,768]{1,0:T(8,128)(2,1)}, bf16[4096,768]{1,0:T(8,128)(2,1)}, f32[96,768]{1,0:T(8,128)}, f32[96,768]{1,0:T(8,128)}, f32[96,768]{1,0:T(...) custom-call(bf16[4096,768]{1,0:T(8,128)(2,1)} %refs_0_.3, bf16[4,768,768]{2,1,0:T(8,128)(2,1)} %bitcast.9, ...), custom_call_target="tpu_custom_call" | custom-call | flops 40000000000 | bytes 30000000 | tf_op jit(solution)/shard_map/pallas_call | solution.py:994
  194.2 9.3 %shard_map.308 = (bf16[2048,768]{1,0:T(8,128)(2,1)}, bf16[4096,768]{1,0:T(8,128)(2,1)}, f32[96,192]{1,0:T(8,128)}, f32[96,192]{1,0:T(8,128)}, f32[96,192]{1,0:T(...) custom-call(f32[96,768]{1,0:T(8,128)} %get-tuple-element.71.a_ref, ...), custom_call_target="tpu_custom_call" | custom-call | tf_op jit(solution)/shard_map/pallas_call | solution.py:1055

commit v5 on v4

--- a/solution.py
+++ b/solution.py
@@ -601,7 +601,7 @@
 
 
 class Scatter:
-    PARTS = 2
+    PARTS = 3
 
     def __init__(self, net, mine, other, bufs):
         self.net, self.mine, self.other = net, mine, other
@@ -636,12 +636,18 @@
         for i in range(self.PARTS):
             self.over_x(i).start()
 
-    def x_to_z(self, i):
+    def x_sum(self, i):
         self.over_x(i).wait_recv()
         rows = self.part(i)
         self.t2[:, rows] += self.t1[:, self.net.lo, rows]
+
+    def start_z(self, i):
         for s in range(1, self.net.n_hi):
             self.over_z(i, s).start()
+
+    def x_to_z(self, i):
+        self.x_sum(i)
+        self.start_z(i)
 
     def finish(self, out):
         for i in range(self.PARTS):
@@ -652,10 +658,13 @@
                 total += self.r3[s, rows].astype(F32)
             out[rows, :] = total
 
-    def sent(self):
+    def sent_x(self):
         self.over_core().wait_send()
         for i in range(self.PARTS):
             self.over_x(i).wait_send()
+
+    def sent_z(self):
+        for i in range(self.PARTS):
             for s in range(1, self.net.n_hi):
                 self.over_z(i, s).wait_send()
 
@@ -732,7 +741,14 @@
     qd2 = jnp.concatenate([qds[2][0:64], jnp.zeros_like(qds[2][0:64])], axis=0).T
     qd = jnp.concatenate([qd01, qd2], axis=1).astype(BF16)
     qd_ref[...] = qd
-    return dot_nt(kvd[...], a_of(slice(0, 384))), dot_nt(qd, a_of(slice(384, 640))) * 0.125
+
+
+def backward_place(step, n_seq):
+    core = my_core()
+    own = jnp.where(step < n_seq, 1 - core, core)
+    rest = 2 + lax.rem(step, 2)
+    first = step < 2 * n_seq
+    return jnp.where(first, own, rest), jnp.where(first, lax.rem(step, n_seq), lax.rem(step, 2 * n_seq) // 2)
 
 
 def backward_kernel(n_seq, length, n_dp, comm, *refs):
@@ -741,7 +757,7 @@
     step = pl.program_id(0)
     n_own = 2 * n_seq
     own = step < n_own
-    b, g = lax.rem(step, n_own) // 2, 2 * (step // n_own) + lax.rem(step, 2)
+    g, b = backward_place(step, n_seq)
     x_any, a_ref, kv_ref, q_ref, p_ref, ctx_any, ag_ref, pb_any = refs[:8]
     refs = refs[8:]
     if comm:
@@ -751,8 +767,8 @@
     else:
         tok_out, ga_ref, sm_ref = refs[:3]
         refs = refs[3:]
-    kvd, qd_all, tacc, tok, pool, x_ref, ctx_ref, pb_ref, fetch = refs[:9]
-    refs = refs[9:]
+    kvd, qd_all, tacc, tok, pool, kvd_rest, qd_rest, x_ref, ctx_ref, pb_ref, fetch = refs[:11]
+    refs = refs[11:]
     core = my_core()
     n_tok = n_seq * length
     late = (
@@ -810,13 +826,16 @@
 
         at(1, vec.core_to_x)
         at(2, mine[0].wait, up.core_to_x, mine[1].wait, down.core_to_x)
-        at(4, lambda: up.x_to_z(0))
-        at(6, lambda: up.x_to_z(1), vec.x_to_z)
-        at(7, lambda: down.x_to_z(0))
-        at(8, att.over_core().start, small.over_core().start)
-        at(9, small.core_to_x, lambda: down.x_to_z(1), att.core_to_x)
-        at(13, lambda: att.x_to_z(0))
-        at(15, small.x_to_z)
+        at(4, lambda: up.x_to_z(0), vec.x_to_z, att.over_core().start, small.over_core().start)
+        at(5, lambda: up.x_to_z(1))
+        at(6, lambda: up.x_to_z(2))
+        at(8, small.core_to_x, att.core_to_x, lambda: down.x_to_z(0))
+        at(9, lambda: down.x_to_z(1))
+        at(10, lambda: down.x_to_z(2))
+        at(12, lambda: att.x_to_z(0), small.x_to_z)
+        at(14, lambda: att.x_to_z(1))
+        at(15, lambda: att.x_to_z(2))
+
     @pl.when(step == 0)
     def _():
         for copy in late:
@@ -824,16 +843,6 @@
 
     krows = pl.ds(pl.multiple_of(b * length, length), length)
     qrows = pl.ds(pl.multiple_of(b * half, half), half)
-
-    def run(is_own):
-        gg = lax.rem(g, 2) if is_own else 0
-        kv_at, q_at = (kvd.at[gg, krows], qd_all.at[gg, qrows]) if is_own else (kvd.at[0, krows], qd_all.at[0, qrows])
-        return backward_step(
-            half,
-            is_own,
-            (kv_ref, q_ref, p_ref, ag_ref[qrows, :], lambda lanes: a_ref[g, :, lanes],
-             tacc.at[gg] if is_own else None, kv_at, q_at),
-        )
 
     @pl.when(own)
     def _():
@@ -841,19 +850,14 @@
         def _():
             tacc[g] = jnp.zeros_like(tacc[g])
 
-        tok_add, pool_add = run(True)
-
-        @pl.when(g == 0)
-        def _():
-            tok[krows, :] = tok_add
-            pool[qrows, :] = pool_add
-
-        @pl.when(g == 1)
-        def _():
-            tok[krows, :] += tok_add
-            pool[qrows, :] += pool_add
-
-        @pl.when(step == n_own - 2)
+        backward_step(
+            half,
+            True,
+            (kv_ref, q_ref, p_ref, ag_ref[qrows, :], lambda lanes: a_ref[g, :, lanes], tacc.at[g],
+             kvd.at[g, krows], qd_all.at[g, qrows]),
+        )
+
+        @pl.when(step == n_seq - 1)
         def _():
             for copy in late:
                 copy.wait()
@@ -885,17 +889,24 @@
 
     @pl.when(jnp.logical_not(own))
     def _():
-        tok_add, pool_add = run(False)
+        backward_step(
+            half,
+            False,
+            (kv_ref, q_ref, p_ref, ag_ref[qrows, :], lambda lanes: a_ref[g, :, lanes], None, kvd_rest, qd_rest),
+        )
+        h = g - 2
+        tok_add = dot_nt(kvd_rest[...], a_ref[g, :, 0:384]) + dot_nt(kvd[h, krows], a_ref[h, :, 0:384])
+        pool_add = dot_nt(qd_rest[...], a_ref[g, :, 384:640]) + dot_nt(qd_all[h, qrows], a_ref[h, :, 384:640])
 
         @pl.when(g == 2)
         def _():
-            tok[krows, :] += tok_add
-            pool[qrows, :] += pool_add
+            tok[...] = tok_add
+            pool[...] = pool_add
 
         @pl.when(g == 3)
         def _():
-            total = (pool[qrows, :] + pool_add + ag_ref[qrows, :].astype(F32)).astype(BF16)
-            final = (tok[krows, :] + tok_add + dot_tn(pool_matrix(half, length), total)).astype(BF16)
+            total = ((pool[...] + pool_add) * 0.125 + ag_ref[qrows, :].astype(F32)).astype(BF16)
+            final = (tok[...] + tok_add + dot_tn(pool_matrix(half, length), total)).astype(BF16)
             if comm:
                 stage[b] = final
                 for copy in tok_copies(b):
@@ -908,13 +919,13 @@
         @pl.when(last)
         def _():
             vec.finish(gv_out)
-            att.x_to_z(1)
             up.finish(up_out)
             down.finish(down_out)
             small.finish(sm_out)
             att.finish(a_out)
             for each in (up, down, att):
-                each.sent()
+                each.sent_x()
+                each.sent_z()
             for copy in o_copies:
                 copy.wait()
             for i in range(n_seq):
@@ -942,7 +953,7 @@
     n_hi, rows = n_dp // 2, width // n_dp
 
     def place(n):
-        return 2 * (n // n_own) + lax.rem(n, 2), lax.rem(n, n_own) // 2
+        return backward_place(n, n_seq)
 
     in_specs = [
         ANY,
@@ -957,8 +968,8 @@
     args = [tokens, a4, kv, q, p, ctx, ag, pb]
     scratch = [
         pltpu.VMEM((2, n_tok, 384), BF16), pltpu.VMEM((2, n_pool, 256), BF16), pltpu.VMEM((2, 3, length, half), F32),
-        pltpu.VMEM((n_tok, width), F32), pltpu.VMEM((n_pool, width), F32),
-        pltpu.VMEM((n_tok, width), BF16), pltpu.VMEM((2, n_pool, 256), BF16), pltpu.VMEM((n_pool, width), BF16),
+        pltpu.VMEM((length, width), F32), pltpu.VMEM((half, width), F32), pltpu.VMEM((length, 384), BF16),
+        pltpu.VMEM((half, 256), BF16), pltpu.VMEM((n_tok, width), BF16), pltpu.VMEM((2, n_pool, 256), BF16), pltpu.VMEM((n_pool, width), BF16),
         pltpu.SemaphoreType.DMA((5,)),
     ]
     params = {"vmem_limit_bytes": VMEM_LIMIT}

time: 204 us -> 198 us (0.971)
  Pallas kernels: 203 us -> 197 us
    pallas_call x1, Pallas kernels: 72.2 us -> 66.6 us  [attention_backward(): pl.pallas_call(functools.partial(backward_kernel, n_seq, length, n_dp, co...]
where the time goes in v5:
time: 198 us
  Pallas kernels  197 us (99%)
    pallas_call x1, Pallas kernels, attention_forward(): pl.pallas_call(functools.partial(attention_kernel, n_seq, length, n_dp, c...  82.9 us
    pallas_call x1, Pallas kernels, attention_backward(): pl.pallas_call(functools.partial(backward_kernel, n_seq, length, n_dp, co...  66.6 us
    pallas_call x1, Pallas kernels, ffn(): pl.pallas_call(functools.partial(ffn_kernel, n_seq, half), out_shape=(jax...  38.4 us
    pallas_call x1, Pallas kernels, finish(): pl.pallas_call(functools.partial(finish_kernel, tuple(cuts)), out_shape=[...  9.3 us

profile of v5, /device:TPU:0, one launch (start us, length us, event | category | flops | bytes accessed | tf_op | source)
XLA Modules:
  0.0 198.1 jit_solution(14467473246138986053)
XLA Ops:
  0.7 82.9 %shard_map.305 = (bf16[4,2048,384]{2,1,0:T(8,128)(2,1)}, bf16[4,1024,256]{2,1,0:T(8,128)(2,1)}, bf16[4,4,3,512,256]{4,3,2,1,0:T(8,128)(2,1)}, bf16[4,1024,256]{2...) custom-call(s32[8]{0:T(128)} %len_ref.1, ...), custom_call_target="tpu_custom_call" | custom-call | flops 20000000000 | bytes 40000000 | tf_op jit(solution)/shard_map/pallas_call | solution.py:451
  83.6 38.4 %shard_map.306 = (bf16[1024,768]{1,0:T(8,128)(2,1)}, bf16[1024,768]{1,0:T(8,128)(2,1)}, bf16[2,768,768]{2,1,0:T(8,128)(2,1)}, bf16[2,768,768]{2,1,0:T(8,128)(2,1)}, f32[8,768]{1,0:T(8,128)}) custom-call(s32[8]{0:T(128)} %len_ref.1, f32[1024,768]{1,0:T(8,128)} %get-tuple-element.61.hid_ref, bf16[2048,768]{1,0:T(8,128)(2,1)} %cot_ref.1, ...), custom_call_target="tpu_custom_call" | custom-call | flops 24000000000 | bytes 30000000 | tf_op jit(solution)/shard_map/pallas_call | solution.py:539
  122.0 66.6 %shard_map.307 = (bf16[2048,768]{1,0:T(8,128)(2,1)}, bf16[4096,768]{1,0:T(8,128)(2,1)}, f32[96,768]{1,0:T(8,128)}, f32[96,768]{1,0:T(8,128)}, f32[96,768]{1,0:T(...) custom-call(bf16[4096,768]{1,0:T(8,128)(2,1)} %refs_0_.3, bf16[4,768,768]{2,1,0:T(8,128)(2,1)} %bitcast.9, ...), custom_call_target="tpu_custom_call" | custom-call | flops 40000000000 | bytes 30000000 | tf_op jit(solution)/shard_map/pallas_call | solution.py:1005
  188.6 9.3 %shard_map.308 = (bf16[2048,768]{1,0:T(8,128)(2,1)}, bf16[4096,768]{1,0:T(8,128)(2,1)}, f32[96,192]{1,0:T(8,128)}, f32[96,192]{1,0:T(8,128)}, f32[96,192]{1,0:T(...) custom-call(f32[96,768]{1,0:T(8,128)} %get-tuple-element.71.a_ref, ...), custom_call_target="tpu_custom_call" | custom-call | tf_op jit(solution)/shard_map/pallas_call | solution.py:1066

commit v6 on v5

--- a/solution.py
+++ b/solution.py
@@ -292,8 +292,8 @@
 
         for d in range(1, n_hi):
             at((1, 2, 3)[d - 1], net.spread, 1, d)
-            at((5, 6, 7)[d - 1], net.spread, 2, d)
-        at(3, net.start, 2)
+            at((4, 5, 6)[d - 1], net.spread, 2, d)
+        at(2, net.start, 2)
         at(4, net.late, 0)
         for d in range(n_hi):
             at(4, net.diagonal, 0, d)
@@ -356,14 +356,15 @@
         (jnp.where(low, zero, q01), 0, 128),
         (q[:, 128:256], 256, 256),
     )
-    contexts = []
-    for h, (qh, k_at, v_at) in enumerate(heads):
-        s = dot_nt(kv_ref[0, :, k_at : k_at + 128], qh) + bias[h]
-        s = jnp.where(valid, s, -1e30)
+    raw = [dot_nt(kv_ref[0, :, k_at : k_at + 128], qh) for qh, k_at, _ in heads]
+    probs = []
+    for h in range(3):
+        s = jnp.where(valid, raw[h] + bias[h], -1e30)
         e = jnp.exp(s - jnp.max(s, axis=0, keepdims=True))
         p = (e * (1.0 / jnp.sum(e, axis=0, keepdims=True))).astype(BF16)
         p_ref[0, 0, h] = p
-        contexts.append(dot_tn(kv_ref[0, :, v_at : v_at + 128], p))
+        probs.append(p)
+    contexts = [dot_tn(kv_ref[0, :, v_at : v_at + 128], p) for (_, _, v_at), p in zip(heads, probs)]
     c0, c1, c2 = contexts
     ctx01 = jnp.concatenate([c0[0:64], c1[64:128]], axis=0).T
     ctx2 = jnp.concatenate([jnp.zeros_like(c2[0:64]), c2[64:128]], axis=0).T
@@ -722,18 +723,18 @@
         (jnp.where(low, zero, q01), jnp.where(low, zero, cg01), 0, 128),
         (q_ref[0, :, 128:256], jnp.where(low, zero, cg2), 256, 256),
     )
-    kds, vds, qds = [], [], []
-    for h, (q, g, k_at, v_at) in enumerate(heads):
-        pb16 = p_ref[0, 0, h]
-        p = pb16.astype(F32)
-        dp = dot_nt(kv_ref[0, :, v_at : v_at + 128], g)
-        row = jnp.sum(p * dp, axis=0, keepdims=True)
-        sg = (p * (dp - row)).astype(BF16)
+    raw = [dot_nt(kv_ref[0, :, v_at : v_at + 128], g) for _, g, _, v_at in heads]
+    vds = [dot_nn(p_ref[0, 0, h], head[1]) for h, head in enumerate(heads)]
+    grads = []
+    for h in range(3):
+        p = p_ref[0, 0, h].astype(F32)
+        row = jnp.sum(p * raw[h], axis=0, keepdims=True)
+        sg = (p * (raw[h] - row)).astype(BF16)
         if own:
             tacc[h] += sg.astype(F32)
-        kds.append(dot_nn(sg, q))
-        vds.append(dot_nn(pb16, g))
-        qds.append(dot_tn(kv_ref[0, :, k_at : k_at + 128], sg))
+        grads.append(sg)
+    kds = [dot_nn(sg, head[0]) for sg, head in zip(grads, heads)]
+    qds = [dot_tn(kv_ref[0, :, head[2] : head[2] + 128], sg) for sg, head in zip(grads, heads)]
     kvd[:, 0:128] = (kds[0] + kds[1]).astype(BF16)
     kvd[:, 128:256] = (vds[0] + vds[1]).astype(BF16)
     kvd[:, 256:384] = (kds[2] + vds[2]).astype(BF16)
@@ -758,17 +759,17 @@
     n_own = 2 * n_seq
     own = step < n_own
     g, b = backward_place(step, n_seq)
-    x_any, a_ref, kv_ref, q_ref, p_ref, ctx_any, ag_ref, pb_any = refs[:8]
+    x_any, a_any, kv_ref, q_ref, p_ref, ctx_any, ag_ref, pb_any = refs[:8]
     refs = refs[8:]
     if comm:
-        gu_any, gd_any, gv_ref, half_ref = refs[:4]
+        gu_any, gd_any, gv_ref, half_any = refs[:4]
         out_any, tok_any, up_out, down_out, a_out, gv_out, sm_out = refs[4:11]
         refs = refs[11:]
     else:
         tok_out, ga_ref, sm_ref = refs[:3]
         refs = refs[3:]
-    kvd, qd_all, tacc, tok, pool, kvd_rest, qd_rest, x_ref, ctx_ref, pb_ref, fetch = refs[:11]
-    refs = refs[11:]
+    kvd, qd_all, tacc, tok, pool, kvd_rest, qd_rest, x_ref, ctx_ref, pb_ref, a_ref, fetch = refs[:12]
+    refs = refs[12:]
     core = my_core()
     n_tok = n_seq * length
     late = (
@@ -776,6 +777,15 @@
         pltpu.make_async_copy(ctx_any.at[0:2], ctx_ref, fetch.at[1]),
         pltpu.make_async_copy(pb_any, pb_ref, fetch.at[2]),
     )
+    a_copies = [
+        pltpu.make_async_copy(a_any.at[pl.ds(i, 2)], a_ref.at[pl.ds(i, 2)], fetch.at[5 + i // 2]) for i in (0, 2)
+    ]
+
+    @pl.when(step == 0)
+    def _():
+        for copy in a_copies:
+            copy.start()
+
     last = step == 2 * n_own - 1
 
     def at(n, *actions):
@@ -785,7 +795,8 @@
                 action()
 
     if comm:
-        ga_ref, sm_ref, gu_mine, gd_mine, stage = refs[:5]
+        ga_ref, sm_ref, gu_mine, gd_mine, stage, half_ref = refs[:6]
+        refs = refs[1:]
         net = Net(n_hi)
         other = 1 - core
         up = Scatter(net, gu_mine, gu_any.at[other], refs[5:13])
@@ -803,6 +814,7 @@
         mine = (
             pltpu.make_async_copy(gu_any.at[core], gu_mine, fetch.at[3]),
             pltpu.make_async_copy(gd_any.at[core], gd_mine, fetch.at[4]),
+            pltpu.make_async_copy(half_any, half_ref, fetch.at[7]),
         )
 
         def tok_copies(i):
@@ -821,25 +833,26 @@
             vec.over_core().start()
             up.over_core().start()
             down.over_core().start()
-            for copy in o_copies:
-                copy.start()
-
-        at(1, vec.core_to_x)
+
+        at(1, vec.core_to_x, mine[2].wait, o_copies[0].start, o_copies[1].start)
         at(2, mine[0].wait, up.core_to_x, mine[1].wait, down.core_to_x)
-        at(4, lambda: up.x_to_z(0), vec.x_to_z, att.over_core().start, small.over_core().start)
+        at(4, att.over_core().start, small.over_core().start, vec.x_to_z, lambda: up.x_to_z(0))
         at(5, lambda: up.x_to_z(1))
         at(6, lambda: up.x_to_z(2))
-        at(8, small.core_to_x, att.core_to_x, lambda: down.x_to_z(0))
-        at(9, lambda: down.x_to_z(1))
-        at(10, lambda: down.x_to_z(2))
-        at(12, lambda: att.x_to_z(0), small.x_to_z)
-        at(14, lambda: att.x_to_z(1))
+        at(7, lambda: down.x_to_z(0))
+        at(8, small.core_to_x, att.core_to_x, lambda: down.x_to_z(1))
+        at(9, lambda: down.x_to_z(2))
+        at(11, lambda: att.x_to_z(0), small.x_to_z)
+        at(13, lambda: att.x_to_z(1))
         at(15, lambda: att.x_to_z(2))
 
     @pl.when(step == 0)
     def _():
         for copy in late:
             copy.start()
+        a_copies[0].wait()
+
+    pl.when(step == n_own)(a_copies[1].wait)
 
     krows = pl.ds(pl.multiple_of(b * length, length), length)
     qrows = pl.ds(pl.multiple_of(b * half, half), half)
@@ -957,7 +970,7 @@
 
     in_specs = [
         ANY,
-        fixed((4, width, 768)),
+        ANY,
         pl.BlockSpec((1, length, 384), lambda n: place(n) + (0,)),
         pl.BlockSpec((1, half, 256), lambda n: place(n) + (0,)),
         pl.BlockSpec((1, 1, 3, length, half), lambda n: place(n) + (0, 0, 0)),
@@ -970,13 +983,13 @@
         pltpu.VMEM((2, n_tok, 384), BF16), pltpu.VMEM((2, n_pool, 256), BF16), pltpu.VMEM((2, 3, length, half), F32),
         pltpu.VMEM((length, width), F32), pltpu.VMEM((half, width), F32), pltpu.VMEM((length, 384), BF16),
         pltpu.VMEM((half, 256), BF16), pltpu.VMEM((n_tok, width), BF16), pltpu.VMEM((2, n_pool, 256), BF16), pltpu.VMEM((n_pool, width), BF16),
-        pltpu.SemaphoreType.DMA((5,)),
+        pltpu.VMEM((4, width, 768), BF16), pltpu.SemaphoreType.DMA((8,)),
     ]
     params = {"vmem_limit_bytes": VMEM_LIMIT}
     small = (8, 2 * length)
     if comm:
         split = (2, n_hi, 2, rows, width)
-        in_specs += [ANY, ANY, fixed(gv.shape), fixed(out_half.shape)]
+        in_specs += [ANY, ANY, fixed(gv.shape), ANY]
         args += [gu.reshape(split), gd.reshape(split), gv, out_half]
         shares = [jax.ShapeDtypeStruct((rows, width), F32)] * 3
         out_shape = [
@@ -987,6 +1000,7 @@
         scratch += [
             pltpu.VMEM(split, BF16), pltpu.VMEM((2,) + small, F32), pltpu.VMEM(split[1:], BF16),
             pltpu.VMEM(split[1:], BF16), pltpu.VMEM((n_seq, length, width), BF16),
+            pltpu.VMEM(out_half.shape, BF16),
         ]
         for _ in range(3):
             scratch += Scatter.scratch(n_hi, rows, width)

time: 198 us -> 191 us (0.965)
  Pallas kernels: 197 us -> 190 us
    pallas_call x1, Pallas kernels: 66.6 us -> 62.3 us  [attention_backward(): pl.pallas_call(functools.partial(backward_kernel, n_seq, length, n_dp, co...]
    pallas_call x1, Pallas kernels: 82.9 us -> 80.4 us  [attention_forward(): pl.pallas_call(functools.partial(attention_kernel, n_seq, length, n_dp, c...]
where the time goes in v6:
time: 191 us
  Pallas kernels  190 us (99%)
    pallas_call x1, Pallas kernels, attention_forward(): pl.pallas_call(functools.partial(attention_kernel, n_seq, length, n_dp, c...  80.4 us
    pallas_call x1, Pallas kernels, attention_backward(): pl.pallas_call(functools.partial(backward_kernel, n_seq, length, n_dp, co...  62.3 us
    pallas_call x1, Pallas kernels, ffn(): pl.pallas_call(functools.partial(ffn_kernel, n_seq, half), out_shape=(jax...  38.4 us
    pallas_call x1, Pallas kernels, finish(): pl.pallas_call(functools.partial(finish_kernel, tuple(cuts)), out_shape=[...  9.3 us

profile of v6, /device:TPU:0, one launch (start us, length us, event | category | flops | bytes accessed | tf_op | source)
XLA Modules:
  0.0 191.2 jit_solution(15148312928798093906)
XLA Ops:
  0.7 80.4 %shard_map.305 = (bf16[4,2048,384]{2,1,0:T(8,128)(2,1)}, bf16[4,1024,256]{2,1,0:T(8,128)(2,1)}, bf16[4,4,3,512,256]{4,3,2,1,0:T(8,128)(2,1)}, bf16[4,1024,256]{2...) custom-call(s32[8]{0:T(128)} %len_ref.1, ...), custom_call_target="tpu_custom_call" | custom-call | flops 20000000000 | bytes 40000000 | tf_op jit(solution)/shard_map/pallas_call | solution.py:452
  81.0 38.4 %shard_map.306 = (bf16[1024,768]{1,0:T(8,128)(2,1)}, bf16[1024,768]{1,0:T(8,128)(2,1)}, bf16[2,768,768]{2,1,0:T(8,128)(2,1)}, bf16[2,768,768]{2,1,0:T(8,128)(2,1)}, f32[8,768]{1,0:T(8,128)}) custom-call(s32[8]{0:T(128)} %len_ref.1, f32[1024,768]{1,0:T(8,128)} %get-tuple-element.61.hid_ref, bf16[2048,768]{1,0:T(8,128)(2,1)} %cot_ref.1, ...), custom_call_target="tpu_custom_call" | custom-call | flops 24000000000 | bytes 30000000 | tf_op jit(solution)/shard_map/pallas_call | solution.py:540
  119.4 62.3 %shard_map.307 = (bf16[2048,768]{1,0:T(8,128)(2,1)}, bf16[4096,768]{1,0:T(8,128)(2,1)}, f32[96,768]{1,0:T(8,128)}, f32[96,768]{1,0:T(8,128)}, f32[96,768]{1,0:T(...) custom-call(bf16[4096,768]{1,0:T(8,128)(2,1)} %refs_0_.3, bf16[4,768,768]{2,1,0:T(8,128)(2,1)} %bitcast.9, ...), custom_call_target="tpu_custom_call" | custom-call | flops 40000000000 | bytes 30000000 | tf_op jit(solution)/shard_map/pallas_call | solution.py:1019
  181.7 9.3 %shard_map.308 = (bf16[2048,768]{1,0:T(8,128)(2,1)}, bf16[4096,768]{1,0:T(8,128)(2,1)}, f32[96,192]{1,0:T(8,128)}, f32[96,192]{1,0:T(8,128)}, f32[96,192]{1,0:T(...) custom-call(f32[96,768]{1,0:T(8,128)} %get-tuple-element.71.a_ref, ...), custom_call_target="tpu_custom_call" | custom-call | tf_op jit(solution)/shard_map/pallas_call | solution.py:1080

commit v7 on v6

--- a/solution.py
+++ b/solution.py
@@ -298,9 +298,9 @@
         for d in range(n_hi):
             at(4, net.diagonal, 0, d)
             at((6, 7, 8, 9)[d], net.pass_on, 1, d)
-            at((10, 10, 11, 11)[d], net.pass_on, 2, d, 0)
-            at((11, 12, 13, 14)[d], net.pass_on, 2, d, 1)
-            at((11, 12, 13, 13)[d], lambda i: net.near(i, lambda s: net.diagonal(1, s)), d)
+            at((9, 9, 10, 10)[d], net.pass_on, 2, d, 0)
+            at((10, 11, 12, 13)[d], net.pass_on, 2, d, 1)
+            at((10, 11, 12, 13)[d], lambda i: net.near(i, lambda s: net.diagonal(1, s)), d)
         at(3, net.lines_y, 1)
         at(2 * n_seq, net.arrived, 0, (2, 3))
         for g in range(4):
@@ -540,7 +540,7 @@
     return pl.pallas_call(
         functools.partial(ffn_kernel, n_seq, half),
         out_shape=(
-            jax.ShapeDtypeStruct((n_seq * half, width), BF16),
+            jax.ShapeDtypeStruct((2 * n_seq * half, width), BF16),
             jax.ShapeDtypeStruct((n_seq * half, width), BF16),
             jax.ShapeDtypeStruct((2, width, 768), BF16),
             jax.ShapeDtypeStruct((2, width, 768), BF16),
@@ -557,7 +557,7 @@
         ]
         + [pl.BlockSpec((width,), lambda b: (0,), pipeline_mode=once)] * 5,
         out_specs=[
-            pl.BlockSpec((half, width), lambda b: (b, 0)),
+            pl.BlockSpec((half, width), lambda b: (my_core() * n_seq + b, 0)),
             pl.BlockSpec((half, width), lambda b: (b, 0)),
             pl.BlockSpec((2, width, 768), lambda b: (0, 0, 0), pipeline_mode=once),
             pl.BlockSpec((2, width, 768), lambda b: (0, 0, 0), pipeline_mode=once),
@@ -795,8 +795,7 @@
                 action()
 
     if comm:
-        ga_ref, sm_ref, gu_mine, gd_mine, stage, half_ref = refs[:6]
-        refs = refs[1:]
+        ga_ref, sm_ref, gu_mine, gd_mine, stage = refs[:5]
         net = Net(n_hi)
         other = 1 - core
         up = Scatter(net, gu_mine, gu_any.at[other], refs[5:13])
@@ -806,15 +805,12 @@
         small = SmallSum(net, sm_ref.at[core], sm_ref.at[other], refs[36:43])
         o_sem, t_sem = refs[43:45]
         n_rows = n_seq * half
-        there = out_any.at[pl.ds(pl.multiple_of(core * n_rows, n_rows), n_rows), :]
-        o_copies = (
-            pltpu.make_async_copy(half_ref, there, o_sem.at[0]),
-            net.remote(half_ref, there, o_sem.at[1], o_sem.at[2], net.to_c),
+        o_copy = net.remote(
+            half_any.at[pl.ds(pl.multiple_of(core * n_rows, n_rows), n_rows), :], out_any, o_sem.at[0], o_sem.at[1], net.to_c
         )
         mine = (
             pltpu.make_async_copy(gu_any.at[core], gu_mine, fetch.at[3]),
             pltpu.make_async_copy(gd_any.at[core], gd_mine, fetch.at[4]),
-            pltpu.make_async_copy(half_any, half_ref, fetch.at[7]),
         )
 
         def tok_copies(i):
@@ -834,7 +830,8 @@
             up.over_core().start()
             down.over_core().start()
 
-        at(1, vec.core_to_x, mine[2].wait, o_copies[0].start, o_copies[1].start)
+        at(3, o_copy.start)
+        at(1, vec.core_to_x)
         at(2, mine[0].wait, up.core_to_x, mine[1].wait, down.core_to_x)
         at(4, att.over_core().start, small.over_core().start, vec.x_to_z, lambda: up.x_to_z(0))
         at(5, lambda: up.x_to_z(1))
@@ -939,8 +936,7 @@
             for each in (up, down, att):
                 each.sent_x()
                 each.sent_z()
-            for copy in o_copies:
-                copy.wait()
+            o_copy.wait()
             for i in range(n_seq):
                 for copy in tok_copies(i):
                     copy.wait()
@@ -983,7 +979,7 @@
         pltpu.VMEM((2, n_tok, 384), BF16), pltpu.VMEM((2, n_pool, 256), BF16), pltpu.VMEM((2, 3, length, half), F32),
         pltpu.VMEM((length, width), F32), pltpu.VMEM((half, width), F32), pltpu.VMEM((length, 384), BF16),
         pltpu.VMEM((half, 256), BF16), pltpu.VMEM((n_tok, width), BF16), pltpu.VMEM((2, n_pool, 256), BF16), pltpu.VMEM((n_pool, width), BF16),
-        pltpu.VMEM((4, width, 768), BF16), pltpu.SemaphoreType.DMA((8,)),
+        pltpu.VMEM((4, width, 768), BF16), pltpu.SemaphoreType.DMA((7,)),
     ]
     params = {"vmem_limit_bytes": VMEM_LIMIT}
     small = (8, 2 * length)
@@ -993,19 +989,18 @@
         args += [gu.reshape(split), gd.reshape(split), gv, out_half]
         shares = [jax.ShapeDtypeStruct((rows, width), F32)] * 3
         out_shape = [
-            jax.ShapeDtypeStruct((2 * n_pool, width), BF16), jax.ShapeDtypeStruct((2 * n_tok, width), BF16), *shares,
+            jax.ShapeDtypeStruct((n_pool, width), BF16), jax.ShapeDtypeStruct((2 * n_tok, width), BF16), *shares,
             jax.ShapeDtypeStruct(gv.shape, F32), jax.ShapeDtypeStruct(small, F32),
         ]
         out_specs = [ANY, ANY] + [fixed((rows, width))] * 3 + [fixed(gv.shape), fixed(small)]
         scratch += [
             pltpu.VMEM(split, BF16), pltpu.VMEM((2,) + small, F32), pltpu.VMEM(split[1:], BF16),
             pltpu.VMEM(split[1:], BF16), pltpu.VMEM((n_seq, length, width), BF16),
-            pltpu.VMEM(out_half.shape, BF16),
         ]
         for _ in range(3):
             scratch += Scatter.scratch(n_hi, rows, width)
         scratch += SmallSum.scratch(n_hi, gv.shape) + SmallSum.scratch(n_hi, small)
-        scratch += [pltpu.SemaphoreType.DMA((3,)), pltpu.SemaphoreType.DMA((3, n_seq))]
+        scratch += [pltpu.SemaphoreType.DMA((2,)), pltpu.SemaphoreType.DMA((3, n_seq))]
         params.update(collective_id=1, has_side_effects=True)
     else:
         out_shape = [
@@ -1028,24 +1023,24 @@
     )(*args)
 
 
-def finish_kernel(big, a_ref, up_ref, down_ref, gv_ref, sm_ref, *refs):
-    n = len(big)
-    moves = [
-        [
-            (
-                pltpu.make_async_copy(src.at[pl.ds(i * chunk, chunk)], buf.at[i], sem.at[0, i]),
-                pltpu.make_async_copy(buf.at[i], dst.at[pl.ds(i * chunk, chunk)], sem.at[1, i]),
-            )
-            for i in range(count)
-        ]
-        for (count, chunk), src, dst, buf, sem in zip(
-            big, refs[:n], refs[n : 2 * n], refs[2 * n + 15 :: 2], refs[2 * n + 16 :: 2]
-        )
-    ]
-    moves = sum(moves, [])
+def finish_kernel(n_out, n_tok, chunk, a_ref, up_ref, down_ref, gv_ref, sm_ref, half_any, other_any, tok_any, *refs):
+    out_any, tok_out = refs[:2]
+    query, key, value, out, up, down, table, vbias, ubias, *vectors = refs[2:17]
+    buf, sem = refs[17:]
+    first = (1 - my_core()) * n_out * chunk
+    moves = []
+    for i in range(n_tok + n_out):
+        if i < n_tok:
+            src = tok_any.at[pl.ds(i * chunk, chunk)]
+            dst = tok_out.at[pl.ds(i * chunk, chunk)]
+        else:
+            at = (i - n_tok) * chunk
+            src = other_any.at[pl.ds(at, chunk)]
+            dst = out_any.at[pl.ds(pl.multiple_of(first + at, chunk), chunk)]
+        come = pltpu.make_async_copy(src, buf.at[i], sem.at[0, i])
+        moves.append((come, pltpu.make_async_copy(buf.at[i], dst, sem.at[1, i])))
     for come, _ in moves:
         come.start()
-    query, key, value, out, up, down, table, vbias, ubias, *vectors = refs[2 * n : 2 * n + 15]
     query[...] = a_ref[:, 384:576]
     key[:, 0:128] = a_ref[:, 0:128]
     key[:, 128:192] = a_ref[:, 256:320]
@@ -1068,24 +1063,23 @@
         go.wait()
 
 
-def finish(big, a_sum, up_sum, down_sum, gv, sm, length):
+def finish(half_done, other, tok, a_sum, up_sum, down_sum, gv, sm, length):
     rows, width = a_sum.shape
     shapes = [(rows, 192)] * 3 + [(192, rows), (rows, 768), (rows, 768), (3, 2 * length), (192,), (768,)] + [(width,)] * 6
-    cuts, scratch = [], []
-    for v in big:
-        count = v.shape[0] // 512
-        cuts.append((count, 512))
-        scratch += [pltpu.VMEM((count, 512, v.shape[1]), v.dtype), pltpu.SemaphoreType.DMA((2, count))]
+    n_out, n_tok = other.shape[0] // length, tok.shape[0] // length
     whole = pl.BlockSpec(memory_space=pltpu.VMEM)
     return pl.pallas_call(
-        functools.partial(finish_kernel, tuple(cuts)),
-        out_shape=[jax.ShapeDtypeStruct(v.shape, v.dtype) for v in big]
+        functools.partial(finish_kernel, n_out, n_tok, length),
+        out_shape=[jax.ShapeDtypeStruct(half_done.shape, BF16), jax.ShapeDtypeStruct(tok.shape, BF16)]
         + [jax.ShapeDtypeStruct(shape, F32) for shape in shapes],
-        in_specs=[whole] * 5 + [ANY] * len(big),
-        out_specs=[ANY] * len(big) + [whole] * len(shapes),
-        scratch_shapes=scratch,
+        in_specs=[whole] * 5 + [ANY] * 3,
+        out_specs=[ANY] * 2 + [whole] * len(shapes),
+        scratch_shapes=[
+            pltpu.VMEM((n_tok + n_out, length, width), BF16), pltpu.SemaphoreType.DMA((2, n_tok + n_out)),
+        ],
+        input_output_aliases={5: 0},
         compiler_params=pltpu.CompilerParams(vmem_limit_bytes=VMEM_LIMIT),
-    )(a_sum, up_sum, down_sum, gv, sm, *big)
+    )(a_sum, up_sum, down_sum, gv, sm, half_done, other, tok)
 
 
 def gather_plain(weights, length):
@@ -1140,7 +1134,7 @@
     out_half, ag, gu, gd, gv = ffn(lengths, hid, cotangent, u4, d4, s4, vectors, n_seq, half)
     sums = attention_backward(tokens, a4, kv, q, p, ctx, ag, pb, gu, gd, gv, out_half, n_seq, n_dp, comm)
     if comm:
-        output, tokens_grad, up_sum, down_sum, a_sum, gv, sm = sums
+        other_half, tokens_grad, up_sum, down_sum, a_sum, gv, sm = sums
     else:
         tok_half, ga, sm = sums
         up_sum, down_sum, a_sum = (sum_plain(v, n_dp) for v in (gu, gd, ga))
@@ -1157,8 +1151,8 @@
             got = over_core(part)
             return jnp.where(core == 0, jnp.concatenate([part, got]), jnp.concatenate([got, part]))
 
-        output, tokens_grad = join(out_half), join(tok_half)
-    output, tokens_grad, *cut = finish((output, tokens_grad), a_sum, up_sum, down_sum, gv, sm, length)
+        other_half, tokens_grad = over_core(lax.dynamic_slice_in_dim(out_half, core * n_seq * half, n_seq * half)), join(tok_half)
+    output, tokens_grad, *cut = finish(out_half, other_half, tokens_grad, a_sum, up_sum, down_sum, gv, sm, length)
     query_sum, key_sum, value_sum, outw_sum, up_sum, down_sum, table_sum, vbias, ubias = cut[:9]
     fgain, fshift, dbias, ngain, nshift, obias = cut[9:]
     return (

time: 191 us -> 191 us (level)
  no operation moved by 1% of the time
where the time goes in v7:
time: 191 us; the launch traced here: 190 us
  Pallas kernels  190 us (99%)
    pallas_call x1, Pallas kernels, attention_forward(): pl.pallas_call(functools.partial(attention_kernel, n_seq, length, n_dp, c...  80.3 us
    pallas_call x1, Pallas kernels, attention_backward(): pl.pallas_call(functools.partial(backward_kernel, n_seq, length, n_dp, co...  62.4 us
    pallas_call x1, Pallas kernels, ffn(): pl.pallas_call(functools.partial(ffn_kernel, n_seq, half), out_shape=(jax...  38.5 us
    pallas_call x1, Pallas kernels, finish(): pl.pallas_call(functools.partial(finish_kernel, n_out, n_tok, length), ou...  8.44 us

profile of v7, /device:TPU:0, one launch (start us, length us, event | category | flops | bytes accessed | tf_op | source)
XLA Modules:
  0.0 190.4 jit_solution(9798680965685190489)
XLA Ops:
  0.7 80.3 %shard_map.305 = (bf16[4,2048,384]{2,1,0:T(8,128)(2,1)}, bf16[4,1024,256]{2,1,0:T(8,128)(2,1)}, bf16[4,4,3,512,256]{4,3,2,1,0:T(8,128)(2,1)}, bf16[4,1024,256]{2...) custom-call(s32[8]{0:T(128)} %len_ref.1, ...), custom_call_target="tpu_custom_call" | custom-call | flops 20000000000 | bytes 40000000 | tf_op jit(solution)/shard_map/pallas_call | solution.py:452
  80.9 38.5 %shard_map.306 = (bf16[2048,768]{1,0:T(8,128)(2,1)}, bf16[1024,768]{1,0:T(8,128)(2,1)}, bf16[2,768,768]{2,1,0:T(8,128)(2,1)}, bf16[2,768,768]{2,1,0:T(8,128)(2,1)}, f32[8,768]{1,0:T(8,128)}) custom-call(s32[8]{0:T(128)} %len_ref.1, f32[1024,768]{1,0:T(8,128)} %get-tuple-element.61.hid_ref, bf16[2048,768]{1,0:T(8,128)(2,1)} %cot_ref.1, ...), custom_call_target="tpu_custom_call" | custom-call | flops 24000000000 | bytes 30000000 | tf_op jit(solution)/shard_map/pallas_call | solution.py:540
  119.4 62.4 %shard_map.307 = (bf16[1024,768]{1,0:T(8,128)(2,1)}, bf16[4096,768]{1,0:T(8,128)(2,1)}, f32[96,768]{1,0:T(8,128)}, f32[96,768]{1,0:T(8,128)}, f32[96,768]{1,0:T(...) custom-call(bf16[4096,768]{1,0:T(8,128)(2,1)} %refs_0_.3, bf16[4,768,768]{2,1,0:T(8,128)(2,1)} %bitcast.9, ...), custom_call_target="tpu_custom_call" | custom-call | flops 40000000000 | bytes 30000000 | tf_op jit(solution)/shard_map/pallas_call | solution.py:1014
  181.8 8.4 %shard_map.308 = (bf16[2048,768]{1,0:T(8,128)(2,1)}, bf16[4096,768]{1,0:T(8,128)(2,1)}, f32[96,192]{1,0:T(8,128)}, f32[96,192]{1,0:T(8,128)}, f32[96,192]{1,0:T(...) custom-call(f32[96,768]{1,0:T(8,128)} %get-tuple-element.71.a_ref, ...), custom_call_target="tpu_custom_call", output_to_operand_aliasing={{0}: (5, {})} | custom-call | tf_op jit(solution)/shard_map/pallas_call | solution.py:1071

commit v8 on v7

--- a/solution.py
+++ b/solution.py
@@ -237,10 +237,16 @@
     n_tok = n_seq * length
     x_copy = pltpu.make_async_copy(x_any.at[pl.ds(pl.multiple_of(core * n_tok, n_tok), n_tok), :], x_ref, x_sem)
 
-    def pool_rows():
-        x_copy.wait()
+    def spread_bias(row_of):
+        for h in range(3):
+            wide = jnp.broadcast_to(row_of(h), (half, 2 * length))
+            bias[h] = pltpu.roll(wide, length, 1, stride=2, stride_axis=0)[:, :length].T
+
+    def pool_rows(first, last):
+        if first == 0:
+            x_copy.wait()
         pool = pool_matrix(half, length)
-        for i in range(n_seq):
+        for i in range(first, last):
             pooled = dot_nn(pool, x_ref[i * length : (i + 1) * length, :])
             hid_ref[i * half : (i + 1) * half, :] = pooled + bo_ref[...].reshape(1, -1)
             pb_ref[i * half : (i + 1) * half, :] = pooled.astype(BF16)
@@ -270,17 +276,20 @@
             net.start(0)
             u_in[...] = uw[...].astype(BF16)
             d_in[...] = dw[...].astype(BF16)
+            cuts = [min(i, n_seq) for i in range(n_dp // 2)]
             for s in range(1, n_dp // 2):
                 net.spread(0, s)
                 net.pass_on(0, s - 1)
+                pool_rows(cuts[s - 1], cuts[s])
             net.start(1)
-            net.pass_on(0, n_dp // 2 - 1)
-            pool_rows()
             small = net.small()
             small[0].wait()
             for copy in small[1:]:
                 copy.wait()
             s_copy.start()
+            spread_bias(lambda h: s_all[0, h : h + 1, :])
+            net.pass_on(0, n_dp // 2 - 1)
+            pool_rows(cuts[-1], n_seq)
             net.local(0).wait()
             net.arrived(0, (0, 1))
 
@@ -325,7 +334,7 @@
         @pl.when(step == 0)
         def _():
             x_copy.start()
-            pool_rows()
+            pool_rows(0, n_seq)
 
         def weights(lanes):
             return a_ref[0, :, lanes]
@@ -336,11 +345,9 @@
     krows = pl.ds(pl.multiple_of(b * length, length), length)
     qrows = pl.ds(pl.multiple_of(b * half, half), half)
 
-    @pl.when(b == 0)
+    @pl.when(jnp.logical_and(b == 0, step > 0) if comm else b == 0)
     def _():
-        for h in range(3):
-            wide = jnp.broadcast_to(small_row(h), (half, 2 * length))
-            bias[h] = pltpu.roll(wide, length, 1, stride=2, stride_axis=0)[:, :length].T
+        spread_bias(small_row)
 
     kv_ref[0] = (dot_nn(x_ref[krows, :], weights(slice(0, 384))) + small_row(3)[:, 0:384]).astype(BF16)
     q = dot_nn(pb_ref[qrows, :], weights(slice(384, 640))) * 0.125

time: 191 us -> 190 us (level)
  no operation moved by 1% of the time
where the time goes in v8:
time: 190 us
  Pallas kernels  189 us (99%)
    pallas_call x1, Pallas kernels, attention_forward(): pl.pallas_call(functools.partial(attention_kernel, n_seq, length, n_dp, c...  79.1 us
    pallas_call x1, Pallas kernels, attention_backward(): pl.pallas_call(functools.partial(backward_kernel, n_seq, length, n_dp, co...  62.7 us
    pallas_call x1, Pallas kernels, ffn(): pl.pallas_call(functools.partial(ffn_kernel, n_seq, half), out_shape=(jax...  38.4 us
    pallas_call x1, Pallas kernels, finish(): pl.pallas_call(functools.partial(finish_kernel, n_out, n_tok, length), ou...  8.44 us

profile of v8, /device:TPU:0, one launch (start us, length us, event | category | flops | bytes accessed | tf_op | source)
XLA Modules:
  0.0 189.6 jit_solution(4956197983300339077)
XLA Ops:
  0.7 79.1 %shard_map.305 = (bf16[4,2048,384]{2,1,0:T(8,128)(2,1)}, bf16[4,1024,256]{2,1,0:T(8,128)(2,1)}, bf16[4,4,3,512,256]{4,3,2,1,0:T(8,128)(2,1)}, bf16[4,1024,256]{2...) custom-call(s32[8]{0:T(128)} %len_ref.1, ...), custom_call_target="tpu_custom_call" | custom-call | flops 20000000000 | bytes 40000000 | tf_op jit(solution)/shard_map/pallas_call | solution.py:459
  79.8 38.4 %shard_map.306 = (bf16[2048,768]{1,0:T(8,128)(2,1)}, bf16[1024,768]{1,0:T(8,128)(2,1)}, bf16[2,768,768]{2,1,0:T(8,128)(2,1)}, bf16[2,768,768]{2,1,0:T(8,128)(2,1)}, f32[8,768]{1,0:T(8,128)}) custom-call(s32[8]{0:T(128)} %len_ref.1, f32[1024,768]{1,0:T(8,128)} %get-tuple-element.61.hid_ref, bf16[2048,768]{1,0:T(8,128)(2,1)} %cot_ref.1, ...), custom_call_target="tpu_custom_call" | custom-call | flops 24000000000 | bytes 30000000 | tf_op jit(solution)/shard_map/pallas_call | solution.py:547
  118.2 62.7 %shard_map.307 = (bf16[1024,768]{1,0:T(8,128)(2,1)}, bf16[4096,768]{1,0:T(8,128)(2,1)}, f32[96,768]{1,0:T(8,128)}, f32[96,768]{1,0:T(8,128)}, f32[96,768]{1,0:T(...) custom-call(bf16[4096,768]{1,0:T(8,128)(2,1)} %refs_0_.3, bf16[4,768,768]{2,1,0:T(8,128)(2,1)} %bitcast.9, ...), custom_call_target="tpu_custom_call" | custom-call | flops 40000000000 | bytes 30000000 | tf_op jit(solution)/shard_map/pallas_call | solution.py:1021
  181.0 8.4 %shard_map.308 = (bf16[2048,768]{1,0:T(8,128)(2,1)}, bf16[4096,768]{1,0:T(8,128)(2,1)}, f32[96,192]{1,0:T(8,128)}, f32[96,192]{1,0:T(8,128)}, f32[96,192]{1,0:T(...) custom-call(f32[96,768]{1,0:T(8,128)} %get-tuple-element.71.a_ref, ...), custom_call_target="tpu_custom_call", output_to_operand_aliasing={{0}: (5, {})} | custom-call | tf_op jit(solution)/shard_map/pallas_call | solution.py:1078

commit v9 on v8

--- a/solution.py
+++ b/solution.py
@@ -1073,16 +1073,17 @@
 def finish(half_done, other, tok, a_sum, up_sum, down_sum, gv, sm, length):
     rows, width = a_sum.shape
     shapes = [(rows, 192)] * 3 + [(192, rows), (rows, 768), (rows, 768), (3, 2 * length), (192,), (768,)] + [(width,)] * 6
-    n_out, n_tok = other.shape[0] // length, tok.shape[0] // length
+    chunk = length // 2
+    n_out, n_tok = other.shape[0] // chunk, tok.shape[0] // chunk
     whole = pl.BlockSpec(memory_space=pltpu.VMEM)
     return pl.pallas_call(
-        functools.partial(finish_kernel, n_out, n_tok, length),
+        functools.partial(finish_kernel, n_out, n_tok, chunk),
         out_shape=[jax.ShapeDtypeStruct(half_done.shape, BF16), jax.ShapeDtypeStruct(tok.shape, BF16)]
         + [jax.ShapeDtypeStruct(shape, F32) for shape in shapes],
         in_specs=[whole] * 5 + [ANY] * 3,
         out_specs=[ANY] * 2 + [whole] * len(shapes),
         scratch_shapes=[
-            pltpu.VMEM((n_tok + n_out, length, width), BF16), pltpu.SemaphoreType.DMA((2, n_tok + n_out)),
+            pltpu.VMEM((n_tok + n_out, chunk, width), BF16), pltpu.SemaphoreType.DMA((2, n_tok + n_out)),
         ],
         input_output_aliases={5: 0},
         compiler_params=pltpu.CompilerParams(vmem_limit_bytes=VMEM_LIMIT),

time: 190 us -> 190 us (level)
  no operation moved by 1% of the time
where the time goes in v9:
time: 190 us
  Pallas kernels  189 us (99%)
    pallas_call x1, Pallas kernels, attention_forward(): pl.pallas_call(functools.partial(attention_kernel, n_seq, length, n_dp, c...  79.1 us
    pallas_call x1, Pallas kernels, attention_backward(): pl.pallas_call(functools.partial(backward_kernel, n_seq, length, n_dp, co...  62.7 us
    pallas_call x1, Pallas kernels, ffn(): pl.pallas_call(functools.partial(ffn_kernel, n_seq, half), out_shape=(jax...  38.4 us
    pallas_call x1, Pallas kernels, finish(): pl.pallas_call(functools.partial(finish_kernel, n_out, n_tok, chunk), out...  8.36 us

profile of v9, /device:TPU:0, one launch (start us, length us, event | category | flops | bytes accessed | tf_op | source)
XLA Modules:
  0.0 189.5 jit_solution(3167280156955751155)
XLA Ops:
  0.7 79.1 %shard_map.305 = (bf16[4,2048,384]{2,1,0:T(8,128)(2,1)}, bf16[4,1024,256]{2,1,0:T(8,128)(2,1)}, bf16[4,4,3,512,256]{4,3,2,1,0:T(8,128)(2,1)}, bf16[4,1024,256]{2...) custom-call(s32[8]{0:T(128)} %len_ref.1, ...), custom_call_target="tpu_custom_call" | custom-call | flops 20000000000 | bytes 40000000 | tf_op jit(solution)/shard_map/pallas_call | solution.py:459
  79.8 38.4 %shard_map.306 = (bf16[2048,768]{1,0:T(8,128)(2,1)}, bf16[1024,768]{1,0:T(8,128)(2,1)}, bf16[2,768,768]{2,1,0:T(8,128)(2,1)}, bf16[2,768,768]{2,1,0:T(8,128)(2,1)}, f32[8,768]{1,0:T(8,128)}) custom-call(s32[8]{0:T(128)} %len_ref.1, f32[1024,768]{1,0:T(8,128)} %get-tuple-element.61.hid_ref, bf16[2048,768]{1,0:T(8,128)(2,1)} %cot_ref.1, ...), custom_call_target="tpu_custom_call" | custom-call | flops 24000000000 | bytes 30000000 | tf_op jit(solution)/shard_map/pallas_call | solution.py:547
  118.2 62.7 %shard_map.307 = (bf16[1024,768]{1,0:T(8,128)(2,1)}, bf16[4096,768]{1,0:T(8,128)(2,1)}, f32[96,768]{1,0:T(8,128)}, f32[96,768]{1,0:T(8,128)}, f32[96,768]{1,0:T(...) custom-call(bf16[4096,768]{1,0:T(8,128)(2,1)} %refs_0_.3, bf16[4,768,768]{2,1,0:T(8,128)(2,1)} %bitcast.9, ...), custom_call_target="tpu_custom_call" | custom-call | flops 40000000000 | bytes 30000000 | tf_op jit(solution)/shard_map/pallas_call | solution.py:1021
  181.0 8.4 %shard_map.308 = (bf16[2048,768]{1,0:T(8,128)(2,1)}, bf16[4096,768]{1,0:T(8,128)(2,1)}, f32[96,192]{1,0:T(8,128)}, f32[96,192]{1,0:T(8,128)}, f32[96,192]{1,0:T(...) custom-call(f32[96,768]{1,0:T(8,128)} %get-tuple-element.71.a_ref, ...), custom_call_target="tpu_custom_call", output_to_operand_aliasing={{0}: (5, {})} | custom-call | tf_op jit(solution)/shard_map/pallas_call | solution.py:1079
